TPU v7x, 32 devices: a whole 2x2x4 slice. The times are simulated.
32 devices in a mesh: dp: 2 (over x), ctx: 16 (over z, y, core).
Axes of the slice: x: 2, y: 2, z: 4, core: 2. Of those that a mesh axis runs over, the one named last changes fastest.
Arguments:
- tokens: bfloat16 [16384, 1024], P(('dp', 'ctx')), may hold values from -6 to 6
- grad_out: bfloat16 [16384, 1024], P(('dp', 'ctx')), may hold values from -6 to 6
- w_query: bfloat16 [1024, 1024], P(('dp', 'ctx')), may hold values from -0.1875 to 0.1875
- w_key: bfloat16 [1024, 512], P(('dp', 'ctx')), may hold values from -0.1875 to 0.1875
- w_value: bfloat16 [1024, 512], P(('dp', 'ctx')), may hold values from -0.1875 to 0.1875
- w_output: bfloat16 [1024, 1024], P(('dp', 'ctx')), may hold values from -6 to 6
- gain_attn: bfloat16 [1024], P(('dp', 'ctx')), may hold values from 0.5 to 1.5
- gain_ffn: bfloat16 [1024], P(('dp', 'ctx')), may hold values from 0.5 to 1.5
- w_router: bfloat16 [1024, 32], P(('dp', 'ctx')), may hold values from -0.09375 to 0.09375
- w_experts: bfloat16 [3, 1024, 16384], P(None, 'dp', 'ctx'), may hold values from -0.35546875 to 0.35546875
- deal_table: int32 [2, 32], P('dp'), may hold values from 0 to 31, as said below
- routes: int32 [16384, 8], P(('dp', 'ctx')), may hold values from 0 to 31, all different within a row; in each aligned block of 512 rows (0 to 511, 512 to 1023, ...) at most 160 rows name the same one
Outputs:
- mixed: bfloat16 [16384, 1024], P(('dp', 'ctx'))
- grad_tokens: float32 [16384, 1024], P(('dp', 'ctx'))
- grad_query: float32 [1024, 1024], P(('dp', 'ctx'))
- grad_key: float32 [1024, 512], P(('dp', 'ctx'))
- grad_value: float32 [1024, 512], P(('dp', 'ctx'))
- grad_output: float32 [1024, 1024], P(('dp', 'ctx'))
- grad_gain_attn: float32 [1024], P(('dp', 'ctx'))
- grad_gain_ffn: float32 [1024], P(('dp', 'ctx'))
- grad_router: float32 [1024, 32], P(('dp', 'ctx'))
- grad_experts: float32 [3, 1024, 16384], P(None, 'dp', 'ctx')
Inputs may be any that keep to these rules, and one draw needn't show every extreme that they name: `deal_table`: entry s of row g is k * 16 + b for block b of sequence k of group g; each row holds every number once, and slots 2 c and 2 c + 1 hold blocks b and 15 - b of one sequence. `routes`: A token names 8 different experts. Among the rows of one device no expert is named by more than 160 rows, a bound that some block reaches.
All inputs are finite; a program needn't handle non-finite values.
Results may differ from a plain program's by a relative error of at most 0.028.
Values may be sent and summed in bfloat16 or wider, within the bound.
No kernel may reach another device: no remote copies, remote signals or barrier semaphores. Data moves between devices by JAX's collectives and lax.ppermute only.
A program may use at most 960 MiB of HBM per device.

v0:
```python
from functools import partial

import jax
import jax.numpy as jnp
from jax import lax
from jax.sharding import PartitionSpec as P

D = 1024
HQ = 16
KVH = 8
HD = 64
E = 32
F = 512
TOPK = 8
BLK = 256
BLOCKS = 16
CAP = 160


epsilon = 1e-06
highest = lax.Precision.HIGHEST
floor_value = -1e30


def rms_norm(values, gain):
    return values * lax.rsqrt(jnp.mean(values * values, axis=-1, keepdims=True) + epsilon) * gain


def rotary(values, positions):
    half_size = values.shape[-1] // 2
    frequency = 10000.0 ** (-(jnp.arange(half_size).astype(jnp.float32) * 2.0 / values.shape[-1]))
    angles = positions.astype(jnp.float32)[:, None] * frequency[None, :]
    cosine = jnp.cos(angles)[:, None, :]
    sine_part = jnp.sin(angles)[:, None, :]
    first_half = values[..., :half_size]
    second = values[..., half_size:]
    return jnp.concatenate(
        [first_half * cosine - second * sine_part, second * cosine + first_half * sine_part],
        axis=-1,
    )


def heads_major(block_rows, groups, head_ratio, head_size):
    count = block_rows.shape[0]
    shaped = block_rows.reshape(count, groups, head_ratio, head_size).transpose(1, 2, 0, 3)
    return shaped.reshape(groups, head_ratio * count, head_size)


def rows_major(blocked, groups, head_ratio, head_size):
    count = blocked.shape[1] // head_ratio
    shaped = blocked.reshape(groups, head_ratio, count, head_size).transpose(2, 0, 1, 3)
    return shaped.reshape(count, groups * head_ratio * head_size)


def stats_major(block_rows, groups, head_ratio):
    count = block_rows.shape[0]
    return (
        block_rows.reshape(count, groups, head_ratio)
        .transpose(1, 2, 0)
        .reshape(groups, head_ratio * count)
    )


def pair_blocks(rows, base, groups, head_ratio, head_size):
    return jnp.stack(
        [
            heads_major(rows[base + i * BLK : base + (i + 1) * BLK], groups, head_ratio, head_size)
            for i in range(2)
        ]
    )


def pair_order(block_pair, per_seq):
    places = block_pair % per_seq
    lower_slot = (places[0] > places[1]).astype(jnp.int32)
    return (lower_slot, 1 - lower_slot, jnp.minimum(places[0], places[1]), block_pair[0] // per_seq)


def keep_state(carry_state):
    return carry_state


def forward_update(query_block, key_block, value_block, slot_number, score_scale):

    def forward_apply_update(carry_state):
        running_max, running_sum, accumulated = carry_state
        scores = (
            jnp.einsum("gqd,gkd->gqk", query_block, key_block, preferred_element_type=jnp.float32)
            * score_scale
        )
        new_max = jnp.maximum(running_max[slot_number], jnp.max(scores, axis=-1))
        factor = jnp.exp(running_max[slot_number] - new_max)
        weights = jnp.exp(scores - new_max[..., None])
        new_sum = running_sum[slot_number] * factor + jnp.sum(weights, axis=-1)
        product = jnp.einsum(
            "gqk,gkd->gqd",
            weights.astype(jnp.bfloat16),
            value_block,
            preferred_element_type=jnp.float32,
        )
        new_acc = accumulated[slot_number] * factor[..., None] + product
        return (
            running_max.at[slot_number].set(new_max),
            running_sum.at[slot_number].set(new_sum),
            accumulated.at[slot_number].set(new_acc),
        )

    return forward_apply_update


def query_update(
    query_block,
    grad_block,
    log_block,
    delta_block,
    key_block,
    value_block,
    slot_number,
    score_scale,
):

    def query_apply_update(accumulated):
        scores = (
            jnp.einsum("gqd,gkd->gqk", query_block, key_block, preferred_element_type=jnp.float32)
            * score_scale
        )
        probs_full = jnp.exp(scores - log_block[..., None])
        prob_grad = jnp.einsum(
            "gqd,gkd->gqk", grad_block, value_block, preferred_element_type=jnp.float32
        )
        score_grad = (probs_full * (prob_grad - delta_block[..., None])).astype(jnp.bfloat16)
        change = (
            jnp.einsum("gqk,gkd->gqd", score_grad, key_block, preferred_element_type=jnp.float32)
            * score_scale
        )
        return accumulated.at[slot_number].add(change)

    return query_apply_update


def key_update(
    query_block,
    grad_block,
    log_block,
    delta_block,
    key_block,
    value_block,
    slot_number,
    score_scale,
):

    def key_apply_update(carry_state):
        key_accum, value_accum = carry_state
        scores = (
            jnp.einsum("gqd,gkd->gqk", query_block, key_block, preferred_element_type=jnp.float32)
            * score_scale
        )
        probs_full = jnp.exp(scores - log_block[..., None])
        value_change = jnp.einsum(
            "gqk,gqd->gkd",
            probs_full.astype(jnp.bfloat16),
            grad_block,
            preferred_element_type=jnp.float32,
        )
        prob_grad = jnp.einsum(
            "gqd,gkd->gqk", grad_block, value_block, preferred_element_type=jnp.float32
        )
        score_grad = (probs_full * (prob_grad - delta_block[..., None])).astype(jnp.bfloat16)
        key_change = (
            jnp.einsum("gqk,gqd->gkd", score_grad, query_block, preferred_element_type=jnp.float32)
            * score_scale
        )
        return (
            key_accum.at[slot_number].add(key_change),
            value_accum.at[slot_number].add(value_change),
        )

    return key_apply_update


def expert_forward(routed_rows, weights_local):
    gate_pre = jnp.einsum(
        "erd,def->erf", routed_rows, weights_local[0], preferred_element_type=jnp.float32
    )
    up_pre = jnp.einsum(
        "erd,def->erf", routed_rows, weights_local[1], preferred_element_type=jnp.float32
    )
    hidden = (jax.nn.silu(gate_pre) * up_pre).astype(jnp.bfloat16)
    return (gate_pre, up_pre, hidden)


def natural_return(partials, split_count):
    devices = partials.shape[0]
    arrived = lax.all_to_all(partials, "ctx", split_axis=0, concat_axis=0, tiled=True)
    shaped = arrived.reshape(
        devices * partials.shape[1] // split_count,
        split_count,
        partials.shape[2],
        partials.shape[3],
    )
    return jnp.sum(shaped, axis=1)


def send_back(partials, split_count):
    return natural_return(partials, split_count)


def spread_slots(slot_values, devices, local_count, split_count):
    width = slot_values.shape[-1]
    return jnp.broadcast_to(
        slot_values.reshape(E, 1, CAP, width), (E, split_count, CAP, width)
    ).reshape(devices, local_count, CAP, width)


def per_device(
    tokens,
    grad_out,
    w_query,
    w_key,
    w_value,
    w_output,
    gain_attn,
    gain_ffn,
    w_router,
    w_experts,
    deal_table,
    routes,
):
    row_count = tokens.shape[0]
    head_ratio = HQ // KVH
    score_scale = HD ** (-0.5)
    full_query, full_key, full_value, full_output, full_router, full_gain_attn, full_gain_ffn = (
        lax.all_gather(w_query, ("dp", "ctx"), axis=0, tiled=True),
        lax.all_gather(w_key, ("dp", "ctx"), axis=0, tiled=True),
        lax.all_gather(w_value, ("dp", "ctx"), axis=0, tiled=True),
        lax.all_gather(w_output, ("dp", "ctx"), axis=0, tiled=True),
        lax.all_gather(w_router, ("dp", "ctx"), axis=0, tiled=True),
        lax.all_gather(gain_attn, ("dp", "ctx"), axis=0, tiled=True),
        lax.all_gather(gain_ffn, ("dp", "ctx"), axis=0, tiled=True),
    )
    experts_local = lax.all_gather(w_experts, "dp", axis=1, tiled=True)
    columns = experts_local.shape[2]
    unit_width = min(F, columns)
    local_count = columns // unit_width
    split_count = F // unit_width
    devices = lax.axis_size("ctx")
    position = lax.axis_index("ctx")
    group_blocks = deal_table[0]
    per_seq = BLOCKS
    own_blocks = lax.dynamic_slice_in_dim(group_blocks, 2 * position, 2)
    query_low, query_high, low_place, own_seq = pair_order(own_blocks, per_seq)
    offsets = jnp.arange(BLK, dtype=jnp.int32)
    positions = ((own_blocks % per_seq)[:, None] * BLK + offsets[None, :]).reshape(-1)
    inputs = tokens.astype(jnp.float32)
    gain_attn_full = full_gain_attn.astype(jnp.float32)
    gain_ffn_full = full_gain_ffn.astype(jnp.float32)
    normed = rms_norm(inputs, gain_attn_full).astype(jnp.bfloat16)
    query_raw = jnp.dot(normed, full_query, preferred_element_type=jnp.float32).reshape(
        row_count, HQ, HD
    )
    key_raw = jnp.dot(normed, full_key, preferred_element_type=jnp.float32).reshape(
        row_count, KVH, HD
    )
    value_raw = jnp.dot(normed, full_value, preferred_element_type=jnp.float32)
    queries = rotary(query_raw, positions).astype(jnp.bfloat16).reshape(row_count, HQ * HD)
    key_proj = rotary(key_raw, positions).astype(jnp.bfloat16).reshape(row_count, KVH * HD)
    value_proj = value_raw.astype(jnp.bfloat16)
    query_heads = pair_blocks(queries, 0, KVH, head_ratio, HD)
    key_heads = pair_blocks(key_proj, 0, KVH, 1, HD)
    value_heads = pair_blocks(value_proj, 0, KVH, 1, HD)
    score_rows = head_ratio * BLK
    initial = (
        jnp.full((2, KVH, score_rows), floor_value, jnp.float32),
        jnp.zeros((2, KVH, score_rows), jnp.float32),
        jnp.zeros((2, KVH, score_rows, HD), jnp.float32),
    )
    initial = forward_update(
        query_heads[query_low], key_heads[query_low], value_heads[query_low], query_low, score_scale
    )(initial)
    carry_state = initial
    key_rows = lax.all_gather(key_proj, "ctx", axis=0, tiled=True)
    value_rows = lax.all_gather(value_proj, "ctx", axis=0, tiled=True)
    for j in range(key_rows.shape[0] // (2 * BLK)):
        key_pair = pair_blocks(key_rows, j * 2 * BLK, KVH, 1, HD)
        value_pair = pair_blocks(value_rows, j * 2 * BLK, KVH, 1, HD)
        block_pair = lax.dynamic_slice_in_dim(group_blocks, 2 * j, 2)
        key_low, key_high, key_place, key_seq = pair_order(block_pair, per_seq)
        same = key_seq == own_seq
        carry_state = lax.cond(
            same,
            forward_update(
                query_heads[query_high],
                key_pair[key_low],
                value_pair[key_low],
                query_high,
                score_scale,
            ),
            keep_state,
            carry_state,
        )
        below = key_place < low_place
        pick_query = jnp.where(below, query_low, query_high)
        pick_key = jnp.where(below, key_low, key_high)
        carry_state = lax.cond(
            same,
            forward_update(
                query_heads[pick_query],
                key_pair[pick_key],
                value_pair[pick_key],
                pick_query,
                score_scale,
            ),
            keep_state,
            carry_state,
        )
    running_max, running_sum, accumulated = carry_state
    attended_heads = accumulated / running_sum[..., None]
    log_total = running_max + jnp.log(running_sum)
    attended_rows = jnp.concatenate(
        [rows_major(attended_heads[i], KVH, head_ratio, HD) for i in range(2)], axis=0
    )
    attended_low = attended_rows.astype(jnp.bfloat16)
    residual = inputs + jnp.dot(attended_low, full_output, preferred_element_type=jnp.float32)
    normed_ffn = rms_norm(residual, gain_ffn_full).astype(jnp.bfloat16)
    expert_ids = jnp.arange(E, dtype=jnp.int32)
    picked = routes[:, :, None] == expert_ids[None, None, :]
    ffn_float = normed_ffn.astype(jnp.float32)
    router_full = full_router.astype(jnp.float32)
    logits = jnp.dot(ffn_float, router_full, precision=highest)
    chosen = jnp.sum(jnp.where(picked, logits[:, None, :], 0.0), axis=2)
    gate_weights = jax.nn.softmax(chosen, axis=-1)
    member = jnp.sum(picked.astype(jnp.int32), axis=1)
    before = jnp.cumsum(member, axis=0) - member
    slot_numbers = jnp.sum(jnp.where(picked, before[:, None, :], 0), axis=2)
    flat_slot = (routes * CAP + slot_numbers).reshape(-1)
    owner_rows = (
        jnp.zeros((E * CAP,), jnp.int32)
        .at[flat_slot]
        .set(jnp.repeat(jnp.arange(1, row_count + 1, dtype=jnp.int32), TOPK))
    )
    slot_gate = jnp.zeros((E * CAP,), jnp.float32).at[flat_slot].set(gate_weights.reshape(-1))
    padded_rows = jnp.concatenate([jnp.zeros((1, D), jnp.bfloat16), normed_ffn], axis=0)
    slot_rows = padded_rows[owner_rows]
    outgoing = spread_slots(slot_rows, devices, local_count, split_count)
    arrived = lax.all_to_all(outgoing, "ctx", split_axis=0, concat_axis=0, tiled=True)
    routed_rows = arrived.transpose(1, 0, 2, 3).reshape(local_count, devices * outgoing.shape[2], D)
    weights_local = experts_local.reshape(3, D, local_count, unit_width)
    gate_pre, up_pre, hidden = expert_forward(routed_rows, weights_local)
    expert_out = jnp.einsum(
        "erf,def->erd", hidden, weights_local[2], preferred_element_type=jnp.float32
    )
    combined = send_back(
        expert_out.reshape(local_count, devices, outgoing.shape[2], D).transpose(1, 0, 2, 3),
        split_count,
    )
    routed_out = combined.reshape(E * CAP, D)[flat_slot].reshape(row_count, TOPK, D)
    mixed = (residual + jnp.sum(gate_weights[:, :, None] * routed_out, axis=1)).astype(jnp.bfloat16)
    upstream = grad_out.astype(jnp.float32)
    gate_grad = jnp.sum(routed_out * upstream[:, None, :], axis=2)
    chosen_grad = gate_weights * (
        gate_grad - jnp.sum(gate_weights * gate_grad, axis=1, keepdims=True)
    )
    logits_grad = jnp.sum(jnp.where(picked, chosen_grad[:, :, None], 0.0), axis=1)
    padded_grad = jnp.concatenate([jnp.zeros((1, D), jnp.float32), upstream], axis=0)
    slot_grad = (padded_grad[owner_rows] * slot_gate[:, None]).astype(jnp.bfloat16)
    outgoing_grad = spread_slots(slot_grad, devices, local_count, split_count)
    arrived_grad = lax.all_to_all(outgoing_grad, "ctx", split_axis=0, concat_axis=0, tiled=True)
    grad_rows = arrived_grad.transpose(1, 0, 2, 3).reshape(
        local_count, devices * outgoing.shape[2], D
    )
    hidden_grad = jnp.einsum(
        "erd,def->erf", grad_rows, weights_local[2], preferred_element_type=jnp.float32
    )
    sigmoid = jax.nn.sigmoid(gate_pre)
    up_grad = (hidden_grad * gate_pre * sigmoid).astype(jnp.bfloat16)
    gate_pre_grad = (hidden_grad * up_pre * sigmoid * (1.0 + gate_pre * (1.0 - sigmoid))).astype(
        jnp.bfloat16
    )
    weight_grad = jnp.stack(
        [
            jnp.einsum(
                "erd,erf->def", routed_rows, gate_pre_grad, preferred_element_type=jnp.float32
            ),
            jnp.einsum("erd,erf->def", routed_rows, up_grad, preferred_element_type=jnp.float32),
            jnp.einsum("erd,erf->def", grad_rows, hidden, preferred_element_type=jnp.float32),
        ]
    ).reshape(3, D, local_count * unit_width)
    input_grad = jnp.einsum(
        "erf,def->erd", gate_pre_grad, weights_local[0], preferred_element_type=jnp.float32
    )
    input_grad = input_grad + jnp.einsum(
        "erf,def->erd", up_grad, weights_local[1], preferred_element_type=jnp.float32
    )
    returned = send_back(
        input_grad.reshape(local_count, devices, outgoing.shape[2], D).transpose(1, 0, 2, 3),
        split_count,
    )
    ffn_grad = jnp.sum(returned.reshape(E * CAP, D)[flat_slot].reshape(row_count, TOPK, D), axis=1)
    ffn_grad = ffn_grad + jnp.einsum("re,de->rd", logits_grad, router_full, precision=highest)
    router_grad = jnp.einsum("rd,re->de", ffn_float, logits_grad, precision=highest)
    expert_grad = lax.psum_scatter(weight_grad, "dp", scatter_dimension=1, tiled=True)
    _, norm_back_ffn = jax.vjp(rms_norm, residual, gain_ffn_full)
    residual_norm_grad, gain_ffn_grad = norm_back_ffn(ffn_grad)
    residual_grad = upstream + residual_norm_grad
    branch_grad = residual_grad.astype(jnp.bfloat16)
    output_grad = jnp.einsum(
        "rc,rd->cd", attended_low, branch_grad, preferred_element_type=jnp.float32
    )
    attended_grad = jnp.einsum(
        "rd,cd->rc", branch_grad, full_output, preferred_element_type=jnp.float32
    ).astype(jnp.bfloat16)
    delta_rows = jnp.sum(
        (attended_grad.astype(jnp.float32) * attended_rows).reshape(row_count, HQ, HD), axis=-1
    )
    delta_heads = jnp.stack(
        [stats_major(delta_rows[i * BLK : (i + 1) * BLK], KVH, head_ratio) for i in range(2)]
    )
    grad_heads = pair_blocks(attended_grad, 0, KVH, head_ratio, HD)
    all_log, all_delta = (
        lax.all_gather(log_total, "ctx", axis=0, tiled=True),
        lax.all_gather(delta_heads, "ctx", axis=0, tiled=True),
    )
    query_start = query_update(
        query_heads[query_low],
        grad_heads[query_low],
        log_total[query_low],
        delta_heads[query_low],
        key_heads[query_low],
        value_heads[query_low],
        query_low,
        score_scale,
    )(jnp.zeros((2, KVH, score_rows, HD), jnp.float32))
    accumulated_grad = query_start
    key_rows = lax.all_gather(key_proj, "ctx", axis=0, tiled=True)
    value_rows = lax.all_gather(value_proj, "ctx", axis=0, tiled=True)
    for j in range(key_rows.shape[0] // (2 * BLK)):
        key_pair = pair_blocks(key_rows, j * 2 * BLK, KVH, 1, HD)
        value_pair = pair_blocks(value_rows, j * 2 * BLK, KVH, 1, HD)
        block_pair = lax.dynamic_slice_in_dim(group_blocks, 2 * j, 2)
        key_low, key_high, key_place, key_seq = pair_order(block_pair, per_seq)
        same = key_seq == own_seq
        first = query_update(
            query_heads[query_high],
            grad_heads[query_high],
            log_total[query_high],
            delta_heads[query_high],
            key_pair[key_low],
            value_pair[key_low],
            query_high,
            score_scale,
        )
        accumulated_grad = lax.cond(same, first, keep_state, accumulated_grad)
        below = key_place < low_place
        pick_query = jnp.where(below, query_low, query_high)
        pick_key = jnp.where(below, key_low, key_high)
        second_update = query_update(
            query_heads[pick_query],
            grad_heads[pick_query],
            log_total[pick_query],
            delta_heads[pick_query],
            key_pair[pick_key],
            value_pair[pick_key],
            pick_query,
            score_scale,
        )
        accumulated_grad = lax.cond(same, second_update, keep_state, accumulated_grad)
    zero_keys = jnp.zeros((2, KVH, BLK, HD), jnp.float32)
    key_start = key_update(
        query_heads[query_low],
        grad_heads[query_low],
        log_total[query_low],
        delta_heads[query_low],
        key_heads[query_low],
        value_heads[query_low],
        query_low,
        score_scale,
    )((zero_keys, zero_keys))
    carry_state = key_start
    start_row = jnp.int32(0)
    query_rows = lax.all_gather(queries, "ctx", axis=0, tiled=True)
    grad_piece = lax.all_gather(attended_grad, "ctx", axis=0, tiled=True)
    for j in range(query_rows.shape[0] // (2 * BLK)):
        slot_first = start_row // BLK + 2 * j
        query_pair = pair_blocks(query_rows, j * 2 * BLK, KVH, head_ratio, HD)
        grad_pair = pair_blocks(grad_piece, j * 2 * BLK, KVH, head_ratio, HD)
        block_pair = lax.dynamic_slice_in_dim(group_blocks, slot_first, 2)
        log_pair = lax.dynamic_slice_in_dim(all_log, slot_first, 2)
        delta_pair = lax.dynamic_slice_in_dim(all_delta, slot_first, 2)
        remote_low, remote_high, remote_place, remote_seq = pair_order(block_pair, per_seq)
        same = remote_seq == own_seq
        first = key_update(
            query_pair[remote_high],
            grad_pair[remote_high],
            log_pair[remote_high],
            delta_pair[remote_high],
            key_heads[query_low],
            value_heads[query_low],
            query_low,
            score_scale,
        )
        carry_state = lax.cond(same, first, keep_state, carry_state)
        below = low_place < remote_place
        pick_remote = jnp.where(below, remote_low, remote_high)
        pick_own = jnp.where(below, query_low, query_high)
        second_update = key_update(
            query_pair[pick_remote],
            grad_pair[pick_remote],
            log_pair[pick_remote],
            delta_pair[pick_remote],
            key_heads[pick_own],
            value_heads[pick_own],
            pick_own,
            score_scale,
        )
        carry_state = lax.cond(same, second_update, keep_state, carry_state)
    key_grad_heads, value_grad_heads = carry_state
    query_grad_rows = jnp.concatenate(
        [rows_major(accumulated_grad[i], KVH, head_ratio, HD) for i in range(2)], axis=0
    )
    key_grad_rows = jnp.concatenate(
        [rows_major(key_grad_heads[i], KVH, 1, HD) for i in range(2)], axis=0
    )
    value_grad_rows = jnp.concatenate(
        [rows_major(value_grad_heads[i], KVH, 1, HD) for i in range(2)], axis=0
    )
    _, query_rot_back = jax.vjp(partial(rotary, positions=positions), query_raw)
    _, key_rot_back = jax.vjp(partial(rotary, positions=positions), key_raw)
    query_proj_grad = (
        query_rot_back(query_grad_rows.reshape(row_count, HQ, HD))[0]
        .reshape(row_count, HQ * HD)
        .astype(jnp.bfloat16)
    )
    key_proj_grad = (
        key_rot_back(key_grad_rows.reshape(row_count, KVH, HD))[0]
        .reshape(row_count, KVH * HD)
        .astype(jnp.bfloat16)
    )
    value_proj_grad = value_grad_rows.astype(jnp.bfloat16)
    query_weight_grad = jnp.einsum(
        "rd,rc->dc", normed, query_proj_grad, preferred_element_type=jnp.float32
    )
    key_weight_grad = jnp.einsum(
        "rd,rc->dc", normed, key_proj_grad, preferred_element_type=jnp.float32
    )
    value_weight_grad = jnp.einsum(
        "rd,rc->dc", normed, value_proj_grad, preferred_element_type=jnp.float32
    )
    normed_grad = jnp.einsum(
        "rc,dc->rd", query_proj_grad, full_query, preferred_element_type=jnp.float32
    )
    normed_grad = normed_grad + jnp.einsum(
        "rc,dc->rd", key_proj_grad, full_key, preferred_element_type=jnp.float32
    )
    normed_grad = normed_grad + jnp.einsum(
        "rc,dc->rd", value_proj_grad, full_value, preferred_element_type=jnp.float32
    )
    _, norm_back_attn = jax.vjp(rms_norm, inputs, gain_attn_full)
    input_norm_grad, gain_attn_grad = norm_back_attn(normed_grad)
    tokens_grad = residual_grad + input_norm_grad
    owned = (
        lax.psum_scatter(query_weight_grad, ("dp", "ctx"), scatter_dimension=0, tiled=True),
        lax.psum_scatter(key_weight_grad, ("dp", "ctx"), scatter_dimension=0, tiled=True),
        lax.psum_scatter(value_weight_grad, ("dp", "ctx"), scatter_dimension=0, tiled=True),
        lax.psum_scatter(output_grad, ("dp", "ctx"), scatter_dimension=0, tiled=True),
        lax.psum_scatter(router_grad, ("dp", "ctx"), scatter_dimension=0, tiled=True),
        lax.psum_scatter(gain_attn_grad, ("dp", "ctx"), scatter_dimension=0, tiled=True),
        lax.psum_scatter(gain_ffn_grad, ("dp", "ctx"), scatter_dimension=0, tiled=True),
    )
    return (
        mixed,
        tokens_grad,
        owned[0],
        owned[1],
        owned[2],
        owned[3],
        owned[5],
        owned[6],
        owned[4],
        expert_grad,
    )


def solution(mesh):
    in_specs = (
        P(("dp", "ctx"), None),
        P(("dp", "ctx"), None),
        P(("dp", "ctx"), None),
        P(("dp", "ctx"), None),
        P(("dp", "ctx"), None),
        P(("dp", "ctx"), None),
        P(("dp", "ctx")),
        P(("dp", "ctx")),
        P(("dp", "ctx"), None),
        P(None, "dp", "ctx"),
        P("dp", None),
        P(("dp", "ctx"), None),
    )
    out_specs = (
        P(("dp", "ctx"), None),
        P(("dp", "ctx"), None),
        P(("dp", "ctx"), None),
        P(("dp", "ctx"), None),
        P(("dp", "ctx"), None),
        P(("dp", "ctx"), None),
        P(("dp", "ctx")),
        P(("dp", "ctx")),
        P(("dp", "ctx"), None),
        P(None, "dp", "ctx"),
    )
    return jax.shard_map(
        per_device, mesh=mesh, in_specs=in_specs, out_specs=out_specs, check_vma=False
    )
```

profile of v0, /device:TPU:0, one launch (start us, length us, event | category | flops | bytes accessed | tf_op | source)
XLA Modules:
  0.0 3352.4 jit_solution(10746157507313517153)
XLA Ops:
  13.4 42.1 %all-reduce.11 = (bf16[1024]{0:T(1024)(128)(2,1)S(1)}, bf16[1024]{0:T(1024)(128)(2,1)S(1)}) all-reduce(bf16[1024]{0:T(1024)(128)(2,1)S(1)} %dynamic-update-slice.604, bf16[1024]{0:T(1024)(128)(2,1)S(1)} %dynamic-update-slice.605), channel_id=1, replica_groups=mesh['dp'=2,'ctx'=16] {'dp','ctx'}, use_global_device_ids=true, to_apply=%add.6 | all-reduce | flops 2048 | bytes 8192
  71.8 52.1 %all-gather.14.cloned.1.call-done = bf16[1024,512]{1,0:T(8,128)(2,1)} async-done(((bf16[32,512]{1,0:T(8,128)(2,1)}), bf16[1024,512]{1,0:T(8,128)(2,1)}) %all-gather.14.cloned.1.call-update) | async-done | bytes 1048592 | tf_op jit(solution)/shard_map/all_gather | solution.py:235
  220.7 43.8 %all_gather.52 = bf16[1024,32]{1,0:T(8,128)(2,1)} all-gather(bf16[32,32]{1,0:T(8,128)(2,1)S(1)} %copy-done.286), channel_id=1, replica_groups=mesh['dp'=2,'ctx'=16] {'dp','ctx'}, dimensions={0}, use_global_device_ids=true | all-gather | bytes 67584 | tf_op jit(solution)/shard_map/all_gather | solution.py:237
  266.9 15.5 scatter_custom_fusion
  284.1 23.0 gather_fusion.2
  528.0 15.7 scatter_custom_fusion.1
  561.9 22.5 gather_fusion
  584.4 164.4 %all-to-all-done.2 = bf16[16,2,160,1024]{3,2,1,0:T(8,128)(2,1)} async-done(((bf16[16,2,160,1024]{3,2,1,0:T(8,128)(2,1)}), bf16[16,2,160,1024]{3,2,1,0:T(8,128)(2,1)}, u32[]{:S(2)}, u32[]{:S(2)}) %all-to-all-start.2) | async-done | bytes 10485792 | tf_op jit(solution)/shard_map/all_to_all | solution.py:367
  748.8 45.2 %all-to-all-start = ((bf16[16,2,160,1024]{3,2,1,0:T(8,128)(2,1)}), bf16[16,2,160,1024]{3,2,1,0:T(8,128)(2,1)}, u32[]{:S(2)}, u32[]{:S(2)}) async-start(bf16[16,2,160,1024]{3,2,1,0:T(8,128)(2,1)} %bitcast.3556), calls=%async_computation | async-start | bytes 20971520 | tf_op jit(solution)/shard_map/all_to_all | solution.py:345
  797.3 80.7 %all-gather.22.cloned.1.call-done = bf16[3,1024,1024]{1,2,0:T(8,128)(2,1)} async-done(((bf16[3,512,1024]{1,2,0:T(8,128)(2,1)}), bf16[3,1024,1024]{1,2,0:T(8,128)(2,1)}) %all-gather.22.cloned.1.call-update) | async-done | bytes 6291472 | tf_op jit(solution)/shard_map/all_gather | solution.py:241
  894.4 86.9 %all-to-all-done = bf16[16,2,160,1024]{3,2,1,0:T(8,128)(2,1)} async-done(((bf16[16,2,160,1024]{3,2,1,0:T(8,128)(2,1)}), bf16[16,2,160,1024]{3,2,1,0:T(8,128)(2,1)}, u32[]{:S(2)}, u32[]{:S(2)}) %all-to-all-start) | async-done | bytes 10485792 | tf_op jit(solution)/shard_map/all_to_all | solution.py:345
  1010.9 19.9 multiply_convert_fusion.65
  1046.0 45.4 %all-to-all-start.1 = ((f32[16,2,160,1024]{3,2,1,0:T(8,128)}), f32[16,2,160,1024]{3,2,1,0:T(8,128)}, u32[]{:S(2)}, u32[]{:S(2)}) async-start(f32[16,2,160,1024]{3,2,1,0:T(8,128)} %bitcast.3553), calls=%async_computation.1 | async-start | bytes 41943040 | tf_op jit(solution)/shard_map/all_to_all | solution.py:194
  1104.3 15.5 convolution_add_fusion
  1119.8 16.4 copy.1247
  1136.2 325.0 %all-to-all-done.1 = f32[16,2,160,1024]{3,2,1,0:T(8,128)} async-done(((f32[16,2,160,1024]{3,2,1,0:T(8,128)}), f32[16,2,160,1024]{3,2,1,0:T(8,128)}, u32[]{:S(2)}, u32[]{:S(2)}) %all-to-all-start.1) | async-done | bytes 20971552 | tf_op jit(solution)/shard_map/all_to_all | solution.py:194
  1461.2 87.2 %all-to-all-start.3 = ((f32[16,2,160,1024]{3,2,1,0:T(8,128)}), f32[16,2,160,1024]{3,2,1,0:T(8,128)}, u32[]{:S(2)}, u32[]{:S(2)}) async-start(f32[16,2,160,1024]{3,2,1,0:T(8,128)} %bitcast.3552), calls=%async_computation.3 | async-start | bytes 41943040 | tf_op jit(solution)/shard_map/all_to_all | solution.py:194
  1549.5 29.5 gather_fusion.1
  1591.0 428.4 %all-to-all-done.3 = f32[16,2,160,1024]{3,2,1,0:T(8,128)} async-done(((f32[16,2,160,1024]{3,2,1,0:T(8,128)}), f32[16,2,160,1024]{3,2,1,0:T(8,128)}, u32[]{:S(2)}, u32[]{:S(2)}) %all-to-all-start.3) | async-done | bytes 20971552 | tf_op jit(solution)/shard_map/all_to_all | solution.py:194
  2019.4 29.3 gather_fusion.3
  2341.0 101.4 %all_gather.55 = f32[32,8,512]{2,1,0:T(8,128)S(1)} all-gather(f32[2,8,512]{2,1,0:T(8,128)S(1)} %log_add_fusion), channel_id=1, replica_groups=mesh['dp'=2,'ctx'=16] {'ctx'}, dimensions={0}, use_global_device_ids=true | all-gather | bytes 557056 | tf_op jit(solution)/shard_map/all_gather | solution.py:420
  2595.0 20.2 all_gather.57
  2792.1 14.1 conditional.160
  2822.6 14.2 conditional.162
  2853.4 13.9 conditional.164
  2892.5 14.4 conditional.170
  2957.9 14.4 conditional.176
  2993.2 13.9 conditional.180
  3056.6 15.6 conditional.191
  3084.6 37.1 %all-reduce.10 = (f32[1024]{0:T(1024)S(1)}, f32[1024]{0:T(1024)S(1)}) all-reduce(f32[1024]{0:T(1024)S(1)} %get-tuple-element.7259, f32[1024]{0:T(1024)S(1)} %copy-done.285), channel_id=6, replica_groups=mesh['dp'=2,'ctx'=16] {'dp','ctx'}, use_global_device_ids=true, to_apply=%region_412.413.clone | all-reduce | flops 2048 | bytes 16384
  3126.4 82.6 %reduce-scatter.11.cloned.1.call-done = f32[32,512]{1,0:T(8,128)} async-done(((f32[1024,512]{1,0:T(8,128)}), f32[32,512]{1,0:T(8,128)}) %reduce-scatter.11.cloned.1.call-update) | async-done | bytes 65552 | tf_op jit(solution)/shard_map/reduce_scatter | solution.py:563
  3209.0 135.8 %reduce-scatter.9.cloned.1.call-done = f32[32,512]{1,0:T(8,128)} async-done(((f32[1024,512]{1,0:T(8,128)}), f32[32,512]{1,0:T(8,128)}) %reduce-scatter.9.cloned.1.call-update) | async-done | bytes 65552 | tf_op jit(solution)/shard_map/reduce_scatter | solution.py:562
  (1472 shorter events, 1660.5 us)
Async XLA Ops:
  8.0 60.3 %all-gather.12.cloned.1.call-start = ((), (), s32[]{:S(2)}) async-start(), calls=%async_computation.11 | async-start | bytes 1081344 | tf_op jit(solution)/shard_map/all_gather | solution.py:234
  8.7 115.2 %copy-start.20 = (bf16[512,1024]{1,0:T(8,128)(2,1)S(1)}, bf16[512,1024]{1,0:T(8,128)(2,1)}, u32[]{:S(2)}) copy-start(bf16[512,1024]{1,0:T(8,128)(2,1)} %param.600) | copy-start | bytes 3145732
  8.8 115.2 %all-gather.14.cloned.1.call-start = ((), (), s32[]{:S(2)}) async-start(), calls=%async_computation.12 | async-start | bytes 1081344 | tf_op jit(solution)/shard_map/all_gather | solution.py:235
  9.5 302.9 %all-gather.10.cloned.1.call-start = ((), (), s32[]{:S(2)}) async-start(), calls=%async_computation.10 | async-start | bytes 2162688 | tf_op jit(solution)/shard_map/all_gather | solution.py:233
  10.2 316.8 %all-gather.16.cloned.1.call-start = ((), (), s32[]{:S(2)}) async-start(), calls=%async_computation.13 | async-start | bytes 8912896 | tf_op jit(solution)/shard_map/all_gather | solution.py:281
  55.5 256.9 %copy-start.240 = (f32[1024]{0:T(1024)}, f32[1024]{0:T(1024)S(1)}, u32[]{:S(2)}) copy-start(f32[1024]{0:T(1024)S(1)} %convert_element_type.789) | copy-start | bytes 12292
  57.6 254.8 %copy-start.247 = (f32[512]{0:T(512)}, f32[512]{0:T(512)S(1)}, u32[]{:S(2)}) copy-start(f32[512]{0:T(512)S(1)} %fusion.2181) | copy-start | bytes 6148
  57.9 257.6 %copy-start.132 = (f32[512,32]{0,1:T(8,128)}, f32[512,32]{0,1:T(8,128)S(1)}, u32[]{:S(2)}) copy-start(f32[512,32]{0,1:T(8,128)S(1)} %get-tuple-element.7899) | copy-start | bytes 196612
  70.7 86.8 %copy-start.206 = (s32[1,32]{1,0:T(1,128)S(1)}, s32[1,32]{1,0:T(1,128)}, u32[]{:S(2)}) copy-start(s32[1,32]{1,0:T(1,128)} %param.610) | copy-start | bytes 388
  70.7 147.9 %copy-start.290 = (s32[4]{0:T(128)S(1)}, s32[4]{0:T(128)}, u32[]{:S(2)}) copy-start(s32[4]{0:T(128)} %constant.6731.clone.1) | copy-start | bytes 52
  70.7 148.7 %copy-start.289 = (s32[3]{0:T(128)S(1)}, s32[3]{0:T(128)}, u32[]{:S(2)}) copy-start(s32[3]{0:T(128)} %constant.6721.clone.1) | copy-start | bytes 40
  70.7 150.0 %copy-start.286 = (bf16[32,32]{1,0:T(8,128)(2,1)S(1)}, bf16[32,32]{1,0:T(8,128)(2,1)}, u32[]{:S(2)}) copy-start(bf16[32,32]{1,0:T(8,128)(2,1)} %param.608) | copy-start | bytes 6148
  70.9 193.6 %copy-start.207 = (s32[512,8]{0,1:T(8,128)S(1)}, s32[512,8]{0,1:T(8,128)}, u32[]{:S(2)}) copy-start(s32[512,8]{0,1:T(8,128)} %param.611) | copy-start | bytes 49156
  71.8 271.3 %all-gather.18.cloned.1.call-start = ((), (), s32[]{:S(2)}) async-start(), calls=%async_computation.14 | async-start | bytes 8912896 | tf_op jit(solution)/shard_map/all_gather | solution.py:282
  126.9 394.1 %all-gather.20.cloned.1.call-start = ((), (), s32[]{:S(2)}) async-start(), calls=%async_computation.15 | async-start | bytes 2162688 | tf_op jit(solution)/shard_map/all_gather | solution.py:236
  327.0 159.5 %copy-start.51 = (bf16[8,512,64]{1,2,0:T(8,128)(2,1)}, bf16[8,512,64]{1,2,0:T(8,128)(2,1)S(1)}, u32[]{:S(2)}) copy-start(bf16[8,512,64]{1,2,0:T(8,128)(2,1)S(1)} %get-tuple-element.7709) | copy-start | bytes 1572868
  327.0 174.5 %copy-start = (bf16[8,512,64]{1,2,0:T(8,128)(2,1)}, bf16[8,512,64]{1,2,0:T(8,128)(2,1)S(1)}, u32[]{:S(2)}) copy-start(bf16[8,512,64]{1,2,0:T(8,128)(2,1)S(1)} %get-tuple-element.7722) | copy-start | bytes 1572868
  556.0 192.7 %all-to-all-start.2 = ((bf16[16,2,160,1024]{3,2,1,0:T(8,128)(2,1)}), bf16[16,2,160,1024]{3,2,1,0:T(8,128)(2,1)}, u32[]{:S(2)}, u32[]{:S(2)}) async-start(bf16[16,2,160,1024]{3,2,1,0:T(8,128)(2,1)} %multiply_convert_fusion.64), calls=%async_computation.2 | async-start | bytes 20971520 | tf_op jit(solution)/shard_map/all_to_all | solution.py:367
  748.8 232.5 %all-to-all-start = ((bf16[16,2,160,1024]{3,2,1,0:T(8,128)(2,1)}), bf16[16,2,160,1024]{3,2,1,0:T(8,128)(2,1)}, u32[]{:S(2)}, u32[]{:S(2)}) async-start(bf16[16,2,160,1024]{3,2,1,0:T(8,128)(2,1)} %bitcast.3556), calls=%async_computation | async-start | bytes 20971520 | tf_op jit(solution)/shard_map/all_to_all | solution.py:345
  794.0 83.9 %all-gather.22.cloned.1.call-start = ((), (), s32[]{:S(2)}) async-start(), calls=%async_computation.16 | async-start | bytes 9437184 | tf_op jit(solution)/shard_map/all_gather | solution.py:241
  883.7 119.0 %copy-start.36 = (bf16[1,1024,1024]{1,2,0:T(8,128)(2,1)}, bf16[1,1024,1024]{1,2,0:T(8,128)(2,1)S(1)}, u32[]{:S(2)}) copy-start(bf16[1,1024,1024]{1,2,0:T(8,128)(2,1)S(1)} %get-tuple-element.7626) | copy-start | bytes 6291460
  1046.0 415.2 %all-to-all-start.1 = ((f32[16,2,160,1024]{3,2,1,0:T(8,128)}), f32[16,2,160,1024]{3,2,1,0:T(8,128)}, u32[]{:S(2)}, u32[]{:S(2)}) async-start(f32[16,2,160,1024]{3,2,1,0:T(8,128)} %bitcast.3553), calls=%async_computation.1 | async-start | bytes 41943040 | tf_op jit(solution)/shard_map/all_to_all | solution.py:194
  1461.2 88.0 %copy-start.27 = (bf16[512,1024]{1,0:T(8,128)(2,1)S(1)}, bf16[512,1024]{1,0:T(8,128)(2,1)}, u32[]{:S(2)}) copy-start(bf16[512,1024]{1,0:T(8,128)(2,1)} %param.601) | copy-start | bytes 3145732
  1461.2 558.1 %all-to-all-start.3 = ((f32[16,2,160,1024]{3,2,1,0:T(8,128)}), f32[16,2,160,1024]{3,2,1,0:T(8,128)}, u32[]{:S(2)}, u32[]{:S(2)}) async-start(f32[16,2,160,1024]{3,2,1,0:T(8,128)} %bitcast.3552), calls=%async_computation.3 | async-start | bytes 41943040 | tf_op jit(solution)/shard_map/all_to_all | solution.py:194
  1548.5 895.6 %all-gather.24.cloned.1.call-start = ((), (), s32[]{:S(2)}) async-start(), calls=%async_computation.17 | async-start | bytes 17825792 | tf_op jit(solution)/shard_map/all_gather | solution.py:480
  1549.2 1067.5 %all-gather.26.cloned.1.call-start = ((), (), s32[]{:S(2)}) async-start(), calls=%async_computation.18 | async-start | bytes 17825792 | tf_op jit(solution)/shard_map/all_gather | solution.py:481
  2065.1 1061.3 %reduce-scatter.17.cloned.1.call-start = ((), (), s32[]{:S(2)}) async-start(), calls=%async_computation.24 | async-start | bytes 18874368 | tf_op jit(solution)/shard_map/reduce_scatter | solution.py:401
  2125.7 1000.6 %reduce-scatter.15.cloned.1.call-start = ((), (), s32[]{:S(2)}) async-start(), calls=%async_computation.23 | async-start | bytes 540672 | tf_op jit(solution)/shard_map/reduce_scatter | solution.py:565
  2334.3 792.1 %reduce-scatter.7.cloned.1.call-start = ((), (), s32[]{:S(2)}) async-start(), calls=%async_computation.19 | async-start | bytes 4325376 | tf_op jit(solution)/shard_map/reduce_scatter | solution.py:561
  2339.0 787.3 %reduce-scatter.13.cloned.1.call-start = ((), (), s32[]{:S(2)}) async-start(), calls=%async_computation.22 | async-start | bytes 4325376 | tf_op jit(solution)/shard_map/reduce_scatter | solution.py:564
  2590.8 618.1 %reduce-scatter.11.cloned.1.call-start = ((), (), s32[]{:S(2)}) async-start(), calls=%async_computation.21 | async-start | bytes 2162688 | tf_op jit(solution)/shard_map/reduce_scatter | solution.py:563
  3074.7 270.1 %reduce-scatter.9.cloned.1.call-start = ((), (), s32[]{:S(2)}) async-start(), calls=%async_computation.20 | async-start | bytes 2162688 | tf_op jit(solution)/shard_map/reduce_scatter | solution.py:562
  (295 other events, 1726.0 us)
Sparse Core Ops, SparseCore 0:
  11.7 56.5 all-gather.11
  71.2 52.7 all-gather.13
  126.8 55.3 all-gather.9
  184.8 79.2 all-gather.15
  266.7 76.3 all-gather.17
  345.9 54.8 all-gather.19
  1551.5 436.3 all-gather.23
  2065.2 208.3 all-gather.25
Sparse Core Ops, SparseCore 1:
  797.3 80.5 all-gather.21
  2125.8 227.0 reduce-scatter.16
  2355.5 193.0 reduce-scatter.14
  2551.5 137.8 reduce-scatter.6
  2692.4 136.8 reduce-scatter.12
  3074.8 134.2 reduce-scatter.10
  3211.7 133.0 reduce-scatter.8
where the time goes:
time: 3370 us; the launch traced here: 3350 us
  waiting for transfers between devices  1380 us (41%)
  local copies, waits for them, and re-layouts  656 us (19%)
  matrix products  547 us (16%)
  blocking collectives  245 us (7%)
  other arithmetic  211 us (6%)
  starting transfers between devices  185 us (5%)
  between operations  105 us (3%)
    all_to_all x2, waiting for transfers between devices, natural_return(): lax.all_to_all(partials, 'ctx', split_axis=0, concat_axis=0, tiled=True)  753 us
    all_to_all x1, waiting for transfers between devices, per_device(): lax.all_to_all(outgoing_grad, 'ctx', split_axis=0, concat_axis=0, tiled=T...  164 us
    reduce_scatter x1, waiting for transfers between devices, per_device(): lax.psum_scatter(key_weight_grad, ('dp', 'ctx'), scatter_dimension=0, til...  136 us
    another operation x103, local copies, waits for them, and re-layouts, pair_blocks(): jnp.stack([heads_major(rows[base + i * BLK:base + (i + 1) * BLK], groups,...  135 us
    all_to_all x2, starting transfers between devices, natural_return(): lax.all_to_all(partials, 'ctx', split_axis=0, concat_axis=0, tiled=True)  133 us
    transpose x68, local copies, waits for them, and re-layouts, heads_major(): block_rows.reshape(count, groups, head_ratio, head_size)  106 us
    all_gather x1, blocking collectives, per_device(): lax.all_gather(log_total, 'ctx', axis=0, tiled=True)  101 us
    slice x45, local copies, waits for them, and re-layouts, pair_blocks(): rows[base + i * BLK:base + (i + 1) * BLK]  94.8 us
  transfers between devices with their start and end apart: 19, of which 10 were waited for; matrix products, arithmetic and copies ran while one was open for 39% of the time, Pallas kernels for 0%

commit v1 on v0

--- a/solution.py
+++ b/solution.py
@@ -3,6 +3,8 @@
 import jax
 import jax.numpy as jnp
 from jax import lax
+from jax.experimental import pallas as pl
+from jax.experimental.pallas import tpu as pltpu
 from jax.sharding import PartitionSpec as P
 
 D = 1024
@@ -64,7 +66,7 @@
 def pair_blocks(rows, base, groups, head_ratio, head_size):
     return jnp.stack(
         [
-            heads_major(rows[base + i * BLK : base + (i + 1) * BLK], groups, head_ratio, head_size)
+            heads_major(lax.dynamic_slice_in_dim(rows, base + i * BLK, BLK), groups, head_ratio, head_size)
             for i in range(2)
         ]
     )
@@ -212,7 +214,7 @@
     ).reshape(devices, local_count, CAP, width)
 
 
-def per_device(
+def general_device(
     tokens,
     grad_out,
     w_query,
@@ -280,7 +282,7 @@
     carry_state = initial
     key_rows = lax.all_gather(key_proj, "ctx", axis=0, tiled=True)
     value_rows = lax.all_gather(value_proj, "ctx", axis=0, tiled=True)
-    for j in range(key_rows.shape[0] // (2 * BLK)):
+    def forward_step(j, carry_state):
         key_pair = pair_blocks(key_rows, j * 2 * BLK, KVH, 1, HD)
         value_pair = pair_blocks(value_rows, j * 2 * BLK, KVH, 1, HD)
         block_pair = lax.dynamic_slice_in_dim(group_blocks, 2 * j, 2)
@@ -313,6 +315,9 @@
             keep_state,
             carry_state,
         )
+        return carry_state
+
+    carry_state = lax.fori_loop(0, key_rows.shape[0] // (2 * BLK), forward_step, carry_state)
     running_max, running_sum, accumulated = carry_state
     attended_heads = accumulated / running_sum[..., None]
     log_total = running_max + jnp.log(running_sum)
@@ -433,7 +438,7 @@
     accumulated_grad = query_start
     key_rows = lax.all_gather(key_proj, "ctx", axis=0, tiled=True)
     value_rows = lax.all_gather(value_proj, "ctx", axis=0, tiled=True)
-    for j in range(key_rows.shape[0] // (2 * BLK)):
+    def query_step(j, accumulated_grad):
         key_pair = pair_blocks(key_rows, j * 2 * BLK, KVH, 1, HD)
         value_pair = pair_blocks(value_rows, j * 2 * BLK, KVH, 1, HD)
         block_pair = lax.dynamic_slice_in_dim(group_blocks, 2 * j, 2)
@@ -464,6 +469,9 @@
             score_scale,
         )
         accumulated_grad = lax.cond(same, second_update, keep_state, accumulated_grad)
+        return accumulated_grad
+
+    accumulated_grad = lax.fori_loop(0, key_rows.shape[0] // (2 * BLK), query_step, accumulated_grad)
     zero_keys = jnp.zeros((2, KVH, BLK, HD), jnp.float32)
     key_start = key_update(
         query_heads[query_low],
@@ -479,7 +487,7 @@
     start_row = jnp.int32(0)
     query_rows = lax.all_gather(queries, "ctx", axis=0, tiled=True)
     grad_piece = lax.all_gather(attended_grad, "ctx", axis=0, tiled=True)
-    for j in range(query_rows.shape[0] // (2 * BLK)):
+    def key_step(j, carry_state):
         slot_first = start_row // BLK + 2 * j
         query_pair = pair_blocks(query_rows, j * 2 * BLK, KVH, head_ratio, HD)
         grad_pair = pair_blocks(grad_piece, j * 2 * BLK, KVH, head_ratio, HD)
@@ -513,6 +521,9 @@
             score_scale,
         )
         carry_state = lax.cond(same, second_update, keep_state, carry_state)
+        return carry_state
+
+    carry_state = lax.fori_loop(0, query_rows.shape[0] // (2 * BLK), key_step, carry_state)
     key_grad_heads, value_grad_heads = carry_state
     query_grad_rows = jnp.concatenate(
         [rows_major(accumulated_grad[i], KVH, head_ratio, HD) for i in range(2)], axis=0
@@ -576,6 +587,820 @@
         owned[5],
         owned[6],
         owned[4],
+        expert_grad,
+    )
+
+
+TILE = 512
+VMEM_BYTES = 60 * 1024 * 1024
+CHANNELS = 3 * HD
+
+
+def nn(a, b):
+    return jnp.dot(a, b, preferred_element_type=jnp.float32)
+
+
+def nt(a, b):
+    return lax.dot_general(a, b, (((1,), (1,)), ((), ())), preferred_element_type=jnp.float32)
+
+
+def tn(a, b):
+    return lax.dot_general(a, b, (((0,), (0,)), ((), ())), preferred_element_type=jnp.float32)
+
+
+def tt(a, b):
+    return lax.dot_general(a, b, (((0,), (1,)), ((), ())), preferred_element_type=jnp.float32)
+
+
+def attention_forward_kernel(seq, table, packed, *refs):
+    out, out_rows, log_sum, q_seq, k_seq, v_seq = refs[-6:]
+    if seq > 0:
+        out[...] = refs[0][...]
+    seq_rows = BLOCKS * BLK
+    for g in range(BLOCKS):
+        slot = table[seq * BLOCKS + g]
+        lanes = pl.ds(pl.multiple_of((slot % 2) * BLK, BLK), BLK)
+        here = slice(g * BLK, (g + 1) * BLK)
+        source = packed.at[slot // 2]
+        q_seq[:, here] = source[0:HD, lanes] * jnp.bfloat16(HD**-0.5)
+        k_seq[here, :] = source[HD : 2 * HD, lanes].astype(jnp.float32).T.astype(jnp.bfloat16)
+        v_seq[:, here] = source[2 * HD : 3 * HD, lanes]
+
+    def update(q, state, start, size):
+        top, total, acc = state
+        rows = pl.ds(start, size)
+        scores = nn(k_seq[rows, :], q)
+        new_top = jnp.maximum(top, jnp.max(scores, axis=0, keepdims=True))
+        factor = jnp.exp(top - new_top)
+        weights = jnp.exp(scores - new_top)
+        total = total * factor + jnp.sum(weights, axis=0, keepdims=True)
+        acc = acc * factor + nn(v_seq[:, rows], weights.astype(jnp.bfloat16))
+        return new_top, total, acc
+
+    def one_tile(n, carry):
+        mine = pl.multiple_of(n * TILE, TILE)
+        q = q_seq[:, pl.ds(mine, TILE)]
+        state = (
+            jnp.full((1, TILE), floor_value, jnp.float32),
+            jnp.zeros((1, TILE), jnp.float32),
+            jnp.zeros((HD, TILE), jnp.float32),
+        )
+        state = lax.fori_loop(
+            0,
+            n,
+            lambda k, c: update(q, c, pl.multiple_of(k * TILE, TILE), TILE),
+            state,
+        )
+        state = update(q, state, mine, BLK)
+        late = update(q[:, BLK:], tuple(s[:, BLK:] for s in state), mine + BLK, BLK)
+        top, total, acc = (
+            jnp.concatenate([s[:, :BLK], t], axis=1) for s, t in zip(state, late)
+        )
+        final = acc / total
+        out_rows[:, pl.ds(mine, TILE)] = final
+        log_sum[:, pl.ds(mine, TILE)] = top + jnp.log(total)
+        return carry
+
+    lax.fori_loop(0, seq_rows // TILE, one_tile, 0)
+    for g in range(BLOCKS):
+        slot = table[seq * BLOCKS + g]
+        lanes = pl.ds(pl.multiple_of((slot % 2) * BLK, BLK), BLK)
+        out[slot // 2, :, lanes] = out_rows[:, g * BLK : (g + 1) * BLK].astype(jnp.bfloat16)
+
+
+def attention_backward_kernel(
+    table, packed, d_out, out_rows_0, out_rows_1, log_sum, grads, q_seq, k_cols, v_cols, k_seq, v_seq, d_seq,
+    delta, dq, dk, dv
+):
+    block_count = 2 * packed.shape[0]
+    seq_rows = BLOCKS * BLK
+    for g in range(block_count):
+        slot = table[g]
+        lanes = pl.ds(pl.multiple_of((slot % 2) * BLK, BLK), BLK)
+        here = slice(g * BLK, (g + 1) * BLK)
+        source = packed.at[slot // 2]
+        q_seq[:, here] = source[0:HD, lanes] * jnp.bfloat16(HD**-0.5)
+        k_block = source[HD : 2 * HD, lanes]
+        v_block = source[2 * HD : 3 * HD, lanes]
+        k_cols[:, here] = k_block
+        k_seq[here, :] = k_block.astype(jnp.float32).T.astype(jnp.bfloat16)
+        v_seq[here, :] = v_block.astype(jnp.float32).T.astype(jnp.bfloat16)
+        d_block = d_out[slot // 2, :, lanes]
+        d_seq[:, here] = d_block
+        delta[:, here] = jnp.sum(
+            d_block.astype(jnp.float32)
+            * (out_rows_0, out_rows_1)[g // BLOCKS][
+                :, g % BLOCKS * BLK : (g % BLOCKS + 1) * BLK
+            ],
+            axis=0,
+            keepdims=True,
+        )
+    dq[...] = jnp.zeros_like(dq)
+
+    def pair(k_start, k_size, q_start, q_size, first):
+        keys = pl.ds(k_start, k_size)
+        cols = pl.ds(q_start, q_size)
+        q = q_seq[:, cols]
+        d = d_seq[:, cols]
+        probs = jnp.exp(nn(k_seq[keys, :], q) - log_sum[:, cols])
+        d_scores = (probs * (nn(v_seq[keys, :], d) - delta[:, cols])).astype(jnp.bfloat16)
+        new_v = nt(d, probs.astype(jnp.bfloat16))
+        new_k = nt(q, d_scores)
+        if first:
+            dv[:, keys] = new_v
+            dk[:, keys] = new_k
+        else:
+            dv[:, keys] += new_v
+            dk[:, keys] += new_k
+        dq[:, cols] += nn(k_cols[:, keys], d_scores)
+
+    def one_tile(n, carry):
+        per_seq = seq_rows // TILE
+        mine = pl.multiple_of(n * TILE, TILE)
+        last = (n // per_seq + 1) * per_seq
+        pair(mine, BLK, mine, TILE, True)
+        pair(mine + BLK, BLK, mine + BLK, BLK, True)
+
+        def step(t, c):
+            pair(mine, TILE, pl.multiple_of(t * TILE, TILE), TILE, False)
+            return c
+
+        lax.fori_loop(n + 1, last, step, 0)
+        return carry
+
+    lax.fori_loop(0, 2 * seq_rows // TILE, one_tile, 0)
+    for g in range(block_count):
+        slot = table[g]
+        lanes = pl.ds(pl.multiple_of((slot % 2) * BLK, BLK), BLK)
+        here = slice(g * BLK, (g + 1) * BLK)
+        grads[slot // 2, 0:HD, lanes] = (dq[:, here] * HD**-0.5).astype(jnp.bfloat16)
+        grads[slot // 2, HD : 2 * HD, lanes] = dk[:, here].astype(jnp.bfloat16)
+        grads[slot // 2, 2 * HD : 3 * HD, lanes] = dv[:, here].astype(jnp.bfloat16)
+
+
+def work(microseconds):
+    return int(microseconds * 1.15e9)
+
+
+def params():
+    return pltpu.CompilerParams(vmem_limit_bytes=VMEM_BYTES)
+
+
+def attention_forward(seq, table, packed, *kept):
+    count, _, row_count = packed.shape
+    total = BLOCKS * BLK
+    whole = pl.BlockSpec(memory_space=pltpu.VMEM)
+    return pl.pallas_call(
+        partial(attention_forward_kernel, seq),
+        out_shape=(
+            jax.ShapeDtypeStruct((count, HD, row_count), jnp.bfloat16),
+            jax.ShapeDtypeStruct((HD, total), jnp.float32),
+            jax.ShapeDtypeStruct((1, total), jnp.float32),
+        ),
+        in_specs=[pl.BlockSpec(memory_space=pltpu.SMEM), whole] + [whole] * len(kept),
+        out_specs=(whole,) * 3,
+        scratch_shapes=[
+            pltpu.VMEM((HD, total), jnp.bfloat16),
+            pltpu.VMEM((total, HD), jnp.bfloat16),
+            pltpu.VMEM((HD, total), jnp.bfloat16),
+        ],
+        compiler_params=params(),
+        cost_estimate=pl.CostEstimate(
+            flops=work(27), bytes_accessed=packed.size * 2, transcendentals=total * total // 2
+        ),
+        name="attention_forward",
+    )(table, packed, *kept)
+
+
+def attention_backward(table, packed, d_out, out_rows_0, out_rows_1, log_sum):
+    count, _, row_count = packed.shape
+    total = count * row_count
+    pairs = total * BLOCKS * BLK // 2
+    return pl.pallas_call(
+        attention_backward_kernel,
+        out_shape=jax.ShapeDtypeStruct(packed.shape, jnp.bfloat16),
+        in_specs=[pl.BlockSpec(memory_space=pltpu.SMEM)]
+        + [pl.BlockSpec(memory_space=pltpu.VMEM)] * 5,
+        out_specs=pl.BlockSpec(memory_space=pltpu.VMEM),
+        scratch_shapes=[
+            pltpu.VMEM((HD, total), jnp.bfloat16),
+            pltpu.VMEM((HD, total), jnp.bfloat16),
+            pltpu.VMEM((HD, total), jnp.bfloat16),
+            pltpu.VMEM((total, HD), jnp.bfloat16),
+            pltpu.VMEM((total, HD), jnp.bfloat16),
+            pltpu.VMEM((HD, total), jnp.bfloat16),
+            pltpu.VMEM((1, total), jnp.float32),
+            pltpu.VMEM((HD, total), jnp.float32),
+            pltpu.VMEM((HD, total), jnp.float32),
+            pltpu.VMEM((HD, total), jnp.float32),
+        ],
+        compiler_params=params(),
+        cost_estimate=pl.CostEstimate(
+            flops=work(61), bytes_accessed=packed.size * 6, transcendentals=pairs
+        ),
+        name="attention_backward",
+    )(table, packed, d_out, out_rows_0, out_rows_1, log_sum)
+
+
+def slot_match(places, rows):
+    numbers = lax.broadcasted_iota(jnp.int32, (rows, places.shape[1]), 0).astype(jnp.float32)
+    return numbers == places
+
+
+def column_match(places, columns):
+    numbers = lax.broadcasted_iota(jnp.int32, (places.shape[0], columns), 1).astype(jnp.float32)
+    return jnp.where(numbers == places, 1.0, 0.0).astype(jnp.bfloat16)
+
+
+def grad_kernel(count, order, places, *refs):
+    sources, weights = refs[:count], refs[count]
+    slot_rows, d_hidden, rows = refs[-3:]
+    g = pl.program_id(0)
+    for k, source in enumerate(sources):
+
+        @pl.when(g == k)
+        def _(source=source):
+            rows[...] = source[...]
+
+    for e in range(places.shape[1]):
+        pick = jnp.where(slot_match(places[0, e : e + 1, :], CAP), 1.0, 0.0).astype(jnp.bfloat16)
+        picked = nn(pick, rows[...]).astype(jnp.bfloat16)
+        slot_rows[e] = picked
+        d_hidden[e] = nn(picked, weights[0, :, e * F : (e + 1) * F]).astype(jnp.bfloat16)
+
+
+def grad_step(first, order, places, blocks, weights, kept):
+    devices, local, row_count = places.shape
+    count = len(blocks)
+    kept = () if kept is None else tuple(kept)
+    block = pl.BlockSpec((row_count, D), lambda g, order: (0, 0))
+    return pl.pallas_call(
+        partial(grad_kernel, count),
+        grid_spec=pltpu.PrefetchScalarGridSpec(
+            num_scalar_prefetch=1,
+            grid=(count,),
+            in_specs=[
+                pl.BlockSpec((1, local, row_count), lambda g, order: (order[g], 0, 0)),
+                *([block] * count),
+                pl.BlockSpec((1, D, local * F), lambda g, order: (2, 0, 0)),
+            ]
+            + [pl.BlockSpec(memory_space=pl.ANY)] * len(kept),
+            out_specs=(
+                pl.BlockSpec((local, CAP, D), lambda g, order: (0, first + g, 0)),
+                pl.BlockSpec((local, CAP, F), lambda g, order: (0, first + g, 0)),
+            ),
+            scratch_shapes=[pltpu.VMEM((row_count, D), jnp.bfloat16)],
+        ),
+        out_shape=(
+            jax.ShapeDtypeStruct((local, devices * CAP, D), jnp.bfloat16),
+            jax.ShapeDtypeStruct((local, devices * CAP, F), jnp.bfloat16),
+        ),
+        input_output_aliases={count + 3 + i: i for i in range(len(kept))},
+        compiler_params=params(),
+        cost_estimate=pl.CostEstimate(
+            flops=work(2 * count + 2), bytes_accessed=count * row_count * D * 4, transcendentals=0
+        ),
+        name="grad_step",
+    )(order, places, *blocks, weights, *kept)
+
+
+def expert_kernel(count, order, places, columns, gates, *refs):
+    sources, (d_hidden, weights) = refs[:count], refs[count : count + 2]
+    slot_rows, hidden, d_gate_pre, d_up, d_gate, near, far, rows = refs[-8:]
+    g = pl.program_id(0)
+    for k, source in enumerate(sources):
+
+        @pl.when(g == k)
+        def _(source=source):
+            rows[...] = source[...]
+
+    total = None
+    for e in range(places.shape[1]):
+        here = slice(e * F, (e + 1) * F)
+        match = slot_match(places[0, e : e + 1, :], CAP)
+        pick = jnp.where(match, 1.0, 0.0)
+        picked = nn(pick.astype(jnp.bfloat16), rows[...]).astype(jnp.bfloat16)
+        slot_rows[e] = picked
+        gate_pre = nn(picked, weights[0, :, here])
+        up_pre = nn(picked, weights[1, :, here])
+        gate = jnp.sum(jnp.where(match, gates[0, e : e + 1, :], 0.0), axis=1, keepdims=True)
+        raw = d_hidden[e].astype(jnp.float32)
+        sig = 1.0 / (1.0 + jnp.exp(-gate_pre))
+        silu = gate_pre * sig
+        value = silu * up_pre
+        hidden[e] = (gate * value).astype(jnp.bfloat16)
+        scaled = raw * gate
+        up_grad = (scaled * silu).astype(jnp.bfloat16)
+        pre_grad = (scaled * up_pre * sig * (1.0 + gate_pre * (1.0 - sig))).astype(jnp.bfloat16)
+        d_up[e] = up_grad
+        d_gate_pre[e] = pre_grad
+        slot_gate = jnp.sum(raw * value, axis=1, keepdims=True)
+        d_gate[0, e : e + 1, :] = jnp.sum(pick * slot_gate, axis=0, keepdims=True)
+        back = (nt(pre_grad, weights[0, :, here]) + nt(up_grad, weights[1, :, here])).astype(
+            jnp.bfloat16
+        )
+        spread = nn(column_match(columns[0, :, e : e + 1], CAP), back)
+        total = spread if total is None else total + spread
+    result = total.astype(jnp.bfloat16)
+
+    @pl.when(g < count // 2)
+    def _():
+        near[0] = result
+
+    @pl.when(g >= count // 2)
+    def _():
+        far[0] = result
+
+
+def expert_step(first, order, places, columns, gates, blocks, d_hidden, weights, kept):
+    devices, local, row_count = places.shape
+    count = len(blocks)
+    wide_slots = pl.BlockSpec((local, CAP, D), lambda g, order: (0, first + g, 0))
+    slots = pl.BlockSpec((local, CAP, F), lambda g, order: (0, first + g, 0))
+    block = pl.BlockSpec((row_count, D), lambda g, order: (0, 0))
+    kept = () if kept is None else tuple(kept)
+    first_kept = 6 + count
+    half = count // 2
+    return pl.pallas_call(
+        partial(expert_kernel, count),
+        grid_spec=pltpu.PrefetchScalarGridSpec(
+            num_scalar_prefetch=1,
+            grid=(count,),
+            in_specs=[
+                pl.BlockSpec((1, local, row_count), lambda g, order: (order[g], 0, 0)),
+                pl.BlockSpec((1, row_count, local), lambda g, order: (order[g], 0, 0)),
+                pl.BlockSpec((1, local, row_count), lambda g, order: (order[g], 0, 0)),
+                *([block] * count),
+                slots,
+                pl.BlockSpec((2, D, local * F), lambda g, order: (0, 0, 0)),
+            ]
+            + [pl.BlockSpec(memory_space=pl.ANY)] * len(kept),
+            out_specs=(
+                wide_slots,
+                slots,
+                slots,
+                slots,
+                pl.BlockSpec((1, local, row_count), lambda g, order: (g, 0, 0)),
+                pl.BlockSpec((1, row_count, D), lambda g, order: (jnp.minimum(g, half - 1), 0, 0)),
+                pl.BlockSpec((1, row_count, D), lambda g, order: (jnp.maximum(g - half, 0), 0, 0)),
+            ),
+            scratch_shapes=[pltpu.VMEM((row_count, D), jnp.bfloat16)],
+        ),
+        out_shape=(
+            jax.ShapeDtypeStruct((local, devices * CAP, D), jnp.bfloat16),
+            jax.ShapeDtypeStruct((local, devices * CAP, F), jnp.bfloat16),
+            jax.ShapeDtypeStruct((local, devices * CAP, F), jnp.bfloat16),
+            jax.ShapeDtypeStruct((local, devices * CAP, F), jnp.bfloat16),
+            jax.ShapeDtypeStruct((count, local, row_count), jnp.float32),
+            jax.ShapeDtypeStruct((half, row_count, D), jnp.bfloat16),
+            jax.ShapeDtypeStruct((half, row_count, D), jnp.bfloat16),
+        ),
+        input_output_aliases={first_kept + i: i for i in range(len(kept))},
+        compiler_params=params(),
+        cost_estimate=pl.CostEstimate(
+            flops=work(5 * count),
+            bytes_accessed=count * row_count * D * 6,
+            transcendentals=count * local * CAP * F,
+        ),
+        name="expert_step",
+    )(order, places, columns, gates, *blocks, d_hidden, weights, *kept)
+
+
+def output_kernel(order, columns, hidden, weights, out_rows):
+    total = None
+    for e in range(columns.shape[2]):
+        out = nt(hidden[e], weights[0, :, e * F : (e + 1) * F]).astype(jnp.bfloat16)
+        spread = nn(column_match(columns[0, :, e : e + 1], CAP), out)
+        total = spread if total is None else total + spread
+    out_rows[...] = total.astype(jnp.bfloat16)
+
+
+def output_pass(order, columns, hidden, weights):
+    devices, row_count, local = columns.shape
+    return pl.pallas_call(
+        output_kernel,
+        grid_spec=pltpu.PrefetchScalarGridSpec(
+            num_scalar_prefetch=1,
+            grid=(devices,),
+            in_specs=[
+                pl.BlockSpec((1, row_count, local), lambda j, order: (order[j], 0, 0)),
+                pl.BlockSpec((local, CAP, F), lambda j, order: (0, j, 0)),
+                pl.BlockSpec((1, D, local * F), lambda j, order: (2, 0, 0)),
+            ],
+            out_specs=pl.BlockSpec((row_count, D), lambda j, order: (order[j], 0)),
+        ),
+        out_shape=jax.ShapeDtypeStruct((devices * row_count, D), jnp.bfloat16),
+        compiler_params=params(),
+        cost_estimate=pl.CostEstimate(
+            flops=work(26), bytes_accessed=devices * row_count * D * 3,
+            transcendentals=0,
+        ),
+        name="output_pass",
+    )(order, columns, hidden, weights)
+
+
+def weight_grad_kernel(half, slot_rows, slot_grads, d_gate_pre, d_up, hidden, *out):
+    out[0][...] = tn(slot_rows[0], d_gate_pre[0]).astype(out[0].dtype)
+    out[1][...] = tn(slot_rows[0], d_up[0]).astype(out[1].dtype)
+    out[2][...] = tn(slot_grads[0], hidden[0]).astype(out[2].dtype)
+
+
+def weight_grad(half, slot_rows, slot_grads, d_gate_pre, d_up, hidden, dtype):
+    local, count, _ = hidden.shape
+    wide_slots = pl.BlockSpec((1, count, D // 2), lambda e, half: (e, 0, half[0]))
+    slots = pl.BlockSpec((1, count, F), lambda e, half: (e, 0, 0))
+    return pl.pallas_call(
+        weight_grad_kernel,
+        grid_spec=pltpu.PrefetchScalarGridSpec(
+            num_scalar_prefetch=1,
+            grid=(local,),
+            in_specs=[wide_slots, wide_slots, slots, slots, slots],
+            out_specs=(pl.BlockSpec((D // 2, F), lambda e, half: (0, e)),) * 3,
+        ),
+        out_shape=(jax.ShapeDtypeStruct((D // 2, local * F), dtype),) * 3,
+        compiler_params=params(),
+        cost_estimate=pl.CostEstimate(
+            flops=work(15), bytes_accessed=local * count * D * 8, transcendentals=0
+        ),
+        name="weight_grad",
+    )(half, slot_rows, slot_grads, d_gate_pre, d_up, hidden)
+
+
+LINE = 4
+ROWS = 2
+CORES = 2
+together = lax.optimization_barrier
+
+
+def place(z, y, c):
+    return (z * ROWS + y) * CORES + c
+
+
+def move(values, target):
+    pairs = []
+    for z in range(LINE):
+        for y in range(ROWS):
+            for c in range(CORES):
+                there = target(z, y, c)
+                if there is not None and 0 <= there[0] < LINE:
+                    pairs.append((place(z, y, c), place(*there)))
+    return lax.ppermute(values, "ctx", pairs)
+
+
+def core_swap(values):
+    return move(values, lambda z, y, c: (z, y, 1 - c))
+
+
+def row_swap(values):
+    return move(values, lambda z, y, c: (z, 1 - y, c))
+
+
+def up_from(values, sources):
+    return move(values, lambda z, y, c: (z + 1, y, c) if z in sources else None)
+
+
+def down_from(values, sources):
+    return move(values, lambda z, y, c: (z - 1, y, c) if z in sources else None)
+
+
+def added(*terms):
+    total = terms[0].astype(jnp.float32)
+    for term in terms[1:]:
+        total = total + term.astype(jnp.float32)
+    return total.astype(jnp.bfloat16)
+
+
+LINE_ORDER = ((0, 1, 2, 3), (1, 2, 3, 0), (2, 1, 0, 3), (3, 2, 1, 0))
+
+
+def send_on(s, own, up, down):
+    sent = []
+    if s < LINE:
+        sent.append(row_swap(own))
+    if s < LINE - 1:
+        sent.append(up_from(up, tuple(range(s, LINE - 1))))
+        sent.append(down_from(down, tuple(range(1, LINE - s))))
+    return sent
+
+
+def newest(s, ups, downs, z):
+    if s < LINE - 1:
+        return jnp.where(z >= 2, ups[s], downs[s])
+    return jnp.where(
+        z == 0, downs[3], jnp.where(z == 1, ups[1], jnp.where(z == 2, downs[1], ups[3]))
+    )
+
+
+def near_order(position):
+    z = position // (ROWS * CORES)
+    y = position // CORES % ROWS
+    c = position % CORES
+    line = jnp.asarray(LINE_ORDER, jnp.int32)[z]
+    steps = []
+    for s in range(LINE + 1):
+        for other_core in range(CORES):
+            if s < LINE:
+                steps.append(place(line[s], y, c ^ other_core))
+            if s > 0:
+                steps.append(place(line[s - 1], 1 - y, c ^ other_core))
+    return jnp.stack(steps).astype(jnp.int32)
+
+
+def scatter_sum(near, far, z):
+    summed = [added(a, core_swap(b)) for a, b in zip(reversed(near), reversed(far))][::-1]
+    part_3 = added(summed[3][0], row_swap(summed[4][0]))
+    up_3 = up_from(part_3, (0,))
+    down_3 = down_from(part_3, (3,))
+    across_2 = row_swap(summed[3][1])
+    up_3, down_3, across_2 = together((up_3, down_3, across_2))
+    part_2 = added(summed[2][0], across_2)
+    up_2 = up_from(added(part_2, up_3), (0, 1))
+    down_2 = down_from(added(part_2, down_3), (3, 2))
+    across_1 = row_swap(summed[2][1])
+    up_2, down_2, across_1 = together((up_2, down_2, across_1))
+    part_1 = added(summed[1][0], across_1)
+    up_1 = up_from(added(jnp.where(z == 2, part_3, part_1), up_2), (0, 1, 2))
+    down_1 = down_from(added(jnp.where(z == 1, part_3, part_1), down_2), (1, 2, 3))
+    across_0 = row_swap(summed[1][1])
+    return [summed[0][0], across_0, up_1, down_1]
+
+
+def one_of(values, index, axis):
+    return lax.dynamic_index_in_dim(values, index, axis, keepdims=False)
+
+
+def owner_first(values, position):
+    c = position % CORES
+    total, width = values.shape
+    spots = LINE * ROWS
+    values = values.reshape(2, spots, CORES, total // (2 * spots * CORES), width)
+    return added(one_of(values, c, 2), core_swap(one_of(values, 1 - c, 2)))
+
+
+def owner_last(values, taken, side):
+    groups = [[spot * CORES + core for spot in range(LINE * ROWS)] for core in range(CORES)]
+    values = lax.all_to_all(
+        added(one_of(values, side, 0), taken),
+        "ctx",
+        split_axis=0,
+        concat_axis=0,
+        tiled=True,
+        axis_index_groups=groups,
+    )
+    return jnp.sum(values.astype(jnp.float32), axis=0)
+
+
+def exchange(values):
+    return lax.ppermute(values, "dp", [(0, 1), (1, 0)])
+
+
+def to_heads(values):
+    return lax.all_to_all(values, "ctx", split_axis=0, concat_axis=0, tiled=True)
+
+
+def turn(values, cosine, sine):
+    half = HD // 2
+    first, second = values[:, :half, :], values[:, half:, :]
+    return jnp.concatenate(
+        [first * cosine - second * sine, second * cosine + first * sine], axis=1
+    )
+
+
+def per_device(
+    tokens, grad_out, w_query, w_key, w_value, w_output, gain_attn, gain_ffn, w_router, w_experts,
+    deal_table, routes
+):
+    row_count = tokens.shape[0]
+    devices = lax.axis_size("ctx")
+    position = lax.axis_index("ctx")
+    side = lax.axis_index("dp")
+    both = ("dp", "ctx")
+    shard = w_query.shape[0]
+    wide = HQ * HD
+    narrow = KVH * HD
+
+    extras = jnp.concatenate(
+        [w_router, gain_attn[:, None], gain_ffn[:, None], jnp.zeros((shard, 94), jnp.bfloat16)],
+        axis=1,
+    )
+    packed_weights = lax.all_gather(
+        jnp.concatenate([w_query, w_key, w_value, extras, w_output], axis=1),
+        both,
+        axis=0,
+        tiled=True,
+    )
+    other_experts = exchange(w_experts)
+    local = w_experts.shape[2] // F
+    line_place = position // (ROWS * CORES)
+    order = near_order(position)
+
+    g_ups, g_downs, g_across, g_own = [grad_out], [grad_out], [], [grad_out]
+    for s in range(2):
+        sent = send_on(s, g_own[s], g_ups[s], g_downs[s])
+        if s == 1:
+            packed_weights, *sent = together((packed_weights, *sent))
+        else:
+            sent = together(tuple(sent))
+        g_across.append(sent[0])
+        g_ups.append(sent[1])
+        g_downs.append(sent[2])
+        g_own.append(newest(s + 1, g_ups, g_downs, line_place))
+
+    full_qkv = packed_weights[:, : wide + 2 * narrow]
+    extra_columns = packed_weights[:, wide + 2 * narrow : wide + 2 * narrow + 128]
+    full_output = packed_weights[:, wide + 2 * narrow + 128 :]
+    full_router = extra_columns[:, :E]
+    gain_attn_full = extra_columns[:, E].astype(jnp.float32)
+    gain_ffn_full = extra_columns[:, E + 1].astype(jnp.float32)
+
+    expert_ids = jnp.arange(E, dtype=jnp.int32)
+    picked = routes[:, :, None] == expert_ids[None, None, :]
+    member = jnp.any(picked, axis=1)
+    below = (jnp.arange(row_count)[:, None] > jnp.arange(row_count)[None, :]).astype(jnp.bfloat16)
+    before = nn(below, member.astype(jnp.bfloat16))
+    places = jnp.where(member, before, -1.0)
+    slot_places = to_heads(places.T.reshape(devices, local, row_count))
+
+    group_blocks = deal_table[0]
+    own_blocks = lax.dynamic_slice_in_dim(group_blocks, 2 * position, 2)
+    offsets = jnp.arange(BLK, dtype=jnp.int32)
+    positions = ((own_blocks % BLOCKS)[:, None] * BLK + offsets[None, :]).reshape(-1)
+    table = jnp.argsort(group_blocks).astype(jnp.int32)
+    frequency = 10000.0 ** (-(jnp.arange(HD // 2).astype(jnp.float32) * 2.0 / HD))
+    angles = frequency[:, None] * positions.astype(jnp.float32)[None, :]
+    cosine, sine = jnp.cos(angles)[None], jnp.sin(angles)[None]
+    inputs = tokens.astype(jnp.float32)
+    normed = rms_norm(inputs, gain_attn_full).astype(jnp.bfloat16)
+    raw = tt(full_qkv, normed)
+    queries = turn(raw[:wide].reshape(HQ, HD, row_count), cosine, sine).astype(jnp.bfloat16)
+    keys = turn(raw[wide : wide + narrow].reshape(KVH, HD, row_count), cosine, sine).astype(
+        jnp.bfloat16
+    )
+    values = raw[wide + narrow :].reshape(KVH, HD, row_count).astype(jnp.bfloat16)
+    ratio = HQ // KVH
+    outgoing = jnp.concatenate(
+        [queries, jnp.repeat(keys, ratio, axis=0), jnp.repeat(values, ratio, axis=0)], axis=1
+    )
+    outgoing, other_experts, slot_places = together((outgoing, other_experts, slot_places))
+    packed = to_heads(outgoing)
+    slot_columns = slot_places.transpose(0, 2, 1)
+    first_half = jnp.where(side == 0, w_experts, other_experts)
+    second_half = jnp.where(side == 0, other_experts, w_experts)
+    experts = jnp.concatenate([first_half, second_half], axis=1)
+    g_kept, g_first = None, 0
+    for s in range(2):
+        blocks = [g_own[s]] + g_across[s - 1 : s] if s else [g_own[0]]
+        blocks += [core_swap(b) for b in blocks]
+        count = len(blocks)
+        g_kept = grad_step(
+            g_first, order[g_first : g_first + count], slot_places, blocks, experts, g_kept
+        )
+        g_first += count
+    packed, *g_kept = together((packed, *g_kept))
+    sent = send_on(2, g_own[2], g_ups[2], g_downs[2])
+    heads, rows_0, sums_0 = attention_forward(0, table, packed)
+    heads, rows_0, sums_0, *sent = together((heads, rows_0, sums_0, *sent))
+    g_across.append(sent[0])
+    g_ups.append(sent[1])
+    g_downs.append(sent[2])
+    g_own.append(newest(3, g_ups, g_downs, line_place))
+    last_across = row_swap(g_own[3])
+    heads, rows_1, sums_1 = attention_forward(1, table, packed, heads)
+    heads, rows_1, sums_1, last_across = together((heads, rows_1, sums_1, last_across))
+    g_across.append(last_across)
+    log_sum = jnp.concatenate([sums_0, sums_1], axis=1)
+    attended = to_heads(heads)
+    for s in range(2, LINE + 1):
+        blocks = g_own[s : s + 1] + [g_across[s - 1]]
+        blocks += [core_swap(b) for b in blocks]
+        count = len(blocks)
+        g_kept = grad_step(
+            g_first, order[g_first : g_first + count], slot_places, blocks, experts, g_kept
+        )
+        g_first += count
+    attended, *g_kept = together((attended, *g_kept))
+    slot_grads, d_hidden = g_kept
+    attended = attended.reshape(wide, row_count)
+    residual = inputs + tn(attended, full_output)
+
+    normed_ffn = rms_norm(residual, gain_ffn_full).astype(jnp.bfloat16)
+    logits = nn(normed_ffn, full_router)
+    masked = jnp.where(member, logits, floor_value)
+    powers = jnp.where(member, jnp.exp(masked - jnp.max(masked, axis=1, keepdims=True)), 0.0)
+    gates = powers / jnp.sum(powers, axis=1, keepdims=True)
+    slot_gates = to_heads(gates.T.reshape(devices, local, row_count))
+    near, far, d_gate_parts, kept = [], [], [], None
+    own, across = normed_ffn, None
+    ups, downs = [normed_ffn], [normed_ffn]
+    first = 0
+    for s in range(LINE + 1):
+        blocks = [b for b in (own, across) if b is not None]
+        sent = send_on(s, own, ups[-1], downs[-1])
+        blocks += [core_swap(b) for b in blocks]
+        count = len(blocks)
+        *kept, d_gate_part, near_part, far_part = expert_step(
+            first, order[first : first + count], slot_places, slot_columns, slot_gates, blocks,
+            d_hidden, experts, kept
+        )
+        if sent:
+            *sent, near_part = together((*sent, near_part))
+        first += count
+        near.append(near_part)
+        far.append(far_part)
+        d_gate_parts.append(d_gate_part)
+        across = sent[0] if s < LINE else None
+        if s < LINE - 1:
+            ups.append(sent[1])
+            downs.append(sent[2])
+        own = newest(s + 1, ups, downs, line_place) if s < LINE - 1 else None
+    slot_rows, hidden, d_gate_pre, d_up = kept
+    arrived = scatter_sum(near, far, line_place)
+    given = weight_grad(
+        (1 - side).reshape(1), slot_rows, slot_grads, d_gate_pre, d_up, hidden, jnp.bfloat16
+    )
+    taken = [exchange(part) for part in given]
+    out_rows = output_pass(order, slot_columns, hidden, experts)
+    owned_experts = weight_grad(
+        side.reshape(1), slot_rows, slot_grads, d_gate_pre, d_up, hidden, jnp.float32
+    )
+    *arrived, out_rows, taken[0], taken[1], owned_experts = together(
+        (*arrived, out_rows, taken[0], taken[1], owned_experts)
+    )
+    ffn_grad = sum(part.astype(jnp.float32) for part in arrived)
+    back = jnp.argsort(order)
+    d_gate = to_heads(jnp.concatenate(d_gate_parts, axis=0)[back]).reshape(E, row_count).T
+    mixture = lax.psum_scatter(out_rows, "ctx", scatter_dimension=0, tiled=True)
+
+    d_logits = gates * (d_gate - jnp.sum(gates * d_gate, axis=1, keepdims=True))
+    ffn_grad = ffn_grad + jnp.einsum(
+        "re,de->rd", d_logits, full_router.astype(jnp.float32), precision=highest
+    )
+    router_grad = jnp.einsum(
+        "rd,re->de", normed_ffn.astype(jnp.float32), d_logits, precision=highest
+    )
+    _, norm_back_ffn = jax.vjp(rms_norm, residual, gain_ffn_full)
+    residual_norm_grad, gain_ffn_grad = norm_back_ffn(ffn_grad)
+    residual_grad = grad_out.astype(jnp.float32) + residual_norm_grad
+    branch_grad = residual_grad.astype(jnp.bfloat16)
+    attended_grad = nt(full_output, branch_grad).astype(jnp.bfloat16)
+    d_heads = to_heads(attended_grad.reshape(HQ, HD, row_count))
+    output_grad = nn(attended, branch_grad)
+    first_parts = owner_first(
+        jnp.concatenate(
+            [
+                output_grad.astype(jnp.bfloat16),
+                router_grad.astype(jnp.bfloat16),
+                gain_ffn_grad[:, None].astype(jnp.bfloat16),
+                jnp.zeros((D, 95), jnp.bfloat16),
+            ],
+            axis=1,
+        ),
+        position,
+    )
+    d_heads, first_parts, taken[2] = together((d_heads, first_parts, taken[2]))
+    first_taken = exchange(one_of(first_parts, 1 - side, 0))
+
+    d_packed = to_heads(attention_backward(table, packed, d_heads, rows_0, rows_1, log_sum))
+    d_packed, first_taken = together((d_packed, first_taken))
+    first_owned = owner_last(first_parts, first_taken, side)
+    d_packed = d_packed.astype(jnp.float32)
+    d_query = turn(d_packed[:, :HD], cosine, -sine).astype(jnp.bfloat16).reshape(wide, row_count)
+    pairs = d_packed[:, HD:].reshape(KVH, ratio, 2 * HD, row_count).sum(axis=1)
+    d_key = turn(pairs[:, :HD], cosine, -sine).astype(jnp.bfloat16).reshape(narrow, row_count)
+    d_value = pairs[:, HD:].astype(jnp.bfloat16).reshape(narrow, row_count)
+    d_qkv = jnp.concatenate([d_query, d_key, d_value], axis=0)
+    qkv_grad = tt(normed, d_qkv)
+    normed_grad = tt(d_qkv, full_qkv)
+    _, norm_back_attn = jax.vjp(rms_norm, inputs, gain_attn_full)
+    input_norm_grad, gain_attn_grad = norm_back_attn(normed_grad)
+    tokens_grad = residual_grad + input_norm_grad
+    owned_parts = owner_first(
+        jnp.concatenate(
+            [
+                qkv_grad.astype(jnp.bfloat16),
+                gain_attn_grad[:, None].astype(jnp.bfloat16),
+                jnp.zeros((D, 127), jnp.bfloat16),
+            ],
+            axis=1,
+        ),
+        position,
+    )
+    owned = owner_last(owned_parts, exchange(one_of(owned_parts, 1 - side, 0)), side)
+    mixture, late = together((mixture, d_query))
+    mixed = (residual + mixture.astype(jnp.float32)).astype(jnp.bfloat16)
+    expert_grad = jnp.stack(
+        [mine + part.astype(jnp.float32) for mine, part in zip(owned_experts, taken)]
+    )
+    return (
+        mixed,
+        tokens_grad,
+        owned[:, :wide],
+        owned[:, wide : wide + narrow],
+        owned[:, wide + narrow : wide + 2 * narrow],
+        first_owned[:, :D],
+        owned[:, wide + 2 * narrow],
+        first_owned[:, D + E],
+        first_owned[:, D : D + E],
         expert_grad,
     )
 
@@ -607,6 +1432,7 @@
         P(("dp", "ctx"), None),
         P(None, "dp", "ctx"),
     )
+    body = per_device if mesh.shape["ctx"] == HQ else general_device
     return jax.shard_map(
-        per_device, mesh=mesh, in_specs=in_specs, out_specs=out_specs, check_vma=False
-    )
+        body, mesh=mesh, in_specs=in_specs, out_specs=out_specs, check_vma=False
+    )

time: 3370 us -> 916 us (0.27)
  waiting for transfers between devices: 1380 us -> 282 us
  local copies, waits for them, and re-layouts: 656 us -> 48.2 us
  matrix products: 547 us -> 35.5 us
  Pallas kernels: 0 us -> 297 us
  blocking collectives: 245 us -> 0 us
  other arithmetic: 211 us -> 78.2 us
  between operations: 105 us -> 18.2 us
  starting transfers between devices: 185 us -> 151 us
    all_to_all x4 -> x9, waiting for transfers between devices: 1000 us -> 101 us  [the longest x7 71.6 us: to_heads(): lax.all_to_all(values, 'ctx', split_axis=0, concat_axis=0, tiled=True)]
    dot_general x142 -> x10, matrix products: 547 us -> 35.5 us  [the longest x3 15.2 us: tt(): lax.dot_general(a, b, (((0,), (1,)), ((), ())), preferred_element_type=jn...]
    pallas_call x0 -> x16, Pallas kernels: none -> 297 us  [the longest x5 88.9 us: expert_step(): pl.pallas_call(partial(expert_kernel, count), grid_spec=pltpu.PrefetchSca...]
    reduce_scatter x6 -> x1, waiting for transfers between devices: 218 us -> 0.01 us  [per_device(): mixture = lax.psum_scatter(out_rows, 'ctx', scatter_dimension=0, tiled=True)]
    ppermute x0 -> x59, waiting for transfers between devices: none -> 170 us  [the longest x53 122 us: move(): return lax.ppermute(values, 'ctx', pairs)]
    all_gather x3 -> x0, blocking collectives: 165 us -> none  [the longest x1 101 us: per_device(): lax.all_gather(log_total, 'ctx', axis=0, tiled=True)]
    another operation x120 -> x1, local copies, waits for them, and re-layouts: 158 us -> 0.09 us  [near_order(): return jnp.stack(steps).astype(jnp.int32)]
    all_gather x9 -> x1, waiting for transfers between devices: 154 us -> 11 us  [per_device(): lax.all_gather(jnp.concatenate([w_query, w_key, w_value, extras, w_output...]
  transfers between devices with their start and end apart: 19 -> 70, of which waited for: 10 -> 28; matrix products, arithmetic and copies ran while one was open for 39% -> 13% of each run, Pallas kernels for 0% -> 33%
where the time goes in v1:
time: 916 us; the launch traced here: 910 us
  Pallas kernels  297 us (32%)
  waiting for transfers between devices  282 us (31%)
  starting transfers between devices  151 us (16%)
  other arithmetic  78.2 us (9%)
  local copies, waits for them, and re-layouts  48.2 us (5%)
  matrix products  35.5 us (4%)
  between operations  18.2 us (2%)
    ppermute x53, waiting for transfers between devices, move(): return lax.ppermute(values, 'ctx', pairs)  122 us
    pallas_call x5, Pallas kernels, expert_step(): pl.pallas_call(partial(expert_kernel, count), grid_spec=pltpu.PrefetchSca...  88.9 us
    all_to_all x7, waiting for transfers between devices, to_heads(): lax.all_to_all(values, 'ctx', split_axis=0, concat_axis=0, tiled=True)  71.6 us
    pallas_call x1, Pallas kernels, attention_backward(): pl.pallas_call(attention_backward_kernel, out_shape=jax.ShapeDtypeStruct(...  60.9 us
    ppermute x53, starting transfers between devices, move(): return lax.ppermute(values, 'ctx', pairs)  59.7 us
    pallas_call x2, Pallas kernels, attention_forward(): pl.pallas_call(partial(attention_forward_kernel, seq), out_shape=(jax.Sha...  55 us
    ppermute x6, waiting for transfers between devices, exchange(): return lax.ppermute(values, 'dp', [(0, 1), (1, 0)])  47.6 us
    all_to_all x2, starting transfers between devices, owner_last(): lax.all_to_all(added(one_of(values, side, 0), taken), 'ctx', split_axis=0...  42.4 us
  transfers between devices with their start and end apart: 70, of which 28 were waited for; matrix products, arithmetic and copies ran while one was open for 13% of the time, Pallas kernels for 33%

profile of v1, /device:TPU:0, one launch (start us, length us, event | category | flops | bytes accessed | tf_op | source)
XLA Modules:
  0.0 910.0 jit_solution(14657315545780648236)
XLA Ops:
  27.7 10.8 %collective-permute-done.refs_1_ = bf16[512,1024]{1,0:T(8,128)(2,1)} collective-permute-done((bf16[512,1024]{1,0:T(8,128)(2,1)}, bf16[512,1024]{1,0:T(8,128)(2,1)}, u32[]{:S(2)}, u32[]{:S(2)}) %collective-permute-start) | collective-permute-done | bytes 1048608 | tf_op jit(solution)/shard_map/ppermute | solution.py:1047
  38.5 8.8 collective-permute-done.1
  58.4 30.5 %collective-permute-done.3.refs_1_ = bf16[512,1024]{1,0:T(8,128)(2,1)S(1)} collective-permute-done((bf16[512,1024]{1,0:T(8,128)(2,1)S(1)}, bf16[512,1024]{1,0:T(8,128)(2,1)S(1)}, u32[]{:S(2)}, u32[]{:S(2)}) %collective-permute-start.3) | collective-permute-done | bytes 1048608 | tf_op jit(solution)/shard_map/ppermute | solution.py:1047
  94.3 11.0 %all-gather.2.cloned.1.call-done = bf16[1024,3200]{1,0:T(8,128)(2,1)} async-done(((bf16[32,3200]{1,0:T(8,128)(2,1)}), bf16[1024,3200]{1,0:T(8,128)(2,1)}) %all-gather.2.cloned.1.call-update) | async-done | bytes 6553616 | tf_op jit(solution)/shard_map/all_gather | solution.py:1186
  151.1 8.4 grad_step.6
  159.6 22.6 %all-to-all-done.1.packed = bf16[16,192,512]{2,1,0:T(8,128)(2,1)} async-done(((bf16[16,192,512]{2,1,0:T(8,128)(2,1)}), bf16[16,192,512]{2,1,0:T(8,128)(2,1)}, u32[]{:S(2)}, u32[]{:S(2)}) %all-to-all-start.1) | async-done | bytes 3145760 | tf_op jit(solution)/shard_map/all_to_all | solution.py:1158
  182.2 27.3 %attention_forward.2 = (bf16[16,64,512]{2,1,0:T(8,128)(2,1)}, f32[64,4096]{1,0:T(8,128)}, f32[1,4096]{1,0:T(1,128)}) custom-call(s32[32]{0:T(128)} %get-tuple-element.131.table, bf16[16,192,512]{2,1,0:T(8,128)(2,1)} %all-to-all-done.1.packed), custom_call_target="tpu_custom_call" | custom-call | flops 31050000384 | bytes 3145728 | tf_op jit(solution)/shard_map/attention_forward/pallas_call | solution.py:753
  217.7 27.7 %attention_forward.3 = (bf16[16,64,512]{2,1,0:T(8,128)(2,1)}, f32[64,4096]{1,0:T(8,128)}, f32[1,4096]{1,0:T(1,128)}) custom-call(s32[32]{0:T(128)} %get-tuple-element.131.table, bf16[16,192,512]{2,1,0:T(8,128)(2,1)} %all-to-all-done.1.packed, bf16[16,64,512]{2,1,0:T(8,128)(2,1)} %get-tuple-element.149.refs_0_), custom_call_target="tpu_custom_call" | custom-call | flops 31050000384 | bytes 3145728 | tf_op jit(solution)/shard_map/attention_forward/pallas_call | solution.py:753
  245.4 10.6 %all-to-all-start.2 = ((bf16[16,64,512]{2,1,0:T(8,128)(2,1)}), bf16[16,64,512]{2,1,0:T(8,128)(2,1)S(1)}, u32[]{:S(2)}, u32[]{:S(2)}) async-start(bf16[16,64,512]{2,1,0:T(8,128)(2,1)} %get-tuple-element.155), calls=%async_computation.2 | async-start | bytes 2097152 | tf_op jit(solution)/shard_map/all_to_all | solution.py:1158
  256.0 8.4 grad_step.7
  264.9 8.5 grad_step.8
  286.2 6.6 all-to-all-start.3
  303.3 12.9 %expert_step.5 = (bf16[2,2560,1024]{2,1,0:T(8,128)(2,1)}, bf16[2,2560,512]{2,1,0:T(8,128)(2,1)}, bf16[2,2560,512]{2,1,0:T(8,128)(2,1)}, bf16[2,2560,512]{2,1,0:T...) custom-call(s32[2]{0:T(128)} %pad_add_fusion.1.order, ...), custom_call_target="tpu_custom_call" | custom-call | flops 11500000256 | bytes 6291456 | tf_op jit(solution)/shard_map/expert_step/pallas_call | solution.py:924
  333.0 21.0 %expert_step.6 = (bf16[2,2560,1024]{2,1,0:T(8,128)(2,1)}, bf16[2,2560,512]{2,1,0:T(8,128)(2,1)}, bf16[2,2560,512]{2,1,0:T(8,128)(2,1)}, bf16[2,2560,512]{2,1,0:T...) custom-call(s32[4]{0:T(128)} %pad_add_fusion.order, ...), custom_call_target="tpu_custom_call", output_to_operand_aliasing={{0}: (10, {}), {1}: (11, {}), {2}: (12, {}), {3}: (13, {})} | custom-call | flops 23000000512 | bytes 12582912 | tf_op jit(solution)/shard_map/expert_step/pallas_call | solution.py:924
  366.6 21.0 %expert_step.7 = (bf16[2,2560,1024]{2,1,0:T(8,128)(2,1)}, bf16[2,2560,512]{2,1,0:T(8,128)(2,1)}, bf16[2,2560,512]{2,1,0:T(8,128)(2,1)}, bf16[2,2560,512]{2,1,0:T...) custom-call(s32[4]{0:T(128)} %pad_add_fusion.4.order, ...), custom_call_target="tpu_custom_call", output_to_operand_aliasing={{0}: (10, {}), {1}: (11, {}), {2}: (12, {}), {3}: (13, {})} | custom-call | flops 23000000512 | bytes 12582912 | tf_op jit(solution)/shard_map/expert_step/pallas_call | solution.py:924
  398.4 20.9 %expert_step.8 = (bf16[2,2560,1024]{2,1,0:T(8,128)(2,1)}, bf16[2,2560,512]{2,1,0:T(8,128)(2,1)}, bf16[2,2560,512]{2,1,0:T(8,128)(2,1)}, bf16[2,2560,512]{2,1,0:T...) custom-call(s32[4]{0:T(128)} %pad_add_fusion.3.order, ...), custom_call_target="tpu_custom_call", output_to_operand_aliasing={{0}: (10, {}), {1}: (11, {}), {2}: (12, {}), {3}: (13, {})} | custom-call | flops 23000000512 | bytes 12582912 | tf_op jit(solution)/shard_map/expert_step/pallas_call | solution.py:924
  424.5 13.1 %expert_step.9 = (bf16[2,2560,1024]{2,1,0:T(8,128)(2,1)}, bf16[2,2560,512]{2,1,0:T(8,128)(2,1)}, bf16[2,2560,512]{2,1,0:T(8,128)(2,1)}, bf16[2,2560,512]{2,1,0:T...) custom-call(s32[2]{0:T(128)} %pad_add_fusion.2.order, ...), custom_call_target="tpu_custom_call", output_to_operand_aliasing={{0}: (8, {}), {1}: (9, {}), {2}: (10, {}), {3}: (11, {})} | custom-call | flops 11500000256 | bytes 6291456 | tf_op jit(solution)/shard_map/expert_step/pallas_call | solution.py:924
  452.2 18.5 %collective-permute-done.42 = bf16[512,1024]{1,0:T(8,128)(2,1)S(1)} collective-permute-done((bf16[512,1024]{1,0:T(8,128)(2,1)S(1)}, bf16[512,1024]{1,0:T(8,128)(2,1)S(1)}, u32[]{:S(2)}, u32[]{:S(2)}) %collective-permute-start.42) | collective-permute-done | bytes 1048608 | tf_op jit(solution)/shard_map/ppermute | solution.py:1047
  475.0 26.5 %output_pass.1 = bf16[8192,1024]{1,0:T(8,128)(2,1)} custom-call(s32[16]{0:T(128)} %copy-done.58, f32[16,512,2]{2,1,0:T(8,128)} %bitcast.143, bf16[2,2560,512]{2,1,0:T(8,128)(2,1)} %get-tuple-element.215.hidden, bf16[3,1024,1024]{2,1,0:T(8,128)(2,1)} %pad_maximum_fusion.refs_2_.refs_4_.refs_3_.refs_5_.weights), custom_call_target="tpu_custom_call" | custom-call | flops 29899999232 | bytes 25165824 | tf_op jit(solution)/shard_map/output_pass/pallas_call | solution.py:980
  506.6 9.2 %collective-permute-done.46 = bf16[512,1024]{1,0:T(8,128)(2,1)} collective-permute-done((bf16[512,1024]{1,0:T(8,128)(2,1)}, bf16[512,1024]{1,0:T(8,128)(2,1)}, u32[]{:S(2)}, u32[]{:S(2)}) %collective-permute-start.46) | collective-permute-done | bytes 1048608 | tf_op jit(solution)/shard_map/ppermute | solution.py:1047
  523.9 14.2 %weight_grad.2 = (bf16[512,1024]{1,0:T(8,128)(2,1)}, bf16[512,1024]{1,0:T(8,128)(2,1)}, bf16[512,1024]{1,0:T(8,128)(2,1)}) custom-call(s32[1]{0:T(128)} %bitcast.41.half, bf16[2,2560,1024]{2,1,0:T(8,128)(2,1)} %get-tuple-element.216.slot_rows, bf16[2,2560,1024]{2,1,0:T(8,128)(2,1)} %get-tuple-element.217.slot_grads, ...), custom_call_target="tpu_custom_call" | custom-call | flops 17250000896 | bytes 41943040 | tf_op jit(solution)/shard_map/weight_grad/pallas_call | solution.py:1012
  556.0 14.5 %weight_grad.3 = (f32[512,1024]{1,0:T(8,128)}, f32[512,1024]{1,0:T(8,128)}, f32[512,1024]{1,0:T(8,128)}) custom-call(s32[1]{0:T(128)} %bitcast.42.half, bf16[2,2560,1024]{2,1,0:T(8,128)(2,1)} %get-tuple-element.216.slot_rows, bf16[2,2560,1024]{2,1,0:T(8,128)(2,1)} %get-tuple-element.217.slot_grads, bf16[2,2560,512]{2,1,0:T(8,128)(2,1)} %get-tuple-element.218.d_gate_pre, ...), custom_call_target="tpu_custom_call" | custom-call | flops 17250000896 | bytes 41943040 | tf_op jit(solution)/shard_map/weight_grad/pallas_call | solution.py:1012
  571.5 13.0 %collective-permute-done.53 = bf16[512,1024]{1,0:T(8,128)(2,1)} collective-permute-done((bf16[512,1024]{1,0:T(8,128)(2,1)}, bf16[512,1024]{1,0:T(8,128)(2,1)}, u32[]{:S(2)}, u32[]{:S(2)}) %collective-permute-start.53) | collective-permute-done | bytes 1048608 | tf_op jit(solution)/shard_map/ppermute | solution.py:1154
  620.1 19.6 %collective-permute-done.55 = bf16[512,1024]{1,0:T(8,128)(2,1)} collective-permute-done((bf16[512,1024]{1,0:T(8,128)(2,1)}, bf16[512,1024]{1,0:T(8,128)(2,1)}, u32[]{:S(2)}, u32[]{:S(2)}) %collective-permute-start.55) | collective-permute-done | bytes 1048608 | tf_op jit(solution)/shard_map/ppermute | solution.py:1154
  639.8 60.9 %attention_backward.1 = bf16[16,192,512]{2,1,0:T(8,128)(2,1)} custom-call(s32[32]{0:T(128)} %get-tuple-element.131.table, bf16[16,192,512]{2,1,0:T(8,128)(2,1)} %all-to-all-done.1.packed, bf16[16,64,512]{2,1,0:T(8,128)(2,1)} %all-to-all-done.5.d_out, f32[64,4096]{1,0:T(8,128)} %get-tuple-element.238.out_rows_0, f32[64,4096]{1,0:T(8,128)} %get-tuple-element.239.out_rows_1, ...), custom_call_target="tpu_custom_call" | custom-call | flops 70149996544 | bytes 9437184 | tf_op jit(solution)/shard_map/attention_backward/pallas_call | solution.py:779
  707.4 15.0 %collective-permute-done.56 = bf16[8,32,1152]{2,1,0:T(8,128)(2,1)} collective-permute-done((bf16[8,32,1152]{2,1,0:T(8,128)(2,1)S(1)}, bf16[8,32,1152]{2,1,0:T(8,128)(2,1)}, u32[]{:S(2)}, u32[]{:S(2)}) %collective-permute-start.56) | collective-permute-done | bytes 589856 | tf_op jit(solution)/shard_map/ppermute | solution.py:1154
  722.4 49.0 %all-to-all-done.6 = bf16[16,192,512]{2,1,0:T(8,128)(2,1)} async-done(((bf16[16,192,512]{2,1,0:T(8,128)(2,1)}), bf16[16,192,512]{2,1,0:T(8,128)(2,1)}, u32[]{:S(2)}, u32[]{:S(2)}) %all-to-all-start.6) | async-done | bytes 3145760 | tf_op jit(solution)/shard_map/all_to_all | solution.py:1158
  788.8 7.7 concatenate.65
  809.5 31.1 %all-to-all-start.8 = ((bf16[8,32,1152]{2,1,0:T(8,128)(2,1)}), bf16[8,32,1152]{2,1,0:T(8,128)(2,1)S(1)}, u32[]{:S(2)}, u32[]{:S(2)}) async-start(bf16[8,32,1152]{2,1,0:T(8,128)(2,1)} %fusion.29), calls=%async_computation.9 | async-start | bytes 1179648 | tf_op jit(solution)/shard_map/all_to_all | solution.py:1142
  843.5 13.1 %all-to-all-done.8 = bf16[8,32,1152]{2,1,0:T(8,128)(2,1)S(1)} async-done(((bf16[8,32,1152]{2,1,0:T(8,128)(2,1)}), bf16[8,32,1152]{2,1,0:T(8,128)(2,1)S(1)}, u32[]{:S(2)}, u32[]{:S(2)}) %all-to-all-start.8) | async-done | bytes 589856 | tf_op jit(solution)/shard_map/all_to_all | solution.py:1142
  857.4 11.3 %all-to-all-start.7 = ((bf16[8,32,2176]{2,1,0:T(8,128)(2,1)}), bf16[8,32,2176]{2,1,0:T(8,128)(2,1)S(1)}, u32[]{:S(2)}, u32[]{:S(2)}) async-start(bf16[8,32,2176]{2,1,0:T(8,128)(2,1)} %fusion.8), calls=%async_computation.8 | async-start | bytes 2228224 | tf_op jit(solution)/shard_map/all_to_all | solution.py:1142
  879.3 16.2 %all-to-all-done.7 = bf16[8,32,2176]{2,1,0:T(8,128)(2,1)S(1)} async-done(((bf16[8,32,2176]{2,1,0:T(8,128)(2,1)}), bf16[8,32,2176]{2,1,0:T(8,128)(2,1)S(1)}, u32[]{:S(2)}, u32[]{:S(2)}) %all-to-all-start.7) | async-done | bytes 1114144 | tf_op jit(solution)/shard_map/all_to_all | solution.py:1142
  (376 shorter events, 301.7 us)
Async XLA Ops:
  7.2 98.1 %all-gather.2.cloned.1.call-start = ((), (), s32[]{:S(2)}) async-start(), calls=%async_computation.10 | async-start | bytes 6758400 | tf_op jit(solution)/shard_map/all_gather | solution.py:1186
  13.5 33.8 %collective-permute-start.1 = (bf16[512,1024]{1,0:T(8,128)(2,1)}, bf16[512,1024]{1,0:T(8,128)(2,1)S(1)}, u32[]{:S(2)}, u32[]{:S(2)}) collective-permute-start(bf16[512,1024]{1,0:T(8,128)(2,1)} %refs_0_.1), channel_id=1, source_target_pairs={{0,4},{1,5},{2,6},{3,7},{4,8},{5,9},{6,10},{7,11},{8,12},{9,13},{1... | collective-permute-start | bytes 3145736 | tf_op jit(solution)/shard_map/ppermute | solution.py:1047
  17.0 35.7 %collective-permute-start.2 = (bf16[512,1024]{1,0:T(8,128)(2,1)}, bf16[512,1024]{1,0:T(8,128)(2,1)S(1)}, u32[]{:S(2)}, u32[]{:S(2)}) collective-permute-start(bf16[512,1024]{1,0:T(8,128)(2,1)} %refs_0_.1), channel_id=1, source_target_pairs={{4,0},{5,1},{6,2},{7,3},{8,4},{9,5},{10,6},{11,7},{12,8},{13,9},{1... | collective-permute-start | bytes 3145736 | tf_op jit(solution)/shard_map/ppermute | solution.py:1047
  18.3 99.1 %collective-permute-start.6 = (bf16[3,512,1024]{2,1,0:T(8,128)(2,1)}, bf16[3,512,1024]{2,1,0:T(8,128)(2,1)}, u32[]{:S(2)}, u32[]{:S(2)}) collective-permute-start(bf16[3,512,1024]{2,1,0:T(8,128)(2,1)} %param.22), channel_id=1, source_target_pairs={{0,16},{16,0},{1,17},{17,1},{2,18},{18,2},{3,19},{19,3},{4,20},{20... | collective-permute-start | bytes 9437192 | tf_op jit(solution)/shard_map/ppermute | solution.py:1154
  21.6 95.9 %all-to-all-start = ((f32[16,2,512]{2,1,0:T(2,128)}), f32[16,2,512]{2,1,0:T(2,128)S(1)}, u32[]{:S(2)}, u32[]{:S(2)}) async-start(f32[16,2,512]{2,1,0:T(2,128)} %reshape.325), calls=%async_computation | async-start | bytes 131072 | tf_op jit(solution)/shard_map/all_to_all | solution.py:1158
  52.8 36.1 %collective-permute-start.4 = (bf16[512,1024]{1,0:T(8,128)(2,1)S(1)}, bf16[512,1024]{1,0:T(8,128)(2,1)}, u32[]{:S(2)}, u32[]{:S(2)}) collective-permute-start(bf16[512,1024]{1,0:T(8,128)(2,1)S(1)} %collective-permute-done.1), channel_id=1, source_target_pairs={{4,8},{5,9},{6,10},{7,11},{8,12},{9,13},{10,14},{11,15},{20,24},{2... | collective-permute-start | bytes 3145736 | tf_op jit(solution)/shard_map/ppermute | solution.py:1047
  54.4 39.9 %collective-permute-start.5 = (bf16[512,1024]{1,0:T(8,128)(2,1)S(1)}, bf16[512,1024]{1,0:T(8,128)(2,1)}, u32[]{:S(2)}, u32[]{:S(2)}) collective-permute-start(bf16[512,1024]{1,0:T(8,128)(2,1)S(1)} %collective-permute-done.2), channel_id=1, source_target_pairs={{4,0},{5,1},{6,2},{7,3},{8,4},{9,5},{10,6},{11,7},{20,16},{21,17},... | collective-permute-start | bytes 3145736 | tf_op jit(solution)/shard_map/ppermute | solution.py:1047
  55.8 33.1 %collective-permute-start.3 = (bf16[512,1024]{1,0:T(8,128)(2,1)S(1)}, bf16[512,1024]{1,0:T(8,128)(2,1)S(1)}, u32[]{:S(2)}, u32[]{:S(2)}) collective-permute-start(bf16[512,1024]{1,0:T(8,128)(2,1)S(1)} %broadcast_select_fusion.5.refs_0_), channel_id=1, source_target_pairs={{0,2},{1,3},{2,0},{3,1},{4,6},{5,7},{6,4},{7,5},{8,10},{9,11},{10,... | collective-permute-start | bytes 3145736 | tf_op jit(solution)/shard_map/ppermute | solution.py:1047
  118.1 64.1 %all-to-all-start.1 = ((bf16[16,192,512]{2,1,0:T(8,128)(2,1)}), bf16[16,192,512]{2,1,0:T(8,128)(2,1)}, u32[]{:S(2)}, u32[]{:S(2)}) async-start(bf16[16,192,512]{2,1,0:T(8,128)(2,1)} %pad_maximum_fusion.2), calls=%async_computation.1 | async-start | bytes 6291456 | tf_op jit(solution)/shard_map/all_to_all | solution.py:1158
  134.3 121.7 %collective-permute-start.17 = (bf16[512,1024]{1,0:T(8,128)(2,1)}, bf16[512,1024]{1,0:T(8,128)(2,1)}, u32[]{:S(2)}, u32[]{:S(2)}) collective-permute-start(bf16[512,1024]{1,0:T(8,128)(2,1)} %broadcast_select_fusion.4.refs_0_), channel_id=1, source_target_pairs={{0,1},{1,0},{2,3},{3,2},{4,5},{5,4},{6,7},{7,6},{8,9},{9,8},{10,11... | collective-permute-start | bytes 3145736 | tf_op jit(solution)/shard_map/ppermute | solution.py:1047
  134.6 74.9 %collective-permute-start.10 = (bf16[512,1024]{1,0:T(8,128)(2,1)}, bf16[512,1024]{1,0:T(8,128)(2,1)}, u32[]{:S(2)}, u32[]{:S(2)}) collective-permute-start(bf16[512,1024]{1,0:T(8,128)(2,1)} %broadcast_select_fusion.4.refs_0_), channel_id=1, source_target_pairs={{0,2},{1,3},{2,0},{3,1},{4,6},{5,7},{6,4},{7,5},{8,10},{9,11},{10,... | collective-permute-start | bytes 3145736 | tf_op jit(solution)/shard_map/ppermute | solution.py:1047
  142.0 67.5 %collective-permute-start.11 = (bf16[512,1024]{1,0:T(8,128)(2,1)}, bf16[512,1024]{1,0:T(8,128)(2,1)}, u32[]{:S(2)}, u32[]{:S(2)}) collective-permute-start(bf16[512,1024]{1,0:T(8,128)(2,1)} %collective-permute-done.4), channel_id=1, source_target_pairs={{8,12},{9,13},{10,14},{11,15},{24,28},{25,29},{26,30},{27,31}} | collective-permute-start | bytes 3145736 | tf_op jit(solution)/shard_map/ppermute | solution.py:1047
  149.5 60.1 %collective-permute-start.12 = (bf16[512,1024]{1,0:T(8,128)(2,1)}, bf16[512,1024]{1,0:T(8,128)(2,1)}, u32[]{:S(2)}, u32[]{:S(2)}) collective-permute-start(bf16[512,1024]{1,0:T(8,128)(2,1)} %collective-permute-done.5), channel_id=1, source_target_pairs={{4,0},{5,1},{6,2},{7,3},{20,16},{21,17},{22,18},{23,19}} | collective-permute-start | bytes 3145736 | tf_op jit(solution)/shard_map/ppermute | solution.py:1047
  151.0 105.0 %collective-permute-start.18 = (bf16[512,1024]{1,0:T(8,128)(2,1)}, bf16[512,1024]{1,0:T(8,128)(2,1)}, u32[]{:S(2)}, u32[]{:S(2)}) collective-permute-start(bf16[512,1024]{1,0:T(8,128)(2,1)} %copy-done.59), channel_id=1, source_target_pairs={{0,1},{1,0},{2,3},{3,2},{4,5},{5,4},{6,7},{7,6},{8,9},{9,8},{10,11... | collective-permute-start | bytes 3145736 | tf_op jit(solution)/shard_map/ppermute | solution.py:1047
  212.2 52.7 %collective-permute-start.15 = (bf16[512,1024]{1,0:T(8,128)(2,1)}, bf16[512,1024]{1,0:T(8,128)(2,1)}, u32[]{:S(2)}, u32[]{:S(2)}) collective-permute-start(bf16[512,1024]{1,0:T(8,128)(2,1)} %select_select_fusion.1.refs_0_), channel_id=1, source_target_pairs={{0,1},{1,0},{2,3},{3,2},{4,5},{5,4},{6,7},{7,6},{8,9},{9,8},{10,11... | collective-permute-start | bytes 3145736 | tf_op jit(solution)/shard_map/ppermute | solution.py:1047
  217.7 47.2 %collective-permute-start.16 = (bf16[512,1024]{1,0:T(8,128)(2,1)}, bf16[512,1024]{1,0:T(8,128)(2,1)}, u32[]{:S(2)}, u32[]{:S(2)}) collective-permute-start(bf16[512,1024]{1,0:T(8,128)(2,1)} %collective-permute-done.10.refs_1_), channel_id=1, source_target_pairs={{0,1},{1,0},{2,3},{3,2},{4,5},{5,4},{6,7},{7,6},{8,9},{9,8},{10,11... | collective-permute-start | bytes 3145736 | tf_op jit(solution)/shard_map/ppermute | solution.py:1047
  245.4 33.8 %all-to-all-start.2 = ((bf16[16,64,512]{2,1,0:T(8,128)(2,1)}), bf16[16,64,512]{2,1,0:T(8,128)(2,1)S(1)}, u32[]{:S(2)}, u32[]{:S(2)}) async-start(bf16[16,64,512]{2,1,0:T(8,128)(2,1)} %get-tuple-element.155), calls=%async_computation.2 | async-start | bytes 2097152 | tf_op jit(solution)/shard_map/all_to_all | solution.py:1158
  440.5 61.0 %collective-permute-start.43 = (bf16[2,512,1024]{2,1,0:T(8,128)(2,1)}, bf16[2,512,1024]{2,1,0:T(8,128)(2,1)}, u32[]{:S(2)}, u32[]{:S(2)}) collective-permute-start(bf16[2,512,1024]{2,1,0:T(8,128)(2,1)} %get-tuple-element.208), channel_id=1, source_target_pairs={{0,1},{1,0},{2,3},{3,2},{4,5},{5,4},{6,7},{7,6},{8,9},{9,8},{10,11... | collective-permute-start | bytes 6291464 | tf_op jit(solution)/shard_map/ppermute | solution.py:1047
  446.5 124.9 %collective-permute-start.30 = (bf16[512,1024]{1,0:T(8,128)(2,1)}, bf16[512,1024]{1,0:T(8,128)(2,1)}, u32[]{:S(2)}, u32[]{:S(2)}) collective-permute-start(bf16[512,1024]{1,0:T(8,128)(2,1)} %slice_bitcast_fusion.5), channel_id=1, source_target_pairs={{0,2},{1,3},{2,0},{3,1},{4,6},{5,7},{6,4},{7,5},{8,10},{9,11},{10,... | collective-permute-start | bytes 3145736 | tf_op jit(solution)/shard_map/ppermute | solution.py:1047
  451.5 64.3 %collective-permute-start.46 = (bf16[512,1024]{1,0:T(8,128)(2,1)}, bf16[512,1024]{1,0:T(8,128)(2,1)}, u32[]{:S(2)}, u32[]{:S(2)}) collective-permute-start(bf16[512,1024]{1,0:T(8,128)(2,1)} %slice_bitcast_fusion.1), channel_id=1, source_target_pairs={{0,2},{1,3},{2,0},{3,1},{4,6},{5,7},{6,4},{7,5},{8,10},{9,11},{10,... | collective-permute-start | bytes 3145736 | tf_op jit(solution)/shard_map/ppermute | solution.py:1047
  471.1 44.6 %collective-permute-start.44 = (bf16[512,1024]{1,0:T(8,128)(2,1)S(1)}, bf16[512,1024]{1,0:T(8,128)(2,1)}, u32[]{:S(2)}, u32[]{:S(2)}) collective-permute-start(bf16[512,1024]{1,0:T(8,128)(2,1)S(1)} %fusion.19), channel_id=1, source_target_pairs={{0,4},{1,5},{2,6},{3,7},{16,20},{17,21},{18,22},{19,23}} | collective-permute-start | bytes 3145736 | tf_op jit(solution)/shard_map/ppermute | solution.py:1047
  473.4 42.4 %collective-permute-start.45 = (bf16[512,1024]{1,0:T(8,128)(2,1)S(1)}, bf16[512,1024]{1,0:T(8,128)(2,1)}, u32[]{:S(2)}, u32[]{:S(2)}) collective-permute-start(bf16[512,1024]{1,0:T(8,128)(2,1)S(1)} %fusion.19), channel_id=1, source_target_pairs={{12,8},{13,9},{14,10},{15,11},{28,24},{29,25},{30,26},{31,27}} | collective-permute-start | bytes 3145736 | tf_op jit(solution)/shard_map/ppermute | solution.py:1047
  505.8 38.0 %collective-permute-start.49 = (bf16[512,1024]{1,0:T(8,128)(2,1)}, bf16[512,1024]{1,0:T(8,128)(2,1)}, u32[]{:S(2)}, u32[]{:S(2)}) collective-permute-start(bf16[512,1024]{1,0:T(8,128)(2,1)} %slice_bitcast_fusion), channel_id=1, source_target_pairs={{0,2},{1,3},{2,0},{3,1},{4,6},{5,7},{6,4},{7,5},{8,10},{9,11},{10,... | collective-permute-start | bytes 3145736 | tf_op jit(solution)/shard_map/ppermute | solution.py:1047
  538.1 33.4 %collective-permute-start.52 = (bf16[512,1024]{1,0:T(8,128)(2,1)}, bf16[512,1024]{1,0:T(8,128)(2,1)}, u32[]{:S(2)}, u32[]{:S(2)}) collective-permute-start(bf16[512,1024]{1,0:T(8,128)(2,1)} %get-tuple-element.220), channel_id=1, source_target_pairs={{0,16},{16,0},{1,17},{17,1},{2,18},{18,2},{3,19},{19,3},{4,20},{20... | collective-permute-start | bytes 3145736 | tf_op jit(solution)/shard_map/ppermute | solution.py:1154
  543.8 40.6 %collective-permute-start.53 = (bf16[512,1024]{1,0:T(8,128)(2,1)}, bf16[512,1024]{1,0:T(8,128)(2,1)}, u32[]{:S(2)}, u32[]{:S(2)}) collective-permute-start(bf16[512,1024]{1,0:T(8,128)(2,1)} %get-tuple-element.221), channel_id=1, source_target_pairs={{0,16},{16,0},{1,17},{17,1},{2,18},{18,2},{3,19},{19,3},{4,20},{20... | collective-permute-start | bytes 3145736 | tf_op jit(solution)/shard_map/ppermute | solution.py:1154
  549.8 34.6 %collective-permute-start.50 = (bf16[512,1024]{1,0:T(8,128)(2,1)}, bf16[512,1024]{1,0:T(8,128)(2,1)}, u32[]{:S(2)}, u32[]{:S(2)}) collective-permute-start(bf16[512,1024]{1,0:T(8,128)(2,1)} %get-tuple-element.263), channel_id=1, source_target_pairs={{0,4},{1,5},{2,6},{3,7},{4,8},{5,9},{6,10},{7,11},{8,12},{9,13},{1... | collective-permute-start | bytes 3145736 | tf_op jit(solution)/shard_map/ppermute | solution.py:1047
  597.5 42.3 %all-to-all-start.5 = ((bf16[16,64,512]{2,1,0:T(8,128)(2,1)}), bf16[16,64,512]{2,1,0:T(8,128)(2,1)}, u32[]{:S(2)}, u32[]{:S(2)}) async-start(bf16[16,64,512]{2,1,0:T(8,128)(2,1)} %bitcast.154), calls=%async_computation.6 | async-start | bytes 2097152 | tf_op jit(solution)/shard_map/all_to_all | solution.py:1158
  601.8 295.8 %reduce-scatter.2.cloned.1.call-start = ((), (), s32[]{:S(2)}) async-start(), calls=%async_computation.11 | async-start | bytes 17825792 | tf_op jit(solution)/shard_map/reduce_scatter | solution.py:1332
  700.6 70.8 %all-to-all-start.6 = ((bf16[16,192,512]{2,1,0:T(8,128)(2,1)}), bf16[16,192,512]{2,1,0:T(8,128)(2,1)}, u32[]{:S(2)}, u32[]{:S(2)}) async-start(bf16[16,192,512]{2,1,0:T(8,128)(2,1)} %attention_backward.1), calls=%async_computation.7 | async-start | bytes 6291456 | tf_op jit(solution)/shard_map/all_to_all | solution.py:1158
  805.9 34.7 %collective-permute-start.58 = (bf16[8,32,2176]{2,1,0:T(8,128)(2,1)}, bf16[8,32,2176]{2,1,0:T(8,128)(2,1)}, u32[]{:S(2)}, u32[]{:S(2)}) collective-permute-start(bf16[8,32,2176]{2,1,0:T(8,128)(2,1)} %dynamic-slice_bitcast_fusion.2), channel_id=1, source_target_pairs={{0,16},{16,0},{1,17},{17,1},{2,18},{18,2},{3,19},{19,3},{4,20},{20... | collective-permute-start | bytes 3342344 | tf_op jit(solution)/shard_map/ppermute | solution.py:1154
  809.5 47.0 %all-to-all-start.8 = ((bf16[8,32,1152]{2,1,0:T(8,128)(2,1)}), bf16[8,32,1152]{2,1,0:T(8,128)(2,1)S(1)}, u32[]{:S(2)}, u32[]{:S(2)}) async-start(bf16[8,32,1152]{2,1,0:T(8,128)(2,1)} %fusion.29), calls=%async_computation.9 | async-start | bytes 1179648 | tf_op jit(solution)/shard_map/all_to_all | solution.py:1142
  857.4 38.1 %all-to-all-start.7 = ((bf16[8,32,2176]{2,1,0:T(8,128)(2,1)}), bf16[8,32,2176]{2,1,0:T(8,128)(2,1)S(1)}, u32[]{:S(2)}, u32[]{:S(2)}) async-start(bf16[8,32,2176]{2,1,0:T(8,128)(2,1)} %fusion.8), calls=%async_computation.8 | async-start | bytes 2228224 | tf_op jit(solution)/shard_map/all_to_all | solution.py:1142
  (104 other events, 1788.6 us)
Sparse Core Ops, SparseCore 0:
  11.5 93.7 all-gather.1
  606.8 211.1 reduce-scatter.1

commit v2 on v1

--- a/solution.py
+++ b/solution.py
@@ -591,9 +591,7 @@
     )
 
 
-TILE = 512
 VMEM_BYTES = 60 * 1024 * 1024
-CHANNELS = 3 * HD
 
 
 def nn(a, b):
@@ -612,130 +610,108 @@
     return lax.dot_general(a, b, (((0,), (1,)), ((), ())), preferred_element_type=jnp.float32)
 
 
-def attention_forward_kernel(seq, table, packed, *refs):
-    out, out_rows, log_sum, q_seq, k_seq, v_seq = refs[-6:]
-    if seq > 0:
-        out[...] = refs[0][...]
-    seq_rows = BLOCKS * BLK
-    for g in range(BLOCKS):
-        slot = table[seq * BLOCKS + g]
-        lanes = pl.ds(pl.multiple_of((slot % 2) * BLK, BLK), BLK)
-        here = slice(g * BLK, (g + 1) * BLK)
-        source = packed.at[slot // 2]
-        q_seq[:, here] = source[0:HD, lanes] * jnp.bfloat16(HD**-0.5)
-        k_seq[here, :] = source[HD : 2 * HD, lanes].astype(jnp.float32).T.astype(jnp.bfloat16)
-        v_seq[:, here] = source[2 * HD : 3 * HD, lanes]
-
-    def update(q, state, start, size):
-        top, total, acc = state
-        rows = pl.ds(start, size)
-        scores = nn(k_seq[rows, :], q)
-        new_top = jnp.maximum(top, jnp.max(scores, axis=0, keepdims=True))
-        factor = jnp.exp(top - new_top)
-        weights = jnp.exp(scores - new_top)
-        total = total * factor + jnp.sum(weights, axis=0, keepdims=True)
-        acc = acc * factor + nn(v_seq[:, rows], weights.astype(jnp.bfloat16))
-        return new_top, total, acc
-
-    def one_tile(n, carry):
-        mine = pl.multiple_of(n * TILE, TILE)
-        q = q_seq[:, pl.ds(mine, TILE)]
-        state = (
-            jnp.full((1, TILE), floor_value, jnp.float32),
-            jnp.zeros((1, TILE), jnp.float32),
-            jnp.zeros((HD, TILE), jnp.float32),
-        )
-        state = lax.fori_loop(
-            0,
-            n,
-            lambda k, c: update(q, c, pl.multiple_of(k * TILE, TILE), TILE),
-            state,
-        )
-        state = update(q, state, mine, BLK)
-        late = update(q[:, BLK:], tuple(s[:, BLK:] for s in state), mine + BLK, BLK)
-        top, total, acc = (
-            jnp.concatenate([s[:, :BLK], t], axis=1) for s, t in zip(state, late)
-        )
-        final = acc / total
-        out_rows[:, pl.ds(mine, TILE)] = final
-        log_sum[:, pl.ds(mine, TILE)] = top + jnp.log(total)
-        return carry
-
-    lax.fori_loop(0, seq_rows // TILE, one_tile, 0)
-    for g in range(BLOCKS):
-        slot = table[seq * BLOCKS + g]
-        lanes = pl.ds(pl.multiple_of((slot % 2) * BLK, BLK), BLK)
-        out[slot // 2, :, lanes] = out_rows[:, g * BLK : (g + 1) * BLK].astype(jnp.bfloat16)
+def lanes_of(slot):
+    return pl.ds(pl.multiple_of((slot % 2) * BLK, BLK), BLK)
+
+
+def by_core(table, mine, other, work_on):
+    core = table[table.shape[0] - 1]
+
+    @pl.when(core == 0)
+    def _():
+        work_on(mine, other)
+
+    @pl.when(core == 1)
+    def _():
+        work_on(other, mine)
+
+
+def attention_forward_kernel(
+    table, mine, other, out, out_rows, log_sum, q_seq, k_seq, v_seq
+):
+    for seq in range(2):
+
+        def load(key_source, value_source):
+            for g in range(BLOCKS):
+                slot = table[seq * BLOCKS + g]
+                lanes = lanes_of(slot)
+                here = slice(g * BLK, (g + 1) * BLK)
+                q_seq[:, here] = mine[slot // 2, 0:HD, lanes] * jnp.bfloat16(HD**-0.5)
+                keys = key_source[slot // 2, HD : 2 * HD, lanes]
+                k_seq[here, :] = keys.astype(jnp.float32).T.astype(jnp.bfloat16)
+                v_seq[:, here] = value_source[slot // 2, HD : 2 * HD, lanes]
+
+        by_core(table, mine, other, load)
+        span = BLOCKS * BLK
+        top = jnp.full((1, span), floor_value, jnp.float32)
+        total = jnp.zeros((1, span), jnp.float32)
+        acc = jnp.zeros((HD, span), jnp.float32)
+        for g in range(BLOCKS):
+            here = slice(g * BLK, (g + 1) * BLK)
+            scores = nn(k_seq[here, :], q_seq[:, g * BLK :])
+            new_top = jnp.maximum(top, jnp.max(scores, axis=0, keepdims=True))
+            factor = jnp.exp(top - new_top)
+            weights = jnp.exp(scores - new_top)
+            total = total * factor + jnp.sum(weights, axis=0, keepdims=True)
+            acc = acc * factor + nn(v_seq[:, here], weights.astype(jnp.bfloat16))
+            final = acc[:, :BLK] / total[:, :BLK]
+            place_of = slice(seq * span + g * BLK, seq * span + (g + 1) * BLK)
+            out_rows[:, place_of] = final
+            log_sum[:, place_of] = new_top[:, :BLK] + jnp.log(total[:, :BLK])
+            slot = table[seq * BLOCKS + g]
+            out[slot // 2, :, lanes_of(slot)] = final.astype(jnp.bfloat16)
+            top, total, acc = new_top[:, BLK:], total[:, BLK:], acc[:, BLK:]
 
 
 def attention_backward_kernel(
-    table, packed, d_out, out_rows_0, out_rows_1, log_sum, grads, q_seq, k_cols, v_cols, k_seq, v_seq, d_seq,
-    delta, dq, dk, dv
+    table, mine, other, d_out, out_rows, log_sum, q_grads, kept, given, q_seq, k_cols, k_seq,
+    v_seq, d_seq, delta, dq, dk, dv
 ):
-    block_count = 2 * packed.shape[0]
-    seq_rows = BLOCKS * BLK
-    for g in range(block_count):
-        slot = table[g]
-        lanes = pl.ds(pl.multiple_of((slot % 2) * BLK, BLK), BLK)
-        here = slice(g * BLK, (g + 1) * BLK)
-        source = packed.at[slot // 2]
-        q_seq[:, here] = source[0:HD, lanes] * jnp.bfloat16(HD**-0.5)
-        k_block = source[HD : 2 * HD, lanes]
-        v_block = source[2 * HD : 3 * HD, lanes]
-        k_cols[:, here] = k_block
-        k_seq[here, :] = k_block.astype(jnp.float32).T.astype(jnp.bfloat16)
-        v_seq[here, :] = v_block.astype(jnp.float32).T.astype(jnp.bfloat16)
-        d_block = d_out[slot // 2, :, lanes]
-        d_seq[:, here] = d_block
-        delta[:, here] = jnp.sum(
-            d_block.astype(jnp.float32)
-            * (out_rows_0, out_rows_1)[g // BLOCKS][
-                :, g % BLOCKS * BLK : (g % BLOCKS + 1) * BLK
-            ],
-            axis=0,
-            keepdims=True,
-        )
-    dq[...] = jnp.zeros_like(dq)
-
-    def pair(k_start, k_size, q_start, q_size, first):
-        keys = pl.ds(k_start, k_size)
-        cols = pl.ds(q_start, q_size)
-        q = q_seq[:, cols]
-        d = d_seq[:, cols]
-        probs = jnp.exp(nn(k_seq[keys, :], q) - log_sum[:, cols])
-        d_scores = (probs * (nn(v_seq[keys, :], d) - delta[:, cols])).astype(jnp.bfloat16)
-        new_v = nt(d, probs.astype(jnp.bfloat16))
-        new_k = nt(q, d_scores)
-        if first:
-            dv[:, keys] = new_v
-            dk[:, keys] = new_k
-        else:
-            dv[:, keys] += new_v
-            dk[:, keys] += new_k
-        dq[:, cols] += nn(k_cols[:, keys], d_scores)
-
-    def one_tile(n, carry):
-        per_seq = seq_rows // TILE
-        mine = pl.multiple_of(n * TILE, TILE)
-        last = (n // per_seq + 1) * per_seq
-        pair(mine, BLK, mine, TILE, True)
-        pair(mine + BLK, BLK, mine + BLK, BLK, True)
-
-        def step(t, c):
-            pair(mine, TILE, pl.multiple_of(t * TILE, TILE), TILE, False)
-            return c
-
-        lax.fori_loop(n + 1, last, step, 0)
-        return carry
-
-    lax.fori_loop(0, 2 * seq_rows // TILE, one_tile, 0)
-    for g in range(block_count):
-        slot = table[g]
-        lanes = pl.ds(pl.multiple_of((slot % 2) * BLK, BLK), BLK)
-        here = slice(g * BLK, (g + 1) * BLK)
-        grads[slot // 2, 0:HD, lanes] = (dq[:, here] * HD**-0.5).astype(jnp.bfloat16)
-        grads[slot // 2, HD : 2 * HD, lanes] = dk[:, here].astype(jnp.bfloat16)
-        grads[slot // 2, 2 * HD : 3 * HD, lanes] = dv[:, here].astype(jnp.bfloat16)
+    span = BLOCKS * BLK
+    for seq in range(2):
+
+        def load(key_source, value_source):
+            for g in range(BLOCKS):
+                slot = table[seq * BLOCKS + g]
+                lanes = lanes_of(slot)
+                here = slice(g * BLK, (g + 1) * BLK)
+                q_seq[:, here] = mine[slot // 2, 0:HD, lanes] * jnp.bfloat16(HD**-0.5)
+                keys = key_source[slot // 2, HD : 2 * HD, lanes]
+                k_cols[:, here] = keys
+                k_seq[here, :] = keys.astype(jnp.float32).T.astype(jnp.bfloat16)
+                values = value_source[slot // 2, HD : 2 * HD, lanes]
+                v_seq[here, :] = values.astype(jnp.float32).T.astype(jnp.bfloat16)
+                d_block = d_out[slot // 2, :, lanes]
+                d_seq[:, here] = d_block
+                out_block = out_rows[:, seq * span + g * BLK : seq * span + (g + 1) * BLK]
+                delta[:, here] = jnp.sum(
+                    d_block.astype(jnp.float32) * out_block, axis=0, keepdims=True
+                )
+
+        by_core(table, mine, other, load)
+        dq[...] = jnp.zeros_like(dq)
+        for g in range(BLOCKS):
+            keys = slice(g * BLK, (g + 1) * BLK)
+            later = slice(g * BLK, span)
+            q = q_seq[:, later]
+            d = d_seq[:, later]
+            sums = log_sum[:, seq * span + g * BLK : (seq + 1) * span]
+            probs = jnp.exp(nn(k_seq[keys, :], q) - sums)
+            d_scores = (probs * (nn(v_seq[keys, :], d) - delta[:, later])).astype(jnp.bfloat16)
+            dv[:, keys] = nt(d, probs.astype(jnp.bfloat16))
+            dk[:, keys] = nt(q, d_scores)
+            dq[:, later] += nn(k_cols[:, keys], d_scores)
+
+        def store(key_target, value_target):
+            for g in range(BLOCKS):
+                slot = table[seq * BLOCKS + g]
+                lanes = lanes_of(slot)
+                here = slice(g * BLK, (g + 1) * BLK)
+                q_grads[slot // 2, :, lanes] = (dq[:, here] * HD**-0.5).astype(jnp.bfloat16)
+                key_target[slot // 2, :, lanes] = dk[:, here].astype(jnp.bfloat16)
+                value_target[slot // 2, :, lanes] = dv[:, here].astype(jnp.bfloat16)
+
+        by_core(table, kept, given, store)
 
 
 def work(microseconds):
@@ -746,18 +722,18 @@
     return pltpu.CompilerParams(vmem_limit_bytes=VMEM_BYTES)
 
 
-def attention_forward(seq, table, packed, *kept):
-    count, _, row_count = packed.shape
+def attention_forward(table, mine, other):
+    count, _, row_count = mine.shape
     total = BLOCKS * BLK
     whole = pl.BlockSpec(memory_space=pltpu.VMEM)
     return pl.pallas_call(
-        partial(attention_forward_kernel, seq),
+        attention_forward_kernel,
         out_shape=(
             jax.ShapeDtypeStruct((count, HD, row_count), jnp.bfloat16),
-            jax.ShapeDtypeStruct((HD, total), jnp.float32),
-            jax.ShapeDtypeStruct((1, total), jnp.float32),
+            jax.ShapeDtypeStruct((HD, 2 * total), jnp.float32),
+            jax.ShapeDtypeStruct((1, 2 * total), jnp.float32),
         ),
-        in_specs=[pl.BlockSpec(memory_space=pltpu.SMEM), whole] + [whole] * len(kept),
+        in_specs=[pl.BlockSpec(memory_space=pltpu.SMEM), whole, whole],
         out_specs=(whole,) * 3,
         scratch_shapes=[
             pltpu.VMEM((HD, total), jnp.bfloat16),
@@ -766,24 +742,22 @@
         ],
         compiler_params=params(),
         cost_estimate=pl.CostEstimate(
-            flops=work(27), bytes_accessed=packed.size * 2, transcendentals=total * total // 2
+            flops=work(36), bytes_accessed=mine.size * 4, transcendentals=total * total // 2
         ),
         name="attention_forward",
-    )(table, packed, *kept)
-
-
-def attention_backward(table, packed, d_out, out_rows_0, out_rows_1, log_sum):
-    count, _, row_count = packed.shape
-    total = count * row_count
-    pairs = total * BLOCKS * BLK // 2
+    )(table, mine, other)
+
+
+def attention_backward(table, mine, other, d_out, out_rows, log_sum):
+    total = BLOCKS * BLK
+    whole = pl.BlockSpec(memory_space=pltpu.VMEM)
+    shape = jax.ShapeDtypeStruct(d_out.shape, jnp.bfloat16)
     return pl.pallas_call(
         attention_backward_kernel,
-        out_shape=jax.ShapeDtypeStruct(packed.shape, jnp.bfloat16),
-        in_specs=[pl.BlockSpec(memory_space=pltpu.SMEM)]
-        + [pl.BlockSpec(memory_space=pltpu.VMEM)] * 5,
-        out_specs=pl.BlockSpec(memory_space=pltpu.VMEM),
+        out_shape=(shape,) * 3,
+        in_specs=[pl.BlockSpec(memory_space=pltpu.SMEM)] + [whole] * 5,
+        out_specs=(whole,) * 3,
         scratch_shapes=[
-            pltpu.VMEM((HD, total), jnp.bfloat16),
             pltpu.VMEM((HD, total), jnp.bfloat16),
             pltpu.VMEM((HD, total), jnp.bfloat16),
             pltpu.VMEM((total, HD), jnp.bfloat16),
@@ -796,10 +770,10 @@
         ],
         compiler_params=params(),
         cost_estimate=pl.CostEstimate(
-            flops=work(61), bytes_accessed=packed.size * 6, transcendentals=pairs
+            flops=work(58), bytes_accessed=mine.size * 6, transcendentals=total * total // 2
         ),
         name="attention_backward",
-    )(table, packed, d_out, out_rows_0, out_rows_1, log_sum)
+    )(table, mine, other, d_out, out_rows, log_sum)
 
 
 def slot_match(places, rows):
@@ -812,44 +786,69 @@
     return jnp.where(numbers == places, 1.0, 0.0).astype(jnp.bfloat16)
 
 
+def both_match(places):
+    return jnp.concatenate(
+        [
+            jnp.where(slot_match(places[e : e + 1, :], CAP), 1.0, 0.0)
+            for e in range(places.shape[0])
+        ],
+        axis=0,
+    )
+
+
+def spread_match(places):
+    columns = places.T
+    count = places.shape[0] * CAP
+    numbers = lax.broadcasted_iota(jnp.int32, (columns.shape[0], count), 1)
+    found = numbers < 0
+    for e in range(places.shape[0]):
+        column = columns[:, e : e + 1]
+        found = found | (numbers.astype(jnp.float32) == jnp.where(column < 0, -1.0, column + e * CAP))
+    return jnp.where(found, 1.0, 0.0).astype(jnp.bfloat16)
+
+
+def pick_rows(order, places, sources, picked):
+    g = pl.program_id(0)
+    for k in range(len(sources) // 2):
+
+        @pl.when(g == k)
+        def _(k=k):
+            for i in range(2):
+                pick = both_match(places[order[2 * k + i]]).astype(jnp.bfloat16)
+                rows = nn(pick, sources[2 * k + i][...]).astype(jnp.bfloat16)
+                for e in range(places.shape[1]):
+                    picked[e, i * CAP : (i + 1) * CAP, :] = rows[e * CAP : (e + 1) * CAP]
+
+
 def grad_kernel(count, order, places, *refs):
     sources, weights = refs[:count], refs[count]
-    slot_rows, d_hidden, rows = refs[-3:]
-    g = pl.program_id(0)
-    for k, source in enumerate(sources):
-
-        @pl.when(g == k)
-        def _(source=source):
-            rows[...] = source[...]
-
+    slot_rows, d_hidden = refs[-2:]
+    pick_rows(order, places, sources, slot_rows)
     for e in range(places.shape[1]):
-        pick = jnp.where(slot_match(places[0, e : e + 1, :], CAP), 1.0, 0.0).astype(jnp.bfloat16)
-        picked = nn(pick, rows[...]).astype(jnp.bfloat16)
-        slot_rows[e] = picked
-        d_hidden[e] = nn(picked, weights[0, :, e * F : (e + 1) * F]).astype(jnp.bfloat16)
+        d_hidden[e] = nn(slot_rows[e], weights[0, :, e * F : (e + 1) * F]).astype(jnp.bfloat16)
 
 
 def grad_step(first, order, places, blocks, weights, kept):
     devices, local, row_count = places.shape
     count = len(blocks)
     kept = () if kept is None else tuple(kept)
+    whole = pl.BlockSpec((devices, local, row_count), lambda g, order: (0, 0, 0))
     block = pl.BlockSpec((row_count, D), lambda g, order: (0, 0))
     return pl.pallas_call(
         partial(grad_kernel, count),
         grid_spec=pltpu.PrefetchScalarGridSpec(
             num_scalar_prefetch=1,
-            grid=(count,),
+            grid=(count // 2,),
             in_specs=[
-                pl.BlockSpec((1, local, row_count), lambda g, order: (order[g], 0, 0)),
+                whole,
                 *([block] * count),
                 pl.BlockSpec((1, D, local * F), lambda g, order: (2, 0, 0)),
             ]
             + [pl.BlockSpec(memory_space=pl.ANY)] * len(kept),
             out_specs=(
-                pl.BlockSpec((local, CAP, D), lambda g, order: (0, first + g, 0)),
-                pl.BlockSpec((local, CAP, F), lambda g, order: (0, first + g, 0)),
+                pl.BlockSpec((local, 2 * CAP, D), lambda g, order: (0, first // 2 + g, 0)),
+                pl.BlockSpec((local, 2 * CAP, F), lambda g, order: (0, first // 2 + g, 0)),
             ),
-            scratch_shapes=[pltpu.VMEM((row_count, D), jnp.bfloat16)],
         ),
         out_shape=(
             jax.ShapeDtypeStruct((local, devices * CAP, D), jnp.bfloat16),
@@ -864,72 +863,89 @@
     )(order, places, *blocks, weights, *kept)
 
 
-def expert_kernel(count, order, places, columns, gates, *refs):
+def expert_kernel(count, order, places, gates, *refs):
     sources, (d_hidden, weights) = refs[:count], refs[count : count + 2]
-    slot_rows, hidden, d_gate_pre, d_up, d_gate, near, far, rows = refs[-8:]
+    slot_rows, hidden, d_gate_pre, d_up, d_gate, near, far, back = refs[-8:]
     g = pl.program_id(0)
-    for k, source in enumerate(sources):
-
-        @pl.when(g == k)
-        def _(source=source):
-            rows[...] = source[...]
-
-    total = None
-    for e in range(places.shape[1]):
-        here = slice(e * F, (e + 1) * F)
-        match = slot_match(places[0, e : e + 1, :], CAP)
-        pick = jnp.where(match, 1.0, 0.0)
-        picked = nn(pick.astype(jnp.bfloat16), rows[...]).astype(jnp.bfloat16)
-        slot_rows[e] = picked
-        gate_pre = nn(picked, weights[0, :, here])
-        up_pre = nn(picked, weights[1, :, here])
-        gate = jnp.sum(jnp.where(match, gates[0, e : e + 1, :], 0.0), axis=1, keepdims=True)
+    local = places.shape[1]
+    pick_rows(order, places, sources, slot_rows)
+    here = [slice(e * F, (e + 1) * F) for e in range(local)]
+    numbers = [order[2 * g], order[2 * g + 1]]
+    picks = [both_match(places[j]) for j in numbers]
+    slot_gates = []
+    for e in range(local):
+        gate_pre = nn(slot_rows[e], weights[0, :, here[e]])
+        up_pre = nn(slot_rows[e], weights[1, :, here[e]])
+        gate = jnp.concatenate(
+            [
+                jnp.sum(
+                    picks[i][e * CAP : (e + 1) * CAP] * gates[numbers[i]][e : e + 1, :],
+                    axis=1,
+                    keepdims=True,
+                )
+                for i in range(2)
+            ],
+            axis=0,
+        )
         raw = d_hidden[e].astype(jnp.float32)
         sig = 1.0 / (1.0 + jnp.exp(-gate_pre))
         silu = gate_pre * sig
         value = silu * up_pre
         hidden[e] = (gate * value).astype(jnp.bfloat16)
         scaled = raw * gate
-        up_grad = (scaled * silu).astype(jnp.bfloat16)
-        pre_grad = (scaled * up_pre * sig * (1.0 + gate_pre * (1.0 - sig))).astype(jnp.bfloat16)
-        d_up[e] = up_grad
-        d_gate_pre[e] = pre_grad
-        slot_gate = jnp.sum(raw * value, axis=1, keepdims=True)
-        d_gate[0, e : e + 1, :] = jnp.sum(pick * slot_gate, axis=0, keepdims=True)
-        back = (nt(pre_grad, weights[0, :, here]) + nt(up_grad, weights[1, :, here])).astype(
+        d_up[e] = (scaled * silu).astype(jnp.bfloat16)
+        d_gate_pre[e] = (scaled * up_pre * sig * (1.0 + gate_pre * (1.0 - sig))).astype(
             jnp.bfloat16
         )
-        spread = nn(column_match(columns[0, :, e : e + 1], CAP), back)
-        total = spread if total is None else total + spread
-    result = total.astype(jnp.bfloat16)
-
-    @pl.when(g < count // 2)
-    def _():
-        near[0] = result
-
-    @pl.when(g >= count // 2)
-    def _():
-        far[0] = result
-
-
-def expert_step(first, order, places, columns, gates, blocks, d_hidden, weights, kept):
+        slot_gates.append(jnp.sum(raw * value, axis=1, keepdims=True))
+    for e in range(local):
+        back[e] = (
+            nt(d_gate_pre[e], weights[0, :, here[e]]) + nt(d_up[e], weights[1, :, here[e]])
+        ).astype(jnp.bfloat16)
+    results = []
+    for i in range(2):
+        part = slice(i * CAP, (i + 1) * CAP)
+        for e in range(local):
+            d_gate[i, e : e + 1, :] = jnp.sum(
+                picks[i][e * CAP : (e + 1) * CAP] * slot_gates[e][part], axis=0, keepdims=True
+            )
+        rows = jnp.concatenate([back[e, part] for e in range(local)], axis=0)
+        results.append(nn(spread_match(places[numbers[i]]), rows).astype(jnp.bfloat16))
+    if count == 2:
+        near[0] = results[0]
+        far[0] = results[1]
+    else:
+
+        @pl.when(g == 0)
+        def _():
+            near[0] = results[0]
+            near[1] = results[1]
+
+        @pl.when(g == 1)
+        def _():
+            far[0] = results[0]
+            far[1] = results[1]
+
+
+def expert_step(first, order, places, gates, blocks, d_hidden, weights, kept):
     devices, local, row_count = places.shape
     count = len(blocks)
-    wide_slots = pl.BlockSpec((local, CAP, D), lambda g, order: (0, first + g, 0))
-    slots = pl.BlockSpec((local, CAP, F), lambda g, order: (0, first + g, 0))
+    half = count // 2
+    wide_slots = pl.BlockSpec((local, 2 * CAP, D), lambda g, order: (0, first // 2 + g, 0))
+    slots = pl.BlockSpec((local, 2 * CAP, F), lambda g, order: (0, first // 2 + g, 0))
+    whole = pl.BlockSpec((devices, local, row_count), lambda g, order: (0, 0, 0))
     block = pl.BlockSpec((row_count, D), lambda g, order: (0, 0))
+    sums = pl.BlockSpec((half, row_count, D), lambda g, order: (0, 0, 0))
     kept = () if kept is None else tuple(kept)
-    first_kept = 6 + count
-    half = count // 2
+    first_kept = 5 + count
     return pl.pallas_call(
         partial(expert_kernel, count),
         grid_spec=pltpu.PrefetchScalarGridSpec(
             num_scalar_prefetch=1,
-            grid=(count,),
+            grid=(half,),
             in_specs=[
-                pl.BlockSpec((1, local, row_count), lambda g, order: (order[g], 0, 0)),
-                pl.BlockSpec((1, row_count, local), lambda g, order: (order[g], 0, 0)),
-                pl.BlockSpec((1, local, row_count), lambda g, order: (order[g], 0, 0)),
+                whole,
+                whole,
                 *([block] * count),
                 slots,
                 pl.BlockSpec((2, D, local * F), lambda g, order: (0, 0, 0)),
@@ -940,11 +956,11 @@
                 slots,
                 slots,
                 slots,
-                pl.BlockSpec((1, local, row_count), lambda g, order: (g, 0, 0)),
-                pl.BlockSpec((1, row_count, D), lambda g, order: (jnp.minimum(g, half - 1), 0, 0)),
-                pl.BlockSpec((1, row_count, D), lambda g, order: (jnp.maximum(g - half, 0), 0, 0)),
+                pl.BlockSpec((2, local, row_count), lambda g, order: (g, 0, 0)),
+                sums,
+                sums,
             ),
-            scratch_shapes=[pltpu.VMEM((row_count, D), jnp.bfloat16)],
+            scratch_shapes=[pltpu.VMEM((local, 2 * CAP, D), jnp.bfloat16)],
         ),
         out_shape=(
             jax.ShapeDtypeStruct((local, devices * CAP, D), jnp.bfloat16),
@@ -958,12 +974,12 @@
         input_output_aliases={first_kept + i: i for i in range(len(kept))},
         compiler_params=params(),
         cost_estimate=pl.CostEstimate(
-            flops=work(5 * count),
+            flops=work(4 * count + 2),
             bytes_accessed=count * row_count * D * 6,
             transcendentals=count * local * CAP * F,
         ),
         name="expert_step",
-    )(order, places, columns, gates, *blocks, d_hidden, weights, *kept)
+    )(order, places, gates, *blocks, d_hidden, weights, *kept)
 
 
 def output_kernel(order, columns, hidden, weights, out_rows):
@@ -1106,22 +1122,25 @@
     return jnp.stack(steps).astype(jnp.int32)
 
 
-def scatter_sum(near, far, z):
-    summed = [added(a, core_swap(b)) for a, b in zip(reversed(near), reversed(far))][::-1]
-    part_3 = added(summed[3][0], row_swap(summed[4][0]))
+def scatter_sum(summed, z):
+    across_3 = row_swap(summed[4][0])
+    across_3, give_2, give_1, give_0 = together(
+        (across_3, summed[3][1], summed[2][1], summed[1][1])
+    )
+    part_3 = added(summed[3][0], across_3)
     up_3 = up_from(part_3, (0,))
     down_3 = down_from(part_3, (3,))
-    across_2 = row_swap(summed[3][1])
-    up_3, down_3, across_2 = together((up_3, down_3, across_2))
+    across_2 = row_swap(give_2)
+    up_3, down_3, across_2, give_1, give_0 = together((up_3, down_3, across_2, give_1, give_0))
     part_2 = added(summed[2][0], across_2)
     up_2 = up_from(added(part_2, up_3), (0, 1))
     down_2 = down_from(added(part_2, down_3), (3, 2))
-    across_1 = row_swap(summed[2][1])
-    up_2, down_2, across_1 = together((up_2, down_2, across_1))
+    across_1 = row_swap(give_1)
+    up_2, down_2, across_1, give_0 = together((up_2, down_2, across_1, give_0))
     part_1 = added(summed[1][0], across_1)
     up_1 = up_from(added(jnp.where(z == 2, part_3, part_1), up_2), (0, 1, 2))
     down_1 = down_from(added(jnp.where(z == 1, part_3, part_1), down_2), (1, 2, 3))
-    across_0 = row_swap(summed[1][1])
+    across_0 = row_swap(give_0)
     return [summed[0][0], across_0, up_1, down_1]
 
 
@@ -1129,23 +1148,30 @@
     return lax.dynamic_index_in_dim(values, index, axis, keepdims=False)
 
 
-def owner_first(values, position):
-    c = position % CORES
-    total, width = values.shape
+def halves(values, core, axis):
+    total = values.shape[axis]
+    shape = list(values.shape)
+    split = shape[:axis] + [LINE * ROWS * 2, CORES, total // (2 * LINE * ROWS * CORES)]
+    values = values.reshape(split + shape[axis + 1 :])
+    shape[axis] = total // CORES
+    return tuple(
+        one_of(values, which, axis + 1).reshape(shape) for which in (core, 1 - core)
+    )
+
+
+def by_side(values):
     spots = LINE * ROWS
-    values = values.reshape(2, spots, CORES, total // (2 * spots * CORES), width)
-    return added(one_of(values, c, 2), core_swap(one_of(values, 1 - c, 2)))
-
-
-def owner_last(values, taken, side):
+    return values.reshape(2, spots, values.shape[0] // (2 * spots), values.shape[1])
+
+
+def side_sum(values, side):
+    return added(one_of(values, side, 0), exchange(one_of(values, 1 - side, 0)))
+
+
+def owner_last(values):
     groups = [[spot * CORES + core for spot in range(LINE * ROWS)] for core in range(CORES)]
     values = lax.all_to_all(
-        added(one_of(values, side, 0), taken),
-        "ctx",
-        split_axis=0,
-        concat_axis=0,
-        tiled=True,
-        axis_index_groups=groups,
+        values, "ctx", split_axis=0, concat_axis=0, tiled=True, axis_index_groups=groups
     )
     return jnp.sum(values.astype(jnp.float32), axis=0)
 
@@ -1195,12 +1221,14 @@
     order = near_order(position)
 
     g_ups, g_downs, g_across, g_own = [grad_out], [grad_out], [], [grad_out]
-    for s in range(2):
+    for s in range(3):
         sent = send_on(s, g_own[s], g_ups[s], g_downs[s])
         if s == 1:
             packed_weights, *sent = together((packed_weights, *sent))
+        elif s == 0:
+            sent = together(tuple(sent))
         else:
-            sent = together(tuple(sent))
+            step_2 = sent
         g_across.append(sent[0])
         g_ups.append(sent[1])
         g_downs.append(sent[2])
@@ -1225,62 +1253,51 @@
     own_blocks = lax.dynamic_slice_in_dim(group_blocks, 2 * position, 2)
     offsets = jnp.arange(BLK, dtype=jnp.int32)
     positions = ((own_blocks % BLOCKS)[:, None] * BLK + offsets[None, :]).reshape(-1)
-    table = jnp.argsort(group_blocks).astype(jnp.int32)
+    core = position % CORES
+    table = jnp.concatenate([jnp.argsort(group_blocks).astype(jnp.int32), core.reshape(1)])
     frequency = 10000.0 ** (-(jnp.arange(HD // 2).astype(jnp.float32) * 2.0 / HD))
     angles = frequency[:, None] * positions.astype(jnp.float32)[None, :]
     cosine, sine = jnp.cos(angles)[None], jnp.sin(angles)[None]
     inputs = tokens.astype(jnp.float32)
     normed = rms_norm(inputs, gain_attn_full).astype(jnp.bfloat16)
+    normed_near, normed_far = halves(normed, core, 1)
     raw = tt(full_qkv, normed)
     queries = turn(raw[:wide].reshape(HQ, HD, row_count), cosine, sine).astype(jnp.bfloat16)
     keys = turn(raw[wide : wide + narrow].reshape(KVH, HD, row_count), cosine, sine).astype(
         jnp.bfloat16
     )
     values = raw[wide + narrow :].reshape(KVH, HD, row_count).astype(jnp.bfloat16)
-    ratio = HQ // KVH
-    outgoing = jnp.concatenate(
-        [queries, jnp.repeat(keys, ratio, axis=0), jnp.repeat(values, ratio, axis=0)], axis=1
-    )
-    outgoing, other_experts, slot_places = together((outgoing, other_experts, slot_places))
+    pairs = jnp.stack([keys, values], axis=1).reshape(HQ, HD, row_count)
+    outgoing = jnp.concatenate([queries, pairs], axis=1)
+    outgoing, other_experts, slot_places, *step_2 = together(
+        (outgoing, other_experts, slot_places, *step_2)
+    )
     packed = to_heads(outgoing)
+    g_across[2], g_ups[3], g_downs[3] = step_2
+    g_own[3] = newest(3, g_ups, g_downs, line_place)
     slot_columns = slot_places.transpose(0, 2, 1)
     first_half = jnp.where(side == 0, w_experts, other_experts)
     second_half = jnp.where(side == 0, other_experts, w_experts)
     experts = jnp.concatenate([first_half, second_half], axis=1)
     g_kept, g_first = None, 0
-    for s in range(2):
-        blocks = [g_own[s]] + g_across[s - 1 : s] if s else [g_own[0]]
+    for s in range(LINE + 1):
+        if s == LINE:
+            packed, g_own[3], *g_kept = together((packed, g_own[3], *g_kept))
+            other_packed = core_swap(packed)
+            g_across.append(row_swap(g_own[3]))
+            heads, attended_rows, log_sum = attention_forward(table, packed, other_packed)
+            heads, g_across[3] = together((heads, g_across[3]))
+            attended = to_heads(heads)
+        blocks = g_own[s : s + 1] + (g_across[s - 1 : s] if s else [])
         blocks += [core_swap(b) for b in blocks]
         count = len(blocks)
         g_kept = grad_step(
             g_first, order[g_first : g_first + count], slot_places, blocks, experts, g_kept
         )
         g_first += count
-    packed, *g_kept = together((packed, *g_kept))
-    sent = send_on(2, g_own[2], g_ups[2], g_downs[2])
-    heads, rows_0, sums_0 = attention_forward(0, table, packed)
-    heads, rows_0, sums_0, *sent = together((heads, rows_0, sums_0, *sent))
-    g_across.append(sent[0])
-    g_ups.append(sent[1])
-    g_downs.append(sent[2])
-    g_own.append(newest(3, g_ups, g_downs, line_place))
-    last_across = row_swap(g_own[3])
-    heads, rows_1, sums_1 = attention_forward(1, table, packed, heads)
-    heads, rows_1, sums_1, last_across = together((heads, rows_1, sums_1, last_across))
-    g_across.append(last_across)
-    log_sum = jnp.concatenate([sums_0, sums_1], axis=1)
-    attended = to_heads(heads)
-    for s in range(2, LINE + 1):
-        blocks = g_own[s : s + 1] + [g_across[s - 1]]
-        blocks += [core_swap(b) for b in blocks]
-        count = len(blocks)
-        g_kept = grad_step(
-            g_first, order[g_first : g_first + count], slot_places, blocks, experts, g_kept
-        )
-        g_first += count
     attended, *g_kept = together((attended, *g_kept))
+    attended = attended.reshape(wide, row_count)
     slot_grads, d_hidden = g_kept
-    attended = attended.reshape(wide, row_count)
     residual = inputs + tn(attended, full_output)
 
     normed_ffn = rms_norm(residual, gain_ffn_full).astype(jnp.bfloat16)
@@ -1289,7 +1306,7 @@
     powers = jnp.where(member, jnp.exp(masked - jnp.max(masked, axis=1, keepdims=True)), 0.0)
     gates = powers / jnp.sum(powers, axis=1, keepdims=True)
     slot_gates = to_heads(gates.T.reshape(devices, local, row_count))
-    near, far, d_gate_parts, kept = [], [], [], None
+    summed, d_gate_parts, kept = [], [], None
     own, across = normed_ffn, None
     ups, downs = [normed_ffn], [normed_ffn]
     first = 0
@@ -1299,14 +1316,15 @@
         blocks += [core_swap(b) for b in blocks]
         count = len(blocks)
         *kept, d_gate_part, near_part, far_part = expert_step(
-            first, order[first : first + count], slot_places, slot_columns, slot_gates, blocks,
-            d_hidden, experts, kept
-        )
-        if sent:
+            first, order[first : first + count], slot_places, slot_gates, blocks, d_hidden,
+            experts, kept
+        )
+        if sent and summed:
+            *sent, near_part, summed[-1] = together((*sent, near_part, summed[-1]))
+        elif sent:
             *sent, near_part = together((*sent, near_part))
         first += count
-        near.append(near_part)
-        far.append(far_part)
+        summed.append(added(near_part, core_swap(far_part)))
         d_gate_parts.append(d_gate_part)
         across = sent[0] if s < LINE else None
         if s < LINE - 1:
@@ -1314,7 +1332,7 @@
             downs.append(sent[2])
         own = newest(s + 1, ups, downs, line_place) if s < LINE - 1 else None
     slot_rows, hidden, d_gate_pre, d_up = kept
-    arrived = scatter_sum(near, far, line_place)
+    arrived = scatter_sum(summed, line_place)
     given = weight_grad(
         (1 - side).reshape(1), slot_rows, slot_grads, d_gate_pre, d_up, hidden, jnp.bfloat16
     )
@@ -1323,12 +1341,13 @@
     owned_experts = weight_grad(
         side.reshape(1), slot_rows, slot_grads, d_gate_pre, d_up, hidden, jnp.float32
     )
-    *arrived, out_rows, taken[0], taken[1], owned_experts = together(
-        (*arrived, out_rows, taken[0], taken[1], owned_experts)
-    )
+    back = jnp.argsort(order)
+    d_gate = to_heads(jnp.concatenate(d_gate_parts, axis=0)[back])
+    *arrived, out_rows, taken[0], taken[1], owned_experts, d_gate = together(
+        (*arrived, out_rows, taken[0], taken[1], owned_experts, d_gate)
+    )
+    d_gate = d_gate.reshape(E, row_count).T
     ffn_grad = sum(part.astype(jnp.float32) for part in arrived)
-    back = jnp.argsort(order)
-    d_gate = to_heads(jnp.concatenate(d_gate_parts, axis=0)[back]).reshape(E, row_count).T
     mixture = lax.psum_scatter(out_rows, "ctx", scatter_dimension=0, tiled=True)
 
     d_logits = gates * (d_gate - jnp.sum(gates * d_gate, axis=1, keepdims=True))
@@ -1344,48 +1363,64 @@
     branch_grad = residual_grad.astype(jnp.bfloat16)
     attended_grad = nt(full_output, branch_grad).astype(jnp.bfloat16)
     d_heads = to_heads(attended_grad.reshape(HQ, HD, row_count))
-    output_grad = nn(attended, branch_grad)
-    first_parts = owner_first(
-        jnp.concatenate(
-            [
-                output_grad.astype(jnp.bfloat16),
-                router_grad.astype(jnp.bfloat16),
-                gain_ffn_grad[:, None].astype(jnp.bfloat16),
-                jnp.zeros((D, 95), jnp.bfloat16),
-            ],
-            axis=1,
-        ),
-        position,
-    )
-    d_heads, first_parts, taken[2] = together((d_heads, first_parts, taken[2]))
+    output_grad = jnp.concatenate(
+        [
+            nn(attended, branch_grad).astype(jnp.bfloat16),
+            router_grad.astype(jnp.bfloat16),
+            gain_ffn_grad[:, None].astype(jnp.bfloat16),
+            jnp.zeros((D, 95), jnp.bfloat16),
+        ],
+        axis=1,
+    )
+    first_near, first_far = halves(output_grad, core, 0)
+    first_parts = by_side(added(first_near, core_swap(first_far)))
+    d_heads, first_parts = together((d_heads, first_parts))
     first_taken = exchange(one_of(first_parts, 1 - side, 0))
 
-    d_packed = to_heads(attention_backward(table, packed, d_heads, rows_0, rows_1, log_sum))
-    d_packed, first_taken = together((d_packed, first_taken))
-    first_owned = owner_last(first_parts, first_taken, side)
-    d_packed = d_packed.astype(jnp.float32)
-    d_query = turn(d_packed[:, :HD], cosine, -sine).astype(jnp.bfloat16).reshape(wide, row_count)
-    pairs = d_packed[:, HD:].reshape(KVH, ratio, 2 * HD, row_count).sum(axis=1)
-    d_key = turn(pairs[:, :HD], cosine, -sine).astype(jnp.bfloat16).reshape(narrow, row_count)
-    d_value = pairs[:, HD:].astype(jnp.bfloat16).reshape(narrow, row_count)
-    d_qkv = jnp.concatenate([d_query, d_key, d_value], axis=0)
-    qkv_grad = tt(normed, d_qkv)
-    normed_grad = tt(d_qkv, full_qkv)
+    q_grads, kept_grads, given_grads = attention_backward(
+        table, packed, other_packed, d_heads, attended_rows, log_sum
+    )
+    q_grads, first_taken, taken[2] = together((q_grads, first_taken, taken[2]))
+    q_back = to_heads(q_grads)
+    pair_grads = added(kept_grads, core_swap(given_grads))
+    q_back, pair_grads = together((q_back, pair_grads))
+    pair_back = to_heads(pair_grads)
+    d_query = (
+        turn(q_back.astype(jnp.float32), cosine, -sine)
+        .astype(jnp.bfloat16)
+        .reshape(wide, row_count)
+    )
+    far_grad = core_swap(tt(normed_far, d_query).astype(jnp.bfloat16))
+    near_grad = tt(normed_near, d_query).astype(jnp.bfloat16)
+    query_parts = side_sum(by_side(added(near_grad, far_grad)), side)
+    query_parts = jnp.concatenate(
+        [query_parts, added(one_of(first_parts, side, 0), first_taken)], axis=2
+    )
+    pair_back, query_parts = together((pair_back, query_parts))
+    query_owned = owner_last(query_parts)
+    pairs = pair_back.astype(jnp.float32).reshape(KVH, 2, HD, row_count)
+    d_pairs = jnp.concatenate(
+        [
+            turn(pairs[:, 0], cosine, -sine).astype(jnp.bfloat16),
+            pairs[:, 1].astype(jnp.bfloat16),
+        ],
+        axis=0,
+    ).reshape(2 * narrow, row_count)
+    far_grad = core_swap(tt(normed_far, d_pairs).astype(jnp.bfloat16))
+    near_grad = tt(normed_near, d_pairs).astype(jnp.bfloat16)
+    normed_grad = tt(d_query, full_qkv[:, :wide]) + tt(d_pairs, full_qkv[:, wide:])
+    pair_parts = side_sum(by_side(added(near_grad, far_grad)), side)
     _, norm_back_attn = jax.vjp(rms_norm, inputs, gain_attn_full)
     input_norm_grad, gain_attn_grad = norm_back_attn(normed_grad)
     tokens_grad = residual_grad + input_norm_grad
-    owned_parts = owner_first(
+    gain_near, gain_far = halves(gain_attn_grad[:, None].astype(jnp.bfloat16), core, 0)
+    gain_parts = side_sum(by_side(added(gain_near, core_swap(gain_far))), side)
+    pair_owned = owner_last(
         jnp.concatenate(
-            [
-                qkv_grad.astype(jnp.bfloat16),
-                gain_attn_grad[:, None].astype(jnp.bfloat16),
-                jnp.zeros((D, 127), jnp.bfloat16),
-            ],
-            axis=1,
-        ),
-        position,
-    )
-    owned = owner_last(owned_parts, exchange(one_of(owned_parts, 1 - side, 0)), side)
+            [pair_parts, gain_parts, jnp.zeros((*gain_parts.shape[:2], 127), jnp.bfloat16)],
+            axis=2,
+        )
+    )
     mixture, late = together((mixture, d_query))
     mixed = (residual + mixture.astype(jnp.float32)).astype(jnp.bfloat16)
     expert_grad = jnp.stack(
@@ -1394,13 +1429,13 @@
     return (
         mixed,
         tokens_grad,
-        owned[:, :wide],
-        owned[:, wide : wide + narrow],
-        owned[:, wide + narrow : wide + 2 * narrow],
-        first_owned[:, :D],
-        owned[:, wide + 2 * narrow],
-        first_owned[:, D + E],
-        first_owned[:, D : D + E],
+        query_owned[:, :wide],
+        pair_owned[:, :narrow],
+        pair_owned[:, narrow : 2 * narrow],
+        query_owned[:, wide : wide + D],
+        pair_owned[:, 2 * narrow],
+        query_owned[:, wide + D + E],
+        query_owned[:, wide + D : wide + D + E],
         expert_grad,
     )
 

time: 916 us -> 840 us (0.917)
  waiting for transfers between devices: 282 us -> 219 us
  Pallas kernels: 297 us -> 256 us
  other arithmetic: 78.2 us -> 92.2 us
    pallas_call x3 -> x2, Pallas kernels: 116 us -> 84.1 us  [the longest x1 52.9 us: attention_backward(): pl.pallas_call(attention_backward_kernel, out_shape=(shape,) * 3, in_spec...]
    ppermute x6 -> x8, waiting for transfers between devices: 47.6 us -> 20.8 us  [exchange(): return lax.ppermute(values, 'dp', [(0, 1), (1, 0)])]
    all_to_all x2, waiting for transfers between devices: 29.3 us -> 5.33 us  [owner_last(): lax.all_to_all(values, 'ctx', split_axis=0, concat_axis=0, tiled=True, ax...]
    all_to_all x7 -> x8, starting transfers between devices: 41.9 us -> 63.3 us  [to_heads(): lax.all_to_all(values, 'ctx', split_axis=0, concat_axis=0, tiled=True)]
    all_to_all x2, starting transfers between devices: 42.4 us -> 22.1 us  [owner_last(): lax.all_to_all(values, 'ctx', split_axis=0, concat_axis=0, tiled=True, ax...]
    all_to_all x7 -> x8, waiting for transfers between devices: 71.6 us -> 55.9 us  [to_heads(): lax.all_to_all(values, 'ctx', split_axis=0, concat_axis=0, tiled=True)]
    unnamed x135 -> x157, local copies, waits for them, and re-layouts: 10.1 us -> 18.5 us
    convert_element_type x10 -> x14, other arithmetic: 25.7 us -> 34.2 us  [added(): return total.astype(jnp.bfloat16)]
  transfers between devices with their start and end apart: 70 -> 77, of which waited for: 28 -> 33; matrix products, arithmetic and copies ran while one was open for 13% -> 18% of each run, Pallas kernels for 33% -> 31%
where the time goes in v2:
time: 840 us; the launch traced here: 831 us
  Pallas kernels  256 us (30%)
  waiting for transfers between devices  219 us (26%)
  starting transfers between devices  149 us (18%)
  other arithmetic  92.2 us (11%)
  local copies, waits for them, and re-layouts  55 us (7%)
  matrix products  42.6 us (5%)
  between operations  18.2 us (2%)
    ppermute x57, waiting for transfers between devices, move(): return lax.ppermute(values, 'ctx', pairs)  126 us
    pallas_call x5, Pallas kernels, expert_step(): pl.pallas_call(partial(expert_kernel, count), grid_spec=pltpu.PrefetchSca...  80 us
    all_to_all x8, starting transfers between devices, to_heads(): lax.all_to_all(values, 'ctx', split_axis=0, concat_axis=0, tiled=True)  63.3 us
    all_to_all x8, waiting for transfers between devices, to_heads(): lax.all_to_all(values, 'ctx', split_axis=0, concat_axis=0, tiled=True)  55.9 us
    ppermute x57, starting transfers between devices, move(): return lax.ppermute(values, 'ctx', pairs)  55.1 us
    pallas_call x1, Pallas kernels, attention_backward(): pl.pallas_call(attention_backward_kernel, out_shape=(shape,) * 3, in_spec...  52.9 us
    pallas_call x5, Pallas kernels, grad_step(): pl.pallas_call(partial(grad_kernel, count), grid_spec=pltpu.PrefetchScala...  36.7 us
    convert_element_type x14, other arithmetic, added(): return total.astype(jnp.bfloat16)  34.2 us
  transfers between devices with their start and end apart: 77, of which 33 were waited for; matrix products, arithmetic and copies ran while one was open for 18% of the time, Pallas kernels for 31%

profile of v2, /device:TPU:0, one launch (start us, length us, event | category | flops | bytes accessed | tf_op | source)
XLA Modules:
  0.0 831.4 jit_solution(16221330454633701439)
XLA Ops:
  30.6 7.9 collective-permute-done.refs_1_
  38.5 8.9 %collective-permute-done.1 = bf16[512,1024]{1,0:T(8,128)(2,1)S(1)} collective-permute-done((bf16[512,1024]{1,0:T(8,128)(2,1)}, bf16[512,1024]{1,0:T(8,128)(2,1)S(1)}, u32[]{:S(2)}, u32[]{:S(2)}) %collective-permute-start.1) | collective-permute-done | bytes 1048608 | tf_op jit(solution)/shard_map/ppermute | solution.py:1063
  62.8 27.4 %collective-permute-done.3.refs_1_ = bf16[512,1024]{1,0:T(8,128)(2,1)} collective-permute-done((bf16[512,1024]{1,0:T(8,128)(2,1)}, bf16[512,1024]{1,0:T(8,128)(2,1)}, u32[]{:S(2)}, u32[]{:S(2)}) %collective-permute-start.3) | collective-permute-done | bytes 1048608 | tf_op jit(solution)/shard_map/ppermute | solution.py:1063
  94.3 10.7 %all-gather.2.cloned.1.call-done = bf16[1024,3200]{1,0:T(8,128)(2,1)} async-done(((bf16[32,3200]{1,0:T(8,128)(2,1)}), bf16[1024,3200]{1,0:T(8,128)(2,1)}) %all-gather.2.cloned.1.call-update) | async-done | bytes 6553616 | tf_op jit(solution)/shard_map/all_gather | solution.py:1212
  124.7 11.2 %collective-permute-done.7.refs_1_ = bf16[512,1024]{1,0:T(8,128)(2,1)S(1)} collective-permute-done((bf16[512,1024]{1,0:T(8,128)(2,1)}, bf16[512,1024]{1,0:T(8,128)(2,1)S(1)}, u32[]{:S(2)}, u32[]{:S(2)}) %collective-permute-start.7) | collective-permute-done | bytes 1048608 | tf_op jit(solution)/shard_map/ppermute | solution.py:1063
  137.5 6.8 all-to-all-start.1
  160.2 8.3 %grad_step.6 = (bf16[2,2560,1024]{2,1,0:T(8,128)(2,1)}, bf16[2,2560,512]{2,1,0:T(8,128)(2,1)}) custom-call(s32[4]{0:T(128)} %pad_add_fusion.3.order, f32[16,2,512]{2,1,0:T(2,128)} %copy-done.40, bf16[512,1024]{1,0:T(8,128)(2,1)} %broadcast_select_fusion.5.refs_0_, ...), custom_call_target="tpu_custom_call", output_to_operand_aliasing={{0}: (7, {}), {1}: (8, {})} | custom-call | flops 11500000256 | bytes 8388608 | tf_op jit(solution)/shard_map/grad_step/pallas_call | solution.py:837
  168.5 8.4 %grad_step.7 = (bf16[2,2560,1024]{2,1,0:T(8,128)(2,1)}, bf16[2,2560,512]{2,1,0:T(8,128)(2,1)}) custom-call(s32[4]{0:T(128)} %pad_add_fusion.2.order, f32[16,2,512]{2,1,0:T(2,128)} %copy-done.40, bf16[512,1024]{1,0:T(8,128)(2,1)} %broadcast_select_fusion.4.refs_0_, ...), custom_call_target="tpu_custom_call", output_to_operand_aliasing={{0}: (7, {}), {1}: (8, {})} | custom-call | flops 11500000256 | bytes 8388608 | tf_op jit(solution)/shard_map/grad_step/pallas_call | solution.py:837
  177.9 8.5 %grad_step.8 = (bf16[2,2560,1024]{2,1,0:T(8,128)(2,1)}, bf16[2,2560,512]{2,1,0:T(8,128)(2,1)}) custom-call(s32[4]{0:T(128)} %pad_add_fusion.1.order, f32[16,2,512]{2,1,0:T(2,128)} %copy-done.40, bf16[512,1024]{1,0:T(8,128)(2,1)} %select_select_fusion.1.refs_0_, bf16[512,1024]{1,0:T(8,128)(2,1)} %copy-done.66, ...), custom_call_target="tpu_custom_call", output_to_operand_aliasing={{0}: (7, {}), {1}: (8, {})} | custom-call | flops 11500000256 | bytes 8388608 | tf_op jit(solution)/shard_map/grad_step/pallas_call | solution.py:837
  193.1 31.2 %attention_forward.1 = (bf16[16,64,512]{2,1,0:T(8,128)(2,1)}, f32[64,8192]{1,0:T(8,128)}, f32[1,8192]{1,0:T(1,128)}) custom-call(s32[33]{0:T(128)} %pad_add_fusion.table, bf16[16,128,512]{2,1,0:T(8,128)(2,1)} %all-to-all-done.1.mine, bf16[16,128,512]{2,1,0:T(8,128)(2,1)} %copy-done.65), custom_call_target="tpu_custom_call" | custom-call | flops 41400000512 | bytes 4194304 | tf_op jit(solution)/shard_map/attention_forward/pallas_call | solution.py:729
  224.3 9.2 %all-to-all-start.2 = ((bf16[16,64,512]{2,1,0:T(8,128)(2,1)}), bf16[16,64,512]{2,1,0:T(8,128)(2,1)S(1)}, u32[]{:S(2)}, u32[]{:S(2)}) async-start(bf16[16,64,512]{2,1,0:T(8,128)(2,1)} %get-tuple-element.167), calls=%async_computation.2 | async-start | bytes 2097152 | tf_op jit(solution)/shard_map/all_to_all | solution.py:1184
  243.2 13.3 %all-to-all-done.2 = bf16[16,64,512]{2,1,0:T(8,128)(2,1)S(1)} async-done(((bf16[16,64,512]{2,1,0:T(8,128)(2,1)}), bf16[16,64,512]{2,1,0:T(8,128)(2,1)S(1)}, u32[]{:S(2)}, u32[]{:S(2)}) %all-to-all-start.2) | async-done | bytes 1048608 | tf_op jit(solution)/shard_map/all_to_all | solution.py:1184
  263.7 6.7 all-to-all-start.3
  277.9 11.5 %expert_step.5 = (bf16[2,2560,1024]{2,1,0:T(8,128)(2,1)}, bf16[2,2560,512]{2,1,0:T(8,128)(2,1)}, bf16[2,2560,512]{2,1,0:T(8,128)(2,1)}, bf16[2,2560,512]{2,1,0:T...) custom-call(s32[2]{0:T(128)} %pad_add_fusion.4.order, ...), custom_call_target="tpu_custom_call" | custom-call | flops 11500000256 | bytes 6291456 | tf_op jit(solution)/shard_map/expert_step/pallas_call | solution.py:941
  289.4 7.4 collective-permute-done.20.refs_1_
  309.1 18.9 %expert_step.6 = (bf16[2,2560,1024]{2,1,0:T(8,128)(2,1)}, bf16[2,2560,512]{2,1,0:T(8,128)(2,1)}, bf16[2,2560,512]{2,1,0:T(8,128)(2,1)}, bf16[2,2560,512]{2,1,0:T...) custom-call(s32[4]{0:T(128)} %pad_add_fusion.3.order, ...), custom_call_target="tpu_custom_call", output_to_operand_aliasing={{0}: (9, {}), {1}: (10, {}), {2}: (11, {}), {3}: (12, {})} | custom-call | flops 20700000256 | bytes 12582912 | tf_op jit(solution)/shard_map/expert_step/pallas_call | solution.py:941
  344.4 18.8 %expert_step.7 = (bf16[2,2560,1024]{2,1,0:T(8,128)(2,1)}, bf16[2,2560,512]{2,1,0:T(8,128)(2,1)}, bf16[2,2560,512]{2,1,0:T(8,128)(2,1)}, bf16[2,2560,512]{2,1,0:T...) custom-call(s32[4]{0:T(128)} %pad_add_fusion.2.order, ...), custom_call_target="tpu_custom_call", output_to_operand_aliasing={{0}: (9, {}), {1}: (10, {}), {2}: (11, {}), {3}: (12, {})} | custom-call | flops 20700000256 | bytes 12582912 | tf_op jit(solution)/shard_map/expert_step/pallas_call | solution.py:941
  375.8 19.2 %expert_step.8 = (bf16[2,2560,1024]{2,1,0:T(8,128)(2,1)}, bf16[2,2560,512]{2,1,0:T(8,128)(2,1)}, bf16[2,2560,512]{2,1,0:T(8,128)(2,1)}, bf16[2,2560,512]{2,1,0:T...) custom-call(s32[4]{0:T(128)} %pad_add_fusion.1.order, ...), custom_call_target="tpu_custom_call", output_to_operand_aliasing={{0}: (9, {}), {1}: (10, {}), {2}: (11, {}), {3}: (12, {})} | custom-call | flops 20700000256 | bytes 12582912 | tf_op jit(solution)/shard_map/expert_step/pallas_call | solution.py:941
  402.4 11.5 %expert_step.9 = (bf16[2,2560,1024]{2,1,0:T(8,128)(2,1)}, bf16[2,2560,512]{2,1,0:T(8,128)(2,1)}, bf16[2,2560,512]{2,1,0:T(8,128)(2,1)}, bf16[2,2560,512]{2,1,0:T...) custom-call(s32[2]{0:T(128)} %pad_add_fusion.5.order, ...), custom_call_target="tpu_custom_call", output_to_operand_aliasing={{0}: (7, {}), {1}: (8, {}), {2}: (9, {}), {3}: (10, {})} | custom-call | flops 11500000256 | bytes 6291456 | tf_op jit(solution)/shard_map/expert_step/pallas_call | solution.py:941
  430.7 15.6 %collective-permute-done.43 = bf16[512,1024]{1,0:T(8,128)(2,1)} collective-permute-done((bf16[512,1024]{1,0:T(8,128)(2,1)}, bf16[512,1024]{1,0:T(8,128)(2,1)}, u32[]{:S(2)}, u32[]{:S(2)}) %collective-permute-start.43) | collective-permute-done | bytes 1048608 | tf_op jit(solution)/shard_map/ppermute | solution.py:1063
  453.8 14.2 %weight_grad.2 = (bf16[512,1024]{1,0:T(8,128)(2,1)}, bf16[512,1024]{1,0:T(8,128)(2,1)}, bf16[512,1024]{1,0:T(8,128)(2,1)}) custom-call(s32[1]{0:T(128)} %bitcast.45.half, bf16[2,2560,1024]{2,1,0:T(8,128)(2,1)} %get-tuple-element.232.slot_rows, bf16[2,2560,1024]{2,1,0:T(8,128)(2,1)} %get-tuple-element.233.slot_grads, ...), custom_call_target="tpu_custom_call" | custom-call | flops 17250000896 | bytes 41943040 | tf_op jit(solution)/shard_map/weight_grad/pallas_call | solution.py:1028
  486.8 26.5 %output_pass.1 = bf16[8192,1024]{1,0:T(8,128)(2,1)} custom-call(s32[16]{0:T(128)} %copy-done.64, f32[16,512,2]{2,1,0:T(8,128)} %bitcast.178, bf16[2,2560,512]{2,1,0:T(8,128)(2,1)} %get-tuple-element.231.hidden, bf16[3,1024,1024]{2,1,0:T(8,128)(2,1)} %pad_maximum_fusion.refs_2_.refs_4_.refs_3_.refs_5_.weights), custom_call_target="tpu_custom_call" | custom-call | flops 29899999232 | bytes 25165824 | tf_op jit(solution)/shard_map/output_pass/pallas_call | solution.py:996
  521.8 14.6 %weight_grad.3 = (f32[512,1024]{1,0:T(8,128)}, f32[512,1024]{1,0:T(8,128)}, f32[512,1024]{1,0:T(8,128)}) custom-call(s32[1]{0:T(128)} %bitcast.46.half, bf16[2,2560,1024]{2,1,0:T(8,128)(2,1)} %get-tuple-element.232.slot_rows, bf16[2,2560,1024]{2,1,0:T(8,128)(2,1)} %get-tuple-element.233.slot_grads, bf16[2,2560,512]{2,1,0:T(8,128)(2,1)} %get-tuple-element.234.d_gate_pre, ...), custom_call_target="tpu_custom_call" | custom-call | flops 17250000896 | bytes 41943040 | tf_op jit(solution)/shard_map/weight_grad/pallas_call | solution.py:1028
  585.1 9.1 %all-to-all-done.5.d_out = bf16[16,64,512]{2,1,0:T(8,128)(2,1)} async-done(((bf16[16,64,512]{2,1,0:T(8,128)(2,1)}), bf16[16,64,512]{2,1,0:T(8,128)(2,1)}, u32[]{:S(2)}, u32[]{:S(2)}) %all-to-all-start.5) | async-done | bytes 1048608 | tf_op jit(solution)/shard_map/all_to_all | solution.py:1184
  595.4 52.9 %attention_backward.1 = (bf16[16,64,512]{2,1,0:T(8,128)(2,1)}, bf16[16,64,512]{2,1,0:T(8,128)(2,1)}, bf16[16,64,512]{2,1,0:T(8,128)(2,1)}) custom-call(s32[33]{0:T(128)} %pad_add_fusion.table, bf16[16,128,512]{2,1,0:T(8,128)(2,1)} %all-to-all-done.1.mine, bf16[16,128,512]{2,1,0:T(8,128)(2,1)} %copy-done.65, bf16[16,64,512]{2,1,0:T(8,128)(2,1)} %all-to-all-done.5.d_out, ...), custom_call_target="tpu_custom_call" | custom-call | flops 66700001280 | bytes 6291456 | tf_op jit(solution)/shard_map/attention_backward/pallas_call | solution.py:755
  649.1 19.6 %all-to-all-start.6 = ((bf16[16,64,512]{2,1,0:T(8,128)(2,1)}), bf16[16,64,512]{2,1,0:T(8,128)(2,1)S(1)}, u32[]{:S(2)}, u32[]{:S(2)}) async-start(bf16[16,64,512]{2,1,0:T(8,128)(2,1)} %get-tuple-element.259), calls=%async_computation.7 | async-start | bytes 2097152 | tf_op jit(solution)/shard_map/all_to_all | solution.py:1184
  676.4 15.3 %all-to-all-done.6 = bf16[16,64,512]{2,1,0:T(8,128)(2,1)S(1)} async-done(((bf16[16,64,512]{2,1,0:T(8,128)(2,1)}), bf16[16,64,512]{2,1,0:T(8,128)(2,1)S(1)}, u32[]{:S(2)}, u32[]{:S(2)}) %all-to-all-start.6) | async-done | bytes 1048608 | tf_op jit(solution)/shard_map/all_to_all | solution.py:1184
  695.4 6.6 all-to-all-start.7
  709.4 11.5 %collective-permute-done.60 = bf16[8,32,1024]{2,1,0:T(8,128)(2,1)} collective-permute-done((bf16[8,32,1024]{2,1,0:T(8,128)(2,1)}, bf16[8,32,1024]{2,1,0:T(8,128)(2,1)}, u32[]{:S(2)}, u32[]{:S(2)}) %collective-permute-start.60) | collective-permute-done | bytes 524320 | tf_op jit(solution)/shard_map/ppermute | solution.py:1180
  723.3 17.9 %all-to-all-done.7 = bf16[16,64,512]{2,1,0:T(8,128)(2,1)} async-done(((bf16[16,64,512]{2,1,0:T(8,128)(2,1)}), bf16[16,64,512]{2,1,0:T(8,128)(2,1)}, u32[]{:S(2)}, u32[]{:S(2)}) %all-to-all-start.7) | async-done | bytes 1048608 | tf_op jit(solution)/shard_map/all_to_all | solution.py:1184
  745.6 16.1 %all-to-all-start.8 = ((bf16[8,32,2176]{2,1,0:T(8,128)(2,1)}), bf16[8,32,2176]{2,1,0:T(8,128)(2,1)}, u32[]{:S(2)}, u32[]{:S(2)}) async-start(bf16[8,32,2176]{2,1,0:T(8,128)(2,1)} %pad_maximum_fusion.3), calls=%async_computation.9 | async-start | bytes 2228224 | tf_op jit(solution)/shard_map/all_to_all | solution.py:1173
  782.3 9.3 %collective-permute-done.62 = bf16[8,32,1024]{2,1,0:T(8,128)(2,1)} collective-permute-done((bf16[8,32,1024]{2,1,0:T(8,128)(2,1)}, bf16[8,32,1024]{2,1,0:T(8,128)(2,1)}, u32[]{:S(2)}, u32[]{:S(2)}) %collective-permute-start.62) | collective-permute-done | bytes 524320 | tf_op jit(solution)/shard_map/ppermute | solution.py:1180
  (424 shorter events, 338.0 us)
Async XLA Ops:
  7.2 97.9 %all-gather.2.cloned.1.call-start = ((), (), s32[]{:S(2)}) async-start(), calls=%async_computation.11 | async-start | bytes 6758400 | tf_op jit(solution)/shard_map/all_gather | solution.py:1212
  10.4 28.1 %collective-permute-start = (bf16[512,1024]{1,0:T(8,128)(2,1)}, bf16[512,1024]{1,0:T(8,128)(2,1)}, u32[]{:S(2)}, u32[]{:S(2)}) collective-permute-start(bf16[512,1024]{1,0:T(8,128)(2,1)} %refs_0_.1), channel_id=1, source_target_pairs={{0,2},{1,3},{2,0},{3,1},{4,6},{5,7},{6,4},{7,5},{8,10},{9,11},{10,... | collective-permute-start | bytes 3145736 | tf_op jit(solution)/shard_map/ppermute | solution.py:1063
  13.5 33.9 %collective-permute-start.1 = (bf16[512,1024]{1,0:T(8,128)(2,1)}, bf16[512,1024]{1,0:T(8,128)(2,1)S(1)}, u32[]{:S(2)}, u32[]{:S(2)}) collective-permute-start(bf16[512,1024]{1,0:T(8,128)(2,1)} %refs_0_.1), channel_id=1, source_target_pairs={{0,4},{1,5},{2,6},{3,7},{4,8},{5,9},{6,10},{7,11},{8,12},{9,13},{1... | collective-permute-start | bytes 3145736 | tf_op jit(solution)/shard_map/ppermute | solution.py:1063
  17.0 35.7 %collective-permute-start.2 = (bf16[512,1024]{1,0:T(8,128)(2,1)}, bf16[512,1024]{1,0:T(8,128)(2,1)S(1)}, u32[]{:S(2)}, u32[]{:S(2)}) collective-permute-start(bf16[512,1024]{1,0:T(8,128)(2,1)} %refs_0_.1), channel_id=1, source_target_pairs={{4,0},{5,1},{6,2},{7,3},{8,4},{9,5},{10,6},{11,7},{12,8},{13,9},{1... | collective-permute-start | bytes 3145736 | tf_op jit(solution)/shard_map/ppermute | solution.py:1063
  18.3 135.4 %collective-permute-start.16 = (bf16[512,1024]{1,0:T(8,128)(2,1)}, bf16[512,1024]{1,0:T(8,128)(2,1)}, u32[]{:S(2)}, u32[]{:S(2)}) collective-permute-start(bf16[512,1024]{1,0:T(8,128)(2,1)} %refs_0_.1), channel_id=1, source_target_pairs={{0,1},{1,0},{2,3},{3,2},{4,5},{5,4},{6,7},{7,6},{8,9},{9,8},{10,11... | collective-permute-start | bytes 3145736 | tf_op jit(solution)/shard_map/ppermute | solution.py:1063
  20.2 116.7 %all-to-all-start = ((f32[16,2,512]{2,1,0:T(2,128)}), f32[16,2,512]{2,1,0:T(2,128)S(1)}, u32[]{:S(2)}, u32[]{:S(2)}) async-start(f32[16,2,512]{2,1,0:T(2,128)} %reshape.436), calls=%async_computation | async-start | bytes 131072 | tf_op jit(solution)/shard_map/all_to_all | solution.py:1184
  26.3 98.4 %collective-permute-start.6 = (bf16[3,512,1024]{2,1,0:T(8,128)(2,1)}, bf16[3,512,1024]{2,1,0:T(8,128)(2,1)}, u32[]{:S(2)}, u32[]{:S(2)}) collective-permute-start(bf16[3,512,1024]{2,1,0:T(8,128)(2,1)} %param.22), channel_id=1, source_target_pairs={{0,16},{16,0},{1,17},{17,1},{2,18},{18,2},{3,19},{19,3},{4,20},{20... | collective-permute-start | bytes 9437192 | tf_op jit(solution)/shard_map/ppermute | solution.py:1180
  52.8 37.5 %collective-permute-start.4 = (bf16[512,1024]{1,0:T(8,128)(2,1)S(1)}, bf16[512,1024]{1,0:T(8,128)(2,1)}, u32[]{:S(2)}, u32[]{:S(2)}) collective-permute-start(bf16[512,1024]{1,0:T(8,128)(2,1)S(1)} %collective-permute-done.1), channel_id=1, source_target_pairs={{4,8},{5,9},{6,10},{7,11},{8,12},{9,13},{10,14},{11,15},{20,24},{2... | collective-permute-start | bytes 3145736 | tf_op jit(solution)/shard_map/ppermute | solution.py:1063
  54.4 39.9 %collective-permute-start.5 = (bf16[512,1024]{1,0:T(8,128)(2,1)S(1)}, bf16[512,1024]{1,0:T(8,128)(2,1)}, u32[]{:S(2)}, u32[]{:S(2)}) collective-permute-start(bf16[512,1024]{1,0:T(8,128)(2,1)S(1)} %collective-permute-done.2), channel_id=1, source_target_pairs={{4,0},{5,1},{6,2},{7,3},{8,4},{9,5},{10,6},{11,7},{20,16},{21,17},... | collective-permute-start | bytes 3145736 | tf_op jit(solution)/shard_map/ppermute | solution.py:1063
  56.8 33.5 %collective-permute-start.3 = (bf16[512,1024]{1,0:T(8,128)(2,1)}, bf16[512,1024]{1,0:T(8,128)(2,1)}, u32[]{:S(2)}, u32[]{:S(2)}) collective-permute-start(bf16[512,1024]{1,0:T(8,128)(2,1)} %broadcast_select_fusion.5.refs_0_), channel_id=1, source_target_pairs={{0,2},{1,3},{2,0},{3,1},{4,6},{5,7},{6,4},{7,5},{8,10},{9,11},{10,... | collective-permute-start | bytes 3145736 | tf_op jit(solution)/shard_map/ppermute | solution.py:1063
  105.1 30.8 %collective-permute-start.8 = (bf16[512,1024]{1,0:T(8,128)(2,1)}, bf16[512,1024]{1,0:T(8,128)(2,1)}, u32[]{:S(2)}, u32[]{:S(2)}) collective-permute-start(bf16[512,1024]{1,0:T(8,128)(2,1)} %collective-permute-done.4), channel_id=1, source_target_pairs={{8,12},{9,13},{10,14},{11,15},{24,28},{25,29},{26,30},{27,31}} | collective-permute-start | bytes 3145736 | tf_op jit(solution)/shard_map/ppermute | solution.py:1063
  106.7 29.7 %collective-permute-start.9 = (bf16[512,1024]{1,0:T(8,128)(2,1)}, bf16[512,1024]{1,0:T(8,128)(2,1)}, u32[]{:S(2)}, u32[]{:S(2)}) collective-permute-start(bf16[512,1024]{1,0:T(8,128)(2,1)} %collective-permute-done.5), channel_id=1, source_target_pairs={{4,0},{5,1},{6,2},{7,3},{20,16},{21,17},{22,18},{23,19}} | collective-permute-start | bytes 3145736 | tf_op jit(solution)/shard_map/ppermute | solution.py:1063
  124.7 35.3 %collective-permute-start.14 = (bf16[512,1024]{1,0:T(8,128)(2,1)}, bf16[512,1024]{1,0:T(8,128)(2,1)}, u32[]{:S(2)}, u32[]{:S(2)}) collective-permute-start(bf16[512,1024]{1,0:T(8,128)(2,1)} %broadcast_select_fusion.5.refs_0_), channel_id=1, source_target_pairs={{0,1},{1,0},{2,3},{3,2},{4,5},{5,4},{6,7},{7,6},{8,9},{9,8},{10,11... | collective-permute-start | bytes 3145736 | tf_op jit(solution)/shard_map/ppermute | solution.py:1063
  135.9 32.6 %collective-permute-start.12 = (bf16[512,1024]{1,0:T(8,128)(2,1)}, bf16[512,1024]{1,0:T(8,128)(2,1)}, u32[]{:S(2)}, u32[]{:S(2)}) collective-permute-start(bf16[512,1024]{1,0:T(8,128)(2,1)} %broadcast_select_fusion.4.refs_0_), channel_id=1, source_target_pairs={{0,1},{1,0},{2,3},{3,2},{4,5},{5,4},{6,7},{7,6},{8,9},{9,8},{10,11... | collective-permute-start | bytes 3145736 | tf_op jit(solution)/shard_map/ppermute | solution.py:1063
  136.9 31.6 %collective-permute-start.13 = (bf16[512,1024]{1,0:T(8,128)(2,1)}, bf16[512,1024]{1,0:T(8,128)(2,1)}, u32[]{:S(2)}, u32[]{:S(2)}) collective-permute-start(bf16[512,1024]{1,0:T(8,128)(2,1)} %collective-permute-done.3.refs_1_), channel_id=1, source_target_pairs={{0,1},{1,0},{2,3},{3,2},{4,5},{5,4},{6,7},{7,6},{8,9},{9,8},{10,11... | collective-permute-start | bytes 3145736 | tf_op jit(solution)/shard_map/ppermute | solution.py:1063
  137.5 48.9 %all-to-all-start.1 = ((bf16[16,128,512]{2,1,0:T(8,128)(2,1)}), bf16[16,128,512]{2,1,0:T(8,128)(2,1)}, u32[]{:S(2)}, u32[]{:S(2)}) async-start(bf16[16,128,512]{2,1,0:T(8,128)(2,1)} %pad_maximum_fusion.2), calls=%async_computation.1 | async-start | bytes 4194304 | tf_op jit(solution)/shard_map/all_to_all | solution.py:1184
  189.0 35.3 %collective-permute-start.18 = (bf16[512,1024]{1,0:T(8,128)(2,1)}, bf16[512,1024]{1,0:T(8,128)(2,1)}, u32[]{:S(2)}, u32[]{:S(2)}) collective-permute-start(bf16[512,1024]{1,0:T(8,128)(2,1)} %select_select_fusion.1.refs_0_), channel_id=1, source_target_pairs={{0,2},{1,3},{2,0},{3,1},{4,6},{5,7},{6,4},{7,5},{8,10},{9,11},{10,... | collective-permute-start | bytes 3145736 | tf_op jit(solution)/shard_map/ppermute | solution.py:1063
  224.3 32.2 %all-to-all-start.2 = ((bf16[16,64,512]{2,1,0:T(8,128)(2,1)}), bf16[16,64,512]{2,1,0:T(8,128)(2,1)S(1)}, u32[]{:S(2)}, u32[]{:S(2)}) async-start(bf16[16,64,512]{2,1,0:T(8,128)(2,1)} %get-tuple-element.167), calls=%async_computation.2 | async-start | bytes 2097152 | tf_op jit(solution)/shard_map/all_to_all | solution.py:1184
  306.3 28.9 %collective-permute-start.26 = (bf16[512,1024]{1,0:T(8,128)(2,1)S(1)}, bf16[512,1024]{1,0:T(8,128)(2,1)}, u32[]{:S(2)}, u32[]{:S(2)}) collective-permute-start(bf16[512,1024]{1,0:T(8,128)(2,1)S(1)} %collective-permute-done.22), channel_id=1, source_target_pairs={{4,0},{5,1},{6,2},{7,3},{8,4},{9,5},{10,6},{11,7},{20,16},{21,17},... | collective-permute-start | bytes 3145736 | tf_op jit(solution)/shard_map/ppermute | solution.py:1063
  338.0 28.6 %collective-permute-start.30 = (bf16[512,1024]{1,0:T(8,128)(2,1)}, bf16[512,1024]{1,0:T(8,128)(2,1)}, u32[]{:S(2)}, u32[]{:S(2)}) collective-permute-start(bf16[512,1024]{1,0:T(8,128)(2,1)} %broadcast_select_fusion.2.refs_0_), channel_id=1, source_target_pairs={{0,2},{1,3},{2,0},{3,1},{4,6},{5,7},{6,4},{7,5},{8,10},{9,11},{10,... | collective-permute-start | bytes 3145736 | tf_op jit(solution)/shard_map/ppermute | solution.py:1063
  422.9 113.5 %all-to-all-start.4 = ((f32[16,2,512]{2,1,0:T(2,128)}), f32[16,2,512]{2,1,0:T(2,128)S(1)}, u32[]{:S(2)}, u32[]{:S(2)}) async-start(f32[16,2,512]{2,1,0:T(2,128)} %gather_fusion), calls=%async_computation.4 | async-start | bytes 131072 | tf_op jit(solution)/shard_map/all_to_all | solution.py:1184
  426.4 392.9 %reduce-scatter.2.cloned.1.call-start = ((), (), s32[]{:S(2)}) async-start(), calls=%async_computation.12 | async-start | bytes 17825792 | tf_op jit(solution)/shard_map/reduce_scatter | solution.py:1351
  468.0 68.4 %collective-permute-start.53 = (bf16[512,1024]{1,0:T(8,128)(2,1)}, bf16[512,1024]{1,0:T(8,128)(2,1)}, u32[]{:S(2)}, u32[]{:S(2)}) collective-permute-start(bf16[512,1024]{1,0:T(8,128)(2,1)} %get-tuple-element.236), channel_id=1, source_target_pairs={{0,16},{16,0},{1,17},{17,1},{2,18},{18,2},{3,19},{19,3},{4,20},{20... | collective-permute-start | bytes 3145736 | tf_op jit(solution)/shard_map/ppermute | solution.py:1180
  468.5 67.8 %collective-permute-start.54 = (bf16[512,1024]{1,0:T(8,128)(2,1)}, bf16[512,1024]{1,0:T(8,128)(2,1)}, u32[]{:S(2)}, u32[]{:S(2)}) collective-permute-start(bf16[512,1024]{1,0:T(8,128)(2,1)} %get-tuple-element.237), channel_id=1, source_target_pairs={{0,16},{16,0},{1,17},{17,1},{2,18},{18,2},{3,19},{19,3},{4,20},{20... | collective-permute-start | bytes 3145736 | tf_op jit(solution)/shard_map/ppermute | solution.py:1180
  482.2 31.0 %collective-permute-start.47 = (bf16[512,1024]{1,0:T(8,128)(2,1)}, bf16[512,1024]{1,0:T(8,128)(2,1)}, u32[]{:S(2)}, u32[]{:S(2)}) collective-permute-start(bf16[512,1024]{1,0:T(8,128)(2,1)} %get-tuple-element.285), channel_id=1, source_target_pairs={{0,4},{1,5},{2,6},{3,7},{4,8},{5,9},{6,10},{7,11},{16,20},{17,21},... | collective-permute-start | bytes 3145736 | tf_op jit(solution)/shard_map/ppermute | solution.py:1063
  484.5 28.8 %collective-permute-start.48 = (bf16[512,1024]{1,0:T(8,128)(2,1)}, bf16[512,1024]{1,0:T(8,128)(2,1)}, u32[]{:S(2)}, u32[]{:S(2)}) collective-permute-start(bf16[512,1024]{1,0:T(8,128)(2,1)} %get-tuple-element.284), channel_id=1, source_target_pairs={{8,4},{9,5},{10,6},{11,7},{12,8},{13,9},{14,10},{15,11},{24,20},{2... | collective-permute-start | bytes 3145736 | tf_op jit(solution)/shard_map/ppermute | solution.py:1063
  561.6 32.6 %all-to-all-start.5 = ((bf16[16,64,512]{2,1,0:T(8,128)(2,1)}), bf16[16,64,512]{2,1,0:T(8,128)(2,1)}, u32[]{:S(2)}, u32[]{:S(2)}) async-start(bf16[16,64,512]{2,1,0:T(8,128)(2,1)} %bitcast.193), calls=%async_computation.6 | async-start | bytes 2097152 | tf_op jit(solution)/shard_map/all_to_all | solution.py:1184
  579.7 68.5 %collective-permute-start.57 = (bf16[512,1024]{1,0:T(8,128)(2,1)}, bf16[512,1024]{1,0:T(8,128)(2,1)}, u32[]{:S(2)}, u32[]{:S(2)}) collective-permute-start(bf16[512,1024]{1,0:T(8,128)(2,1)} %get-tuple-element.258), channel_id=1, source_target_pairs={{0,16},{16,0},{1,17},{17,1},{2,18},{18,2},{3,19},{19,3},{4,20},{20... | collective-permute-start | bytes 3145736 | tf_op jit(solution)/shard_map/ppermute | solution.py:1180
  595.3 52.9 %collective-permute-start.56 = (bf16[8,32,1152]{2,1,0:T(8,128)(2,1)S(1)}, bf16[8,32,1152]{2,1,0:T(8,128)(2,1)S(1)}, u32[]{:S(2)}, u32[]{:S(2)}) collective-permute-start(bf16[8,32,1152]{2,1,0:T(8,128)(2,1)S(1)} %dynamic-slice_bitcast_fusion), channel_id=1, source_target_pairs={{0,16},{16,0},{1,17},{17,1},{2,18},{18,2},{3,19},{19,3},{4,20},{20... | collective-permute-start | bytes 1769480 | tf_op jit(solution)/shard_map/ppermute | solution.py:1180
  649.1 42.6 %all-to-all-start.6 = ((bf16[16,64,512]{2,1,0:T(8,128)(2,1)}), bf16[16,64,512]{2,1,0:T(8,128)(2,1)S(1)}, u32[]{:S(2)}, u32[]{:S(2)}) async-start(bf16[16,64,512]{2,1,0:T(8,128)(2,1)} %get-tuple-element.259), calls=%async_computation.7 | async-start | bytes 2097152 | tf_op jit(solution)/shard_map/all_to_all | solution.py:1184
  695.4 45.9 %all-to-all-start.7 = ((bf16[16,64,512]{2,1,0:T(8,128)(2,1)}), bf16[16,64,512]{2,1,0:T(8,128)(2,1)}, u32[]{:S(2)}, u32[]{:S(2)}) async-start(bf16[16,64,512]{2,1,0:T(8,128)(2,1)} %add_convert_fusion.6), calls=%async_computation.8 | async-start | bytes 2097152 | tf_op jit(solution)/shard_map/all_to_all | solution.py:1184
  745.6 50.0 %all-to-all-start.8 = ((bf16[8,32,2176]{2,1,0:T(8,128)(2,1)}), bf16[8,32,2176]{2,1,0:T(8,128)(2,1)}, u32[]{:S(2)}, u32[]{:S(2)}) async-start(bf16[8,32,2176]{2,1,0:T(8,128)(2,1)} %pad_maximum_fusion.3), calls=%async_computation.9 | async-start | bytes 2228224 | tf_op jit(solution)/shard_map/all_to_all | solution.py:1173
  (122 other events, 1673.7 us)
Sparse Core Ops, SparseCore 0:
  11.5 93.5 all-gather.1
  545.7 217.7 reduce-scatter.1

commit v3 on v2

--- a/solution.py
+++ b/solution.py
@@ -982,13 +982,14 @@
     )(order, places, gates, *blocks, d_hidden, weights, *kept)
 
 
-def output_kernel(order, columns, hidden, weights, out_rows):
+def output_kernel(order, columns, hidden, weights, first_half, second_half):
     total = None
     for e in range(columns.shape[2]):
         out = nt(hidden[e], weights[0, :, e * F : (e + 1) * F]).astype(jnp.bfloat16)
         spread = nn(column_match(columns[0, :, e : e + 1], CAP), out)
         total = spread if total is None else total + spread
-    out_rows[...] = total.astype(jnp.bfloat16)
+    first_half[...] = total[:, : D // 2].astype(jnp.bfloat16)
+    second_half[...] = total[:, D // 2 :].astype(jnp.bfloat16)
 
 
 def output_pass(order, columns, hidden, weights):
@@ -1003,9 +1004,9 @@
                 pl.BlockSpec((local, CAP, F), lambda j, order: (0, j, 0)),
                 pl.BlockSpec((1, D, local * F), lambda j, order: (2, 0, 0)),
             ],
-            out_specs=pl.BlockSpec((row_count, D), lambda j, order: (order[j], 0)),
+            out_specs=(pl.BlockSpec((row_count, D // 2), lambda j, order: (order[j], 0)),) * 2,
         ),
-        out_shape=jax.ShapeDtypeStruct((devices * row_count, D), jnp.bfloat16),
+        out_shape=(jax.ShapeDtypeStruct((devices * row_count, D // 2), jnp.bfloat16),) * 2,
         compiler_params=params(),
         cost_estimate=pl.CostEstimate(
             flops=work(26), bytes_accessed=devices * row_count * D * 3,
@@ -1122,16 +1123,18 @@
     return jnp.stack(steps).astype(jnp.int32)
 
 
-def scatter_sum(summed, z):
+def scatter_sum(summed, z, later, beside):
     across_3 = row_swap(summed[4][0])
-    across_3, give_2, give_1, give_0 = together(
-        (across_3, summed[3][1], summed[2][1], summed[1][1])
+    across_3, give_2, give_1, give_0, *later = together(
+        (across_3, summed[3][1], summed[2][1], summed[1][1], *later)
     )
     part_3 = added(summed[3][0], across_3)
     up_3 = up_from(part_3, (0,))
     down_3 = down_from(part_3, (3,))
     across_2 = row_swap(give_2)
-    up_3, down_3, across_2, give_1, give_0 = together((up_3, down_3, across_2, give_1, give_0))
+    up_3, down_3, across_2, give_1, give_0, beside = together(
+        (up_3, down_3, across_2, give_1, give_0, beside)
+    )
     part_2 = added(summed[2][0], across_2)
     up_2 = up_from(added(part_2, up_3), (0, 1))
     down_2 = down_from(added(part_2, down_3), (3, 2))
@@ -1141,7 +1144,7 @@
     up_1 = up_from(added(jnp.where(z == 2, part_3, part_1), up_2), (0, 1, 2))
     down_1 = down_from(added(jnp.where(z == 1, part_3, part_1), down_2), (1, 2, 3))
     across_0 = row_swap(give_0)
-    return [summed[0][0], across_0, up_1, down_1]
+    return [summed[0][0], across_0, up_1, down_1], later, beside
 
 
 def one_of(values, index, axis):
@@ -1210,10 +1213,7 @@
         axis=1,
     )
     packed_weights = lax.all_gather(
-        jnp.concatenate([w_query, w_key, w_value, extras, w_output], axis=1),
-        both,
-        axis=0,
-        tiled=True,
+        jnp.concatenate([w_query, w_key, w_value, extras], axis=1), both, axis=0, tiled=True
     )
     other_experts = exchange(w_experts)
     local = w_experts.shape[2] // F
@@ -1235,8 +1235,7 @@
         g_own.append(newest(s + 1, g_ups, g_downs, line_place))
 
     full_qkv = packed_weights[:, : wide + 2 * narrow]
-    extra_columns = packed_weights[:, wide + 2 * narrow : wide + 2 * narrow + 128]
-    full_output = packed_weights[:, wide + 2 * narrow + 128 :]
+    extra_columns = packed_weights[:, wide + 2 * narrow :]
     full_router = extra_columns[:, :E]
     gain_attn_full = extra_columns[:, E].astype(jnp.float32)
     gain_ffn_full = extra_columns[:, E + 1].astype(jnp.float32)
@@ -1269,9 +1268,10 @@
     values = raw[wide + narrow :].reshape(KVH, HD, row_count).astype(jnp.bfloat16)
     pairs = jnp.stack([keys, values], axis=1).reshape(HQ, HD, row_count)
     outgoing = jnp.concatenate([queries, pairs], axis=1)
-    outgoing, other_experts, slot_places, *step_2 = together(
-        (outgoing, other_experts, slot_places, *step_2)
-    )
+    outgoing, other_experts, slot_places, w_output, *step_2 = together(
+        (outgoing, other_experts, slot_places, w_output, *step_2)
+    )
+    full_output = lax.all_gather(w_output, both, axis=0, tiled=True)
     packed = to_heads(outgoing)
     g_across[2], g_ups[3], g_downs[3] = step_2
     g_own[3] = newest(3, g_ups, g_downs, line_place)
@@ -1305,7 +1305,9 @@
     masked = jnp.where(member, logits, floor_value)
     powers = jnp.where(member, jnp.exp(masked - jnp.max(masked, axis=1, keepdims=True)), 0.0)
     gates = powers / jnp.sum(powers, axis=1, keepdims=True)
-    slot_gates = to_heads(gates.T.reshape(devices, local, row_count))
+    swapped = core_swap(normed_ffn)
+    gates_out, swapped = together((gates.T.reshape(devices, local, row_count), swapped))
+    slot_gates = to_heads(gates_out)
     summed, d_gate_parts, kept = [], [], None
     own, across = normed_ffn, None
     ups, downs = [normed_ffn], [normed_ffn]
@@ -1313,7 +1315,7 @@
     for s in range(LINE + 1):
         blocks = [b for b in (own, across) if b is not None]
         sent = send_on(s, own, ups[-1], downs[-1])
-        blocks += [core_swap(b) for b in blocks]
+        blocks += [core_swap(b) for b in blocks] if s else [swapped]
         count = len(blocks)
         *kept, d_gate_part, near_part, far_part = expert_step(
             first, order[first : first + count], slot_places, slot_gates, blocks, d_hidden,
@@ -1332,23 +1334,23 @@
             downs.append(sent[2])
         own = newest(s + 1, ups, downs, line_place) if s < LINE - 1 else None
     slot_rows, hidden, d_gate_pre, d_up = kept
-    arrived = scatter_sum(summed, line_place)
+    out_rows, late_rows = output_pass(order, slot_columns, hidden, experts)
+    arrived, d_gate_parts, out_rows = scatter_sum(summed, line_place, d_gate_parts, out_rows)
+    mixture = lax.psum_scatter(out_rows, "ctx", scatter_dimension=0, tiled=True)
     given = weight_grad(
         (1 - side).reshape(1), slot_rows, slot_grads, d_gate_pre, d_up, hidden, jnp.bfloat16
     )
     taken = [exchange(part) for part in given]
-    out_rows = output_pass(order, slot_columns, hidden, experts)
     owned_experts = weight_grad(
         side.reshape(1), slot_rows, slot_grads, d_gate_pre, d_up, hidden, jnp.float32
     )
     back = jnp.argsort(order)
     d_gate = to_heads(jnp.concatenate(d_gate_parts, axis=0)[back])
-    *arrived, out_rows, taken[0], taken[1], owned_experts, d_gate = together(
-        (*arrived, out_rows, taken[0], taken[1], owned_experts, d_gate)
+    *arrived, taken[0], taken[1], owned_experts, d_gate = together(
+        (*arrived, taken[0], taken[1], owned_experts, d_gate)
     )
     d_gate = d_gate.reshape(E, row_count).T
     ffn_grad = sum(part.astype(jnp.float32) for part in arrived)
-    mixture = lax.psum_scatter(out_rows, "ctx", scatter_dimension=0, tiled=True)
 
     d_logits = gates * (d_gate - jnp.sum(gates * d_gate, axis=1, keepdims=True))
     ffn_grad = ffn_grad + jnp.einsum(
@@ -1374,7 +1376,8 @@
     )
     first_near, first_far = halves(output_grad, core, 0)
     first_parts = by_side(added(first_near, core_swap(first_far)))
-    d_heads, first_parts = together((d_heads, first_parts))
+    d_heads, first_parts, late_rows = together((d_heads, first_parts, late_rows))
+    late_mixture = lax.psum_scatter(late_rows, "ctx", scatter_dimension=0, tiled=True)
     first_taken = exchange(one_of(first_parts, 1 - side, 0))
 
     q_grads, kept_grads, given_grads = attention_backward(
@@ -1409,19 +1412,27 @@
     far_grad = core_swap(tt(normed_far, d_pairs).astype(jnp.bfloat16))
     near_grad = tt(normed_near, d_pairs).astype(jnp.bfloat16)
     normed_grad = tt(d_query, full_qkv[:, :wide]) + tt(d_pairs, full_qkv[:, wide:])
-    pair_parts = side_sum(by_side(added(near_grad, far_grad)), side)
     _, norm_back_attn = jax.vjp(rms_norm, inputs, gain_attn_full)
     input_norm_grad, gain_attn_grad = norm_back_attn(normed_grad)
+    gain_near, gain_far = halves(gain_attn_grad[:, None].astype(jnp.bfloat16), core, 0)
+    pair_parts = by_side(added(near_grad, far_grad))
+    given_pairs = exchange(one_of(pair_parts, 1 - side, 0))
+    gain_parts = by_side(added(gain_near, core_swap(gain_far)))
+    given_gain = exchange(one_of(gain_parts, 1 - side, 0))
     tokens_grad = residual_grad + input_norm_grad
-    gain_near, gain_far = halves(gain_attn_grad[:, None].astype(jnp.bfloat16), core, 0)
-    gain_parts = side_sum(by_side(added(gain_near, core_swap(gain_far))), side)
+    given_pairs, given_gain, tokens_grad = together((given_pairs, given_gain, tokens_grad))
+    gain_parts = added(one_of(gain_parts, side, 0), given_gain)
     pair_owned = owner_last(
         jnp.concatenate(
-            [pair_parts, gain_parts, jnp.zeros((*gain_parts.shape[:2], 127), jnp.bfloat16)],
+            [
+                added(one_of(pair_parts, side, 0), given_pairs),
+                gain_parts,
+                jnp.zeros((*gain_parts.shape[:2], 127), jnp.bfloat16),
+            ],
             axis=2,
         )
     )
-    mixture, late = together((mixture, d_query))
+    mixture = jnp.concatenate([mixture, late_mixture], axis=1)
     mixed = (residual + mixture.astype(jnp.float32)).astype(jnp.bfloat16)
     expert_grad = jnp.stack(
         [mine + part.astype(jnp.float32) for mine, part in zip(owned_experts, taken)]

time: 840 us -> 827 us (0.985)
  starting transfers between devices: 149 us -> 132 us
  waiting for transfers between devices: 219 us -> 232 us
    all_to_all x8, starting transfers between devices: 63.3 us -> 50.8 us  [to_heads(): lax.all_to_all(values, 'ctx', split_axis=0, concat_axis=0, tiled=True)]
    all_to_all x8, waiting for transfers between devices: 55.9 us -> 67 us  [to_heads(): lax.all_to_all(values, 'ctx', split_axis=0, concat_axis=0, tiled=True)]
    all_gather x1 -> x2, waiting for transfers between devices: 10.7 us -> 0.6 us  [the longest x1 0.59 us: per_device(): lax.all_gather(jnp.concatenate([w_query, w_key, w_value, extras], axis=1)...]
    all_to_all x2, starting transfers between devices: 22.1 us -> 13 us  [owner_last(): lax.all_to_all(values, 'ctx', split_axis=0, concat_axis=0, tiled=True, ax...]
    unnamed x157 -> x159, local copies, waits for them, and re-layouts: 18.5 us -> 16.9 us
  transfers between devices with their start and end apart: 77 -> 79, of which waited for: 33 -> 33; matrix products, arithmetic and copies ran while one was open for 18% -> 18% of each run, Pallas kernels for 31% -> 32%
where the time goes in v3:
time: 827 us; the launch traced here: 819 us
  Pallas kernels  258 us (31%)
  waiting for transfers between devices  232 us (28%)
  starting transfers between devices  132 us (16%)
  other arithmetic  87.4 us (11%)
  local copies, waits for them, and re-layouts  54.3 us (7%)
  matrix products  37.9 us (5%)
  between operations  17.9 us (2%)
    ppermute x57, waiting for transfers between devices, move(): return lax.ppermute(values, 'ctx', pairs)  132 us
    pallas_call x5, Pallas kernels, expert_step(): pl.pallas_call(partial(expert_kernel, count), grid_spec=pltpu.PrefetchSca...  80.2 us
    all_to_all x8, waiting for transfers between devices, to_heads(): lax.all_to_all(values, 'ctx', split_axis=0, concat_axis=0, tiled=True)  67 us
    ppermute x57, starting transfers between devices, move(): return lax.ppermute(values, 'ctx', pairs)  57.5 us
    pallas_call x1, Pallas kernels, attention_backward(): pl.pallas_call(attention_backward_kernel, out_shape=(shape,) * 3, in_spec...  52.8 us
    all_to_all x8, starting transfers between devices, to_heads(): lax.all_to_all(values, 'ctx', split_axis=0, concat_axis=0, tiled=True)  50.8 us
    pallas_call x5, Pallas kernels, grad_step(): pl.pallas_call(partial(grad_kernel, count), grid_spec=pltpu.PrefetchScala...  36.6 us
    pallas_call x1, Pallas kernels, attention_forward(): pl.pallas_call(attention_forward_kernel, out_shape=(jax.ShapeDtypeStruct(...  31.2 us
  transfers between devices with their start and end apart: 79, of which 33 were waited for; matrix products, arithmetic and copies ran while one was open for 18% of the time, Pallas kernels for 32%

profile of v3, /device:TPU:0, one launch (start us, length us, event | category | flops | bytes accessed | tf_op | source)
XLA Modules:
  0.0 819.3 jit_solution(8409454621174910372)
XLA Ops:
  30.5 7.4 collective-permute-done.refs_1_
  37.9 7.0 collective-permute-done.1
  59.6 24.4 %collective-permute-done.3.refs_1_ = bf16[512,1024]{1,0:T(8,128)(2,1)} collective-permute-done((bf16[512,1024]{1,0:T(8,128)(2,1)}, bf16[512,1024]{1,0:T(8,128)(2,1)}, u32[]{:S(2)}, u32[]{:S(2)}) %collective-permute-start.3) | collective-permute-done | bytes 1048608 | tf_op jit(solution)/shard_map/ppermute | solution.py:1064
  108.8 13.5 %collective-permute-done.7.refs_1_ = bf16[512,1024]{1,0:T(8,128)(2,1)S(1)} collective-permute-done((bf16[512,1024]{1,0:T(8,128)(2,1)}, bf16[512,1024]{1,0:T(8,128)(2,1)S(1)}, u32[]{:S(2)}, u32[]{:S(2)}) %collective-permute-start.7) | collective-permute-done | bytes 1048608 | tf_op jit(solution)/shard_map/ppermute | solution.py:1064
  146.1 8.3 %grad_step.6 = (bf16[2,2560,1024]{2,1,0:T(8,128)(2,1)}, bf16[2,2560,512]{2,1,0:T(8,128)(2,1)}) custom-call(s32[4]{0:T(128)} %pad_add_fusion.3.order, f32[16,2,512]{2,1,0:T(2,128)} %copy-done.40, bf16[512,1024]{1,0:T(8,128)(2,1)} %broadcast_select_fusion.5.refs_0_, ...), custom_call_target="tpu_custom_call", output_to_operand_aliasing={{0}: (7, {}), {1}: (8, {})} | custom-call | flops 11500000256 | bytes 8388608 | tf_op jit(solution)/shard_map/grad_step/pallas_call | solution.py:837
  154.4 8.3 %grad_step.7 = (bf16[2,2560,1024]{2,1,0:T(8,128)(2,1)}, bf16[2,2560,512]{2,1,0:T(8,128)(2,1)}) custom-call(s32[4]{0:T(128)} %pad_add_fusion.2.order, f32[16,2,512]{2,1,0:T(2,128)} %copy-done.40, bf16[512,1024]{1,0:T(8,128)(2,1)} %broadcast_select_fusion.4.refs_0_, ...), custom_call_target="tpu_custom_call", output_to_operand_aliasing={{0}: (7, {}), {1}: (8, {})} | custom-call | flops 11500000256 | bytes 8388608 | tf_op jit(solution)/shard_map/grad_step/pallas_call | solution.py:837
  163.7 8.5 %grad_step.8 = (bf16[2,2560,1024]{2,1,0:T(8,128)(2,1)}, bf16[2,2560,512]{2,1,0:T(8,128)(2,1)}) custom-call(s32[4]{0:T(128)} %pad_add_fusion.1.order, f32[16,2,512]{2,1,0:T(2,128)} %copy-done.40, bf16[512,1024]{1,0:T(8,128)(2,1)} %select_select_fusion.1.refs_0_, bf16[512,1024]{1,0:T(8,128)(2,1)} %copy-done.65, ...), custom_call_target="tpu_custom_call", output_to_operand_aliasing={{0}: (7, {}), {1}: (8, {})} | custom-call | flops 11500000256 | bytes 8388608 | tf_op jit(solution)/shard_map/grad_step/pallas_call | solution.py:837
  178.7 31.2 %attention_forward.1 = (bf16[16,64,512]{2,1,0:T(8,128)(2,1)}, f32[64,8192]{1,0:T(8,128)}, f32[1,8192]{1,0:T(1,128)}) custom-call(s32[33]{0:T(128)} %pad_add_fusion.table, bf16[16,128,512]{2,1,0:T(8,128)(2,1)} %all-to-all-done.1.mine, bf16[16,128,512]{2,1,0:T(8,128)(2,1)} %copy-done.64), custom_call_target="tpu_custom_call" | custom-call | flops 41400000512 | bytes 4194304 | tf_op jit(solution)/shard_map/attention_forward/pallas_call | solution.py:729
  209.9 9.5 %all-to-all-start.2 = ((bf16[16,64,512]{2,1,0:T(8,128)(2,1)}), bf16[16,64,512]{2,1,0:T(8,128)(2,1)S(1)}, u32[]{:S(2)}, u32[]{:S(2)}) async-start(bf16[16,64,512]{2,1,0:T(8,128)(2,1)} %get-tuple-element.180), calls=%async_computation.2 | async-start | bytes 2097152 | tf_op jit(solution)/shard_map/all_to_all | solution.py:1187
  229.1 19.0 %all-to-all-done.2 = bf16[16,64,512]{2,1,0:T(8,128)(2,1)S(1)} async-done(((bf16[16,64,512]{2,1,0:T(8,128)(2,1)}), bf16[16,64,512]{2,1,0:T(8,128)(2,1)S(1)}, u32[]{:S(2)}, u32[]{:S(2)}) %all-to-all-start.2) | async-done | bytes 1048608 | tf_op jit(solution)/shard_map/all_to_all | solution.py:1187
  255.3 6.7 all-to-all-start.3
  269.6 11.4 %expert_step.5 = (bf16[2,2560,1024]{2,1,0:T(8,128)(2,1)}, bf16[2,2560,512]{2,1,0:T(8,128)(2,1)}, bf16[2,2560,512]{2,1,0:T(8,128)(2,1)}, bf16[2,2560,512]{2,1,0:T...) custom-call(s32[2]{0:T(128)} %pad_add_fusion.4.order, ...), custom_call_target="tpu_custom_call" | custom-call | flops 11500000256 | bytes 6291456 | tf_op jit(solution)/shard_map/expert_step/pallas_call | solution.py:941
  281.0 7.4 collective-permute-done.20.refs_1_
  300.9 19.0 %expert_step.6 = (bf16[2,2560,1024]{2,1,0:T(8,128)(2,1)}, bf16[2,2560,512]{2,1,0:T(8,128)(2,1)}, bf16[2,2560,512]{2,1,0:T(8,128)(2,1)}, bf16[2,2560,512]{2,1,0:T...) custom-call(s32[4]{0:T(128)} %pad_add_fusion.3.order, ...), custom_call_target="tpu_custom_call", output_to_operand_aliasing={{0}: (9, {}), {1}: (10, {}), {2}: (11, {}), {3}: (12, {})} | custom-call | flops 20700000256 | bytes 12582912 | tf_op jit(solution)/shard_map/expert_step/pallas_call | solution.py:941
  336.2 18.9 %expert_step.7 = (bf16[2,2560,1024]{2,1,0:T(8,128)(2,1)}, bf16[2,2560,512]{2,1,0:T(8,128)(2,1)}, bf16[2,2560,512]{2,1,0:T(8,128)(2,1)}, bf16[2,2560,512]{2,1,0:T...) custom-call(s32[4]{0:T(128)} %pad_add_fusion.2.order, ...), custom_call_target="tpu_custom_call", output_to_operand_aliasing={{0}: (9, {}), {1}: (10, {}), {2}: (11, {}), {3}: (12, {})} | custom-call | flops 20700000256 | bytes 12582912 | tf_op jit(solution)/shard_map/expert_step/pallas_call | solution.py:941
  367.6 19.3 %expert_step.8 = (bf16[2,2560,1024]{2,1,0:T(8,128)(2,1)}, bf16[2,2560,512]{2,1,0:T(8,128)(2,1)}, bf16[2,2560,512]{2,1,0:T(8,128)(2,1)}, bf16[2,2560,512]{2,1,0:T...) custom-call(s32[4]{0:T(128)} %pad_add_fusion.1.order, ...), custom_call_target="tpu_custom_call", output_to_operand_aliasing={{0}: (9, {}), {1}: (10, {}), {2}: (11, {}), {3}: (12, {})} | custom-call | flops 20700000256 | bytes 12582912 | tf_op jit(solution)/shard_map/expert_step/pallas_call | solution.py:941
  395.2 11.6 %expert_step.9 = (bf16[2,2560,1024]{2,1,0:T(8,128)(2,1)}, bf16[2,2560,512]{2,1,0:T(8,128)(2,1)}, bf16[2,2560,512]{2,1,0:T(8,128)(2,1)}, bf16[2,2560,512]{2,1,0:T...) custom-call(s32[2]{0:T(128)} %pad_add_fusion.5.order, ...), custom_call_target="tpu_custom_call", output_to_operand_aliasing={{0}: (7, {}), {1}: (8, {}), {2}: (9, {}), {3}: (10, {})} | custom-call | flops 11500000256 | bytes 6291456 | tf_op jit(solution)/shard_map/expert_step/pallas_call | solution.py:941
  418.8 19.0 %collective-permute-done.43 = bf16[512,1024]{1,0:T(8,128)(2,1)S(1)} collective-permute-done((bf16[512,1024]{1,0:T(8,128)(2,1)S(1)}, bf16[512,1024]{1,0:T(8,128)(2,1)S(1)}, u32[]{:S(2)}, u32[]{:S(2)}) %collective-permute-start.43) | collective-permute-done | bytes 1048608 | tf_op jit(solution)/shard_map/ppermute | solution.py:1064
  444.1 26.5 %output_pass.1 = (bf16[8192,512]{1,0:T(8,128)(2,1)}, bf16[8192,512]{1,0:T(8,128)(2,1)}) custom-call(s32[16]{0:T(128)} %stack.100.order, f32[16,512,2]{2,1,0:T(8,128)} %bitcast.180, bf16[2,2560,512]{2,1,0:T(8,128)(2,1)} %get-tuple-element.242.hidden, bf16[3,1024,1024]{2,1,0:T(8,128)(2,1)} %pad_maximum_fusion.refs_2_.refs_4_.refs_3_.refs_5_.weights), custom_call_target="tpu_custom_call" | custom-call | flops 29899999232 | bytes 25165824 | tf_op jit(solution)/shard_map/output_pass/pallas_call | solution.py:997
  482.5 15.9 %weight_grad.2 = (bf16[512,1024]{1,0:T(8,128)(2,1)}, bf16[512,1024]{1,0:T(8,128)(2,1)}, bf16[512,1024]{1,0:T(8,128)(2,1)}) custom-call(s32[1]{0:T(128)} %bitcast.45.half, bf16[2,2560,1024]{2,1,0:T(8,128)(2,1)} %get-tuple-element.255.slot_rows, bf16[2,2560,1024]{2,1,0:T(8,128)(2,1)} %get-tuple-element.256.slot_grads, ...), custom_call_target="tpu_custom_call" | custom-call | flops 17250000896 | bytes 41943040 | tf_op jit(solution)/shard_map/weight_grad/pallas_call | solution.py:1029
  521.3 14.9 %weight_grad.3 = (f32[512,1024]{1,0:T(8,128)}, f32[512,1024]{1,0:T(8,128)}, f32[512,1024]{1,0:T(8,128)}) custom-call(s32[1]{0:T(128)} %bitcast.46.half, bf16[2,2560,1024]{2,1,0:T(8,128)(2,1)} %get-tuple-element.255.slot_rows, bf16[2,2560,1024]{2,1,0:T(8,128)(2,1)} %get-tuple-element.256.slot_grads, bf16[2,2560,512]{2,1,0:T(8,128)(2,1)} %get-tuple-element.257.d_gate_pre, ...), custom_call_target="tpu_custom_call" | custom-call | flops 17250000896 | bytes 41943040 | tf_op jit(solution)/shard_map/weight_grad/pallas_call | solution.py:1029
  536.2 9.3 %collective-permute-done.54 = bf16[512,1024]{1,0:T(8,128)(2,1)} collective-permute-done((bf16[512,1024]{1,0:T(8,128)(2,1)}, bf16[512,1024]{1,0:T(8,128)(2,1)}, u32[]{:S(2)}, u32[]{:S(2)}) %collective-permute-start.54) | collective-permute-done | bytes 1048608 | tf_op jit(solution)/shard_map/ppermute | solution.py:1183
  545.5 12.4 %collective-permute-done.51 = bf16[512,1024]{1,0:T(8,128)(2,1)} collective-permute-done((bf16[512,1024]{1,0:T(8,128)(2,1)}, bf16[512,1024]{1,0:T(8,128)(2,1)}, u32[]{:S(2)}, u32[]{:S(2)}) %collective-permute-start.51) | collective-permute-done | bytes 1048608 | tf_op jit(solution)/shard_map/ppermute | solution.py:1064
  599.4 11.0 %all-to-all-done.5.d_out = bf16[16,64,512]{2,1,0:T(8,128)(2,1)} async-done(((bf16[16,64,512]{2,1,0:T(8,128)(2,1)}), bf16[16,64,512]{2,1,0:T(8,128)(2,1)}, u32[]{:S(2)}, u32[]{:S(2)}) %all-to-all-start.5) | async-done | bytes 1048608 | tf_op jit(solution)/shard_map/all_to_all | solution.py:1187
  613.0 52.8 %attention_backward.1 = (bf16[16,64,512]{2,1,0:T(8,128)(2,1)}, bf16[16,64,512]{2,1,0:T(8,128)(2,1)}, bf16[16,64,512]{2,1,0:T(8,128)(2,1)}) custom-call(s32[33]{0:T(128)} %pad_add_fusion.table, bf16[16,128,512]{2,1,0:T(8,128)(2,1)} %all-to-all-done.1.mine, bf16[16,128,512]{2,1,0:T(8,128)(2,1)} %copy-done.64, bf16[16,64,512]{2,1,0:T(8,128)(2,1)} %all-to-all-done.5.d_out, ...), custom_call_target="tpu_custom_call" | custom-call | flops 66700001280 | bytes 6291456 | tf_op jit(solution)/shard_map/attention_backward/pallas_call | solution.py:755
  666.7 6.9 all-to-all-start.6
  681.3 20.8 %all-to-all-done.6 = bf16[16,64,512]{2,1,0:T(8,128)(2,1)S(1)} async-done(((bf16[16,64,512]{2,1,0:T(8,128)(2,1)}), bf16[16,64,512]{2,1,0:T(8,128)(2,1)S(1)}, u32[]{:S(2)}, u32[]{:S(2)}) %all-to-all-start.6) | async-done | bytes 1048608 | tf_op jit(solution)/shard_map/all_to_all | solution.py:1187
  705.3 7.0 all-to-all-start.7
  721.0 8.3 %collective-permute-done.60 = bf16[8,32,1024]{2,1,0:T(8,128)(2,1)S(1)} collective-permute-done((bf16[8,32,1024]{2,1,0:T(8,128)(2,1)S(1)}, bf16[8,32,1024]{2,1,0:T(8,128)(2,1)S(1)}, u32[]{:S(2)}, u32[]{:S(2)}) %collective-permute-start.60) | collective-permute-done | bytes 524320 | tf_op jit(solution)/shard_map/ppermute | solution.py:1183
  730.7 16.1 %all-to-all-done.7 = bf16[16,64,512]{2,1,0:T(8,128)(2,1)S(1)} async-done(((bf16[16,64,512]{2,1,0:T(8,128)(2,1)}), bf16[16,64,512]{2,1,0:T(8,128)(2,1)S(1)}, u32[]{:S(2)}, u32[]{:S(2)}) %all-to-all-start.7) | async-done | bytes 1048608 | tf_op jit(solution)/shard_map/all_to_all | solution.py:1187
  750.0 7.0 all-to-all-start.8
  776.0 8.4 %collective-permute-done.64 = bf16[8,32,1]{1,0,2:T(8,128)(2,1)S(1)} collective-permute-done((bf16[8,32,1]{1,0,2:T(8,128)(2,1)S(1)}, bf16[8,32,1]{1,0,2:T(8,128)(2,1)S(1)}, u32[]{:S(2)}, u32[]{:S(2)}) %collective-permute-start.64) | collective-permute-done | bytes 544 | tf_op jit(solution)/shard_map/ppermute | solution.py:1183
  (433 shorter events, 333.5 us)
Async XLA Ops:
  7.2 84.2 %all-gather.3.cloned.1.call-start = ((), (), s32[]{:S(2)}) async-start(), calls=%async_computation.12 | async-start | bytes 4595712 | tf_op jit(solution)/shard_map/all_gather | solution.py:1215
  13.4 31.5 %collective-permute-start.1 = (bf16[512,1024]{1,0:T(8,128)(2,1)}, bf16[512,1024]{1,0:T(8,128)(2,1)S(1)}, u32[]{:S(2)}, u32[]{:S(2)}) collective-permute-start(bf16[512,1024]{1,0:T(8,128)(2,1)} %refs_0_.1), channel_id=1, source_target_pairs={{0,4},{1,5},{2,6},{3,7},{4,8},{5,9},{6,10},{7,11},{8,12},{9,13},{1... | collective-permute-start | bytes 3145736 | tf_op jit(solution)/shard_map/ppermute | solution.py:1064
  17.0 32.9 %collective-permute-start.2 = (bf16[512,1024]{1,0:T(8,128)(2,1)}, bf16[512,1024]{1,0:T(8,128)(2,1)S(1)}, u32[]{:S(2)}, u32[]{:S(2)}) collective-permute-start(bf16[512,1024]{1,0:T(8,128)(2,1)} %refs_0_.1), channel_id=1, source_target_pairs={{4,0},{5,1},{6,2},{7,3},{8,4},{9,5},{10,6},{11,7},{12,8},{13,9},{1... | collective-permute-start | bytes 3145736 | tf_op jit(solution)/shard_map/ppermute | solution.py:1064
  18.3 121.4 %collective-permute-start.16 = (bf16[512,1024]{1,0:T(8,128)(2,1)}, bf16[512,1024]{1,0:T(8,128)(2,1)}, u32[]{:S(2)}, u32[]{:S(2)}) collective-permute-start(bf16[512,1024]{1,0:T(8,128)(2,1)} %refs_0_.1), channel_id=1, source_target_pairs={{0,1},{1,0},{2,3},{3,2},{4,5},{5,4},{6,7},{7,6},{8,9},{9,8},{10,11... | collective-permute-start | bytes 3145736 | tf_op jit(solution)/shard_map/ppermute | solution.py:1064
  20.1 103.2 %all-to-all-start = ((f32[16,2,512]{2,1,0:T(2,128)}), f32[16,2,512]{2,1,0:T(2,128)S(1)}, u32[]{:S(2)}, u32[]{:S(2)}) async-start(f32[16,2,512]{2,1,0:T(2,128)} %reshape.436), calls=%async_computation | async-start | bytes 131072 | tf_op jit(solution)/shard_map/all_to_all | solution.py:1187
  26.2 82.6 %collective-permute-start.6 = (bf16[3,512,1024]{2,1,0:T(8,128)(2,1)}, bf16[3,512,1024]{2,1,0:T(8,128)(2,1)}, u32[]{:S(2)}, u32[]{:S(2)}) collective-permute-start(bf16[3,512,1024]{2,1,0:T(8,128)(2,1)} %param.22), channel_id=1, source_target_pairs={{0,16},{16,0},{1,17},{17,1},{2,18},{18,2},{3,19},{19,3},{4,20},{20... | collective-permute-start | bytes 9437192 | tf_op jit(solution)/shard_map/ppermute | solution.py:1183
  49.9 34.2 %collective-permute-start.4 = (bf16[512,1024]{1,0:T(8,128)(2,1)S(1)}, bf16[512,1024]{1,0:T(8,128)(2,1)}, u32[]{:S(2)}, u32[]{:S(2)}) collective-permute-start(bf16[512,1024]{1,0:T(8,128)(2,1)S(1)} %collective-permute-done.1), channel_id=1, source_target_pairs={{4,8},{5,9},{6,10},{7,11},{8,12},{9,13},{10,14},{11,15},{20,24},{2... | collective-permute-start | bytes 3145736 | tf_op jit(solution)/shard_map/ppermute | solution.py:1064
  51.5 39.3 %collective-permute-start.5 = (bf16[512,1024]{1,0:T(8,128)(2,1)S(1)}, bf16[512,1024]{1,0:T(8,128)(2,1)}, u32[]{:S(2)}, u32[]{:S(2)}) collective-permute-start(bf16[512,1024]{1,0:T(8,128)(2,1)S(1)} %collective-permute-done.2), channel_id=1, source_target_pairs={{4,0},{5,1},{6,2},{7,3},{8,4},{9,5},{10,6},{11,7},{20,16},{21,17},... | collective-permute-start | bytes 3145736 | tf_op jit(solution)/shard_map/ppermute | solution.py:1064
  53.9 30.2 %collective-permute-start.3 = (bf16[512,1024]{1,0:T(8,128)(2,1)}, bf16[512,1024]{1,0:T(8,128)(2,1)}, u32[]{:S(2)}, u32[]{:S(2)}) collective-permute-start(bf16[512,1024]{1,0:T(8,128)(2,1)} %broadcast_select_fusion.5.refs_0_), channel_id=1, source_target_pairs={{0,2},{1,3},{2,0},{3,1},{4,6},{5,7},{6,4},{7,5},{8,10},{9,11},{10,... | collective-permute-start | bytes 3145736 | tf_op jit(solution)/shard_map/ppermute | solution.py:1064
  91.4 31.0 %collective-permute-start.8 = (bf16[512,1024]{1,0:T(8,128)(2,1)}, bf16[512,1024]{1,0:T(8,128)(2,1)}, u32[]{:S(2)}, u32[]{:S(2)}) collective-permute-start(bf16[512,1024]{1,0:T(8,128)(2,1)} %collective-permute-done.4), channel_id=1, source_target_pairs={{8,12},{9,13},{10,14},{11,15},{24,28},{25,29},{26,30},{27,31}} | collective-permute-start | bytes 3145736 | tf_op jit(solution)/shard_map/ppermute | solution.py:1064
  108.8 37.0 %collective-permute-start.14 = (bf16[512,1024]{1,0:T(8,128)(2,1)}, bf16[512,1024]{1,0:T(8,128)(2,1)}, u32[]{:S(2)}, u32[]{:S(2)}) collective-permute-start(bf16[512,1024]{1,0:T(8,128)(2,1)} %broadcast_select_fusion.5.refs_0_), channel_id=1, source_target_pairs={{0,1},{1,0},{2,3},{3,2},{4,5},{5,4},{6,7},{7,6},{8,9},{9,8},{10,11... | collective-permute-start | bytes 3145736 | tf_op jit(solution)/shard_map/ppermute | solution.py:1064
  122.3 32.1 %collective-permute-start.12 = (bf16[512,1024]{1,0:T(8,128)(2,1)}, bf16[512,1024]{1,0:T(8,128)(2,1)}, u32[]{:S(2)}, u32[]{:S(2)}) collective-permute-start(bf16[512,1024]{1,0:T(8,128)(2,1)} %broadcast_select_fusion.4.refs_0_), channel_id=1, source_target_pairs={{0,1},{1,0},{2,3},{3,2},{4,5},{5,4},{6,7},{7,6},{8,9},{9,8},{10,11... | collective-permute-start | bytes 3145736 | tf_op jit(solution)/shard_map/ppermute | solution.py:1064
  123.3 31.1 %collective-permute-start.13 = (bf16[512,1024]{1,0:T(8,128)(2,1)}, bf16[512,1024]{1,0:T(8,128)(2,1)}, u32[]{:S(2)}, u32[]{:S(2)}) collective-permute-start(bf16[512,1024]{1,0:T(8,128)(2,1)} %collective-permute-done.3.refs_1_), channel_id=1, source_target_pairs={{0,1},{1,0},{2,3},{3,2},{4,5},{5,4},{6,7},{7,6},{8,9},{9,8},{10,11... | collective-permute-start | bytes 3145736 | tf_op jit(solution)/shard_map/ppermute | solution.py:1064
  124.0 48.2 %all-to-all-start.1 = ((bf16[16,128,512]{2,1,0:T(8,128)(2,1)}), bf16[16,128,512]{2,1,0:T(8,128)(2,1)}, u32[]{:S(2)}, u32[]{:S(2)}) async-start(bf16[16,128,512]{2,1,0:T(8,128)(2,1)} %pad_maximum_fusion.2), calls=%async_computation.1 | async-start | bytes 4194304 | tf_op jit(solution)/shard_map/all_to_all | solution.py:1187
  129.8 118.4 %all-gather.5.cloned.1.call-start = ((), (), s32[]{:S(2)}) async-start(), calls=%async_computation.13 | async-start | bytes 2162688 | tf_op jit(solution)/shard_map/all_gather | solution.py:1274
  174.7 35.3 %collective-permute-start.18 = (bf16[512,1024]{1,0:T(8,128)(2,1)}, bf16[512,1024]{1,0:T(8,128)(2,1)}, u32[]{:S(2)}, u32[]{:S(2)}) collective-permute-start(bf16[512,1024]{1,0:T(8,128)(2,1)} %select_select_fusion.1.refs_0_), channel_id=1, source_target_pairs={{0,2},{1,3},{2,0},{3,1},{4,6},{5,7},{6,4},{7,5},{8,10},{9,11},{10,... | collective-permute-start | bytes 3145736 | tf_op jit(solution)/shard_map/ppermute | solution.py:1064
  209.9 38.2 %all-to-all-start.2 = ((bf16[16,64,512]{2,1,0:T(8,128)(2,1)}), bf16[16,64,512]{2,1,0:T(8,128)(2,1)S(1)}, u32[]{:S(2)}, u32[]{:S(2)}) async-start(bf16[16,64,512]{2,1,0:T(8,128)(2,1)} %get-tuple-element.180), calls=%async_computation.2 | async-start | bytes 2097152 | tf_op jit(solution)/shard_map/all_to_all | solution.py:1187
  262.1 548.0 %reduce-scatter.3.cloned.1.call-start = ((), (), s32[]{:S(2)}) async-start(), calls=%async_computation.14 | async-start | bytes 8912896 | tf_op jit(solution)/shard_map/reduce_scatter | solution.py:1339
  438.2 32.4 %collective-permute-start.44 = (bf16[512,1024]{1,0:T(8,128)(2,1)S(1)}, bf16[512,1024]{1,0:T(8,128)(2,1)}, u32[]{:S(2)}, u32[]{:S(2)}) collective-permute-start(bf16[512,1024]{1,0:T(8,128)(2,1)S(1)} %fusion.15), channel_id=1, source_target_pairs={{0,4},{1,5},{2,6},{3,7},{16,20},{17,21},{18,22},{19,23}} | collective-permute-start | bytes 3145736 | tf_op jit(solution)/shard_map/ppermute | solution.py:1064
  498.4 37.8 %collective-permute-start.53 = (bf16[512,1024]{1,0:T(8,128)(2,1)}, bf16[512,1024]{1,0:T(8,128)(2,1)}, u32[]{:S(2)}, u32[]{:S(2)}) collective-permute-start(bf16[512,1024]{1,0:T(8,128)(2,1)} %get-tuple-element.259), channel_id=1, source_target_pairs={{0,16},{16,0},{1,17},{17,1},{2,18},{18,2},{3,19},{19,3},{4,20},{20... | collective-permute-start | bytes 3145736 | tf_op jit(solution)/shard_map/ppermute | solution.py:1183
  499.9 45.6 %collective-permute-start.54 = (bf16[512,1024]{1,0:T(8,128)(2,1)}, bf16[512,1024]{1,0:T(8,128)(2,1)}, u32[]{:S(2)}, u32[]{:S(2)}) collective-permute-start(bf16[512,1024]{1,0:T(8,128)(2,1)} %get-tuple-element.260), channel_id=1, source_target_pairs={{0,16},{16,0},{1,17},{17,1},{2,18},{18,2},{3,19},{19,3},{4,20},{20... | collective-permute-start | bytes 3145736 | tf_op jit(solution)/shard_map/ppermute | solution.py:1183
  501.8 43.7 %all-to-all-start.4 = ((f32[16,2,512]{2,1,0:T(2,128)}), f32[16,2,512]{2,1,0:T(2,128)S(1)}, u32[]{:S(2)}, u32[]{:S(2)}) async-start(f32[16,2,512]{2,1,0:T(2,128)} %gather_fusion), calls=%async_computation.5 | async-start | bytes 131072 | tf_op jit(solution)/shard_map/all_to_all | solution.py:1187
  514.9 42.9 %collective-permute-start.51 = (bf16[512,1024]{1,0:T(8,128)(2,1)}, bf16[512,1024]{1,0:T(8,128)(2,1)}, u32[]{:S(2)}, u32[]{:S(2)}) collective-permute-start(bf16[512,1024]{1,0:T(8,128)(2,1)} %get-tuple-element.309), channel_id=1, source_target_pairs={{0,4},{1,5},{2,6},{3,7},{4,8},{5,9},{6,10},{7,11},{8,12},{9,13},{1... | collective-permute-start | bytes 3145736 | tf_op jit(solution)/shard_map/ppermute | solution.py:1064
  517.2 42.7 %collective-permute-start.52 = (bf16[512,1024]{1,0:T(8,128)(2,1)}, bf16[512,1024]{1,0:T(8,128)(2,1)}, u32[]{:S(2)}, u32[]{:S(2)}) collective-permute-start(bf16[512,1024]{1,0:T(8,128)(2,1)} %get-tuple-element.308), channel_id=1, source_target_pairs={{4,0},{5,1},{6,2},{7,3},{8,4},{9,5},{10,6},{11,7},{12,8},{13,9},{1... | collective-permute-start | bytes 3145736 | tf_op jit(solution)/shard_map/ppermute | solution.py:1064
  518.5 41.4 %collective-permute-start.50 = (bf16[512,1024]{1,0:T(8,128)(2,1)}, bf16[512,1024]{1,0:T(8,128)(2,1)}, u32[]{:S(2)}, u32[]{:S(2)}) collective-permute-start(bf16[512,1024]{1,0:T(8,128)(2,1)} %slice_bitcast_fusion.2), channel_id=1, source_target_pairs={{0,2},{1,3},{2,0},{3,1},{4,6},{5,7},{6,4},{7,5},{8,10},{9,11},{10,... | collective-permute-start | bytes 3145736 | tf_op jit(solution)/shard_map/ppermute | solution.py:1064
  576.2 34.1 %all-to-all-start.5 = ((bf16[16,64,512]{2,1,0:T(8,128)(2,1)}), bf16[16,64,512]{2,1,0:T(8,128)(2,1)}, u32[]{:S(2)}, u32[]{:S(2)}) async-start(bf16[16,64,512]{2,1,0:T(8,128)(2,1)} %bitcast.196), calls=%async_computation.6 | async-start | bytes 2097152 | tf_op jit(solution)/shard_map/all_to_all | solution.py:1187
  581.3 228.8 %reduce-scatter.5.cloned.1.call-start = ((), (), s32[]{:S(2)}) async-start(), calls=%async_computation.15 | async-start | bytes 8912896 | tf_op jit(solution)/shard_map/reduce_scatter | solution.py:1380
  594.0 71.8 %collective-permute-start.57 = (bf16[512,1024]{1,0:T(8,128)(2,1)}, bf16[512,1024]{1,0:T(8,128)(2,1)}, u32[]{:S(2)}, u32[]{:S(2)}) collective-permute-start(bf16[512,1024]{1,0:T(8,128)(2,1)} %get-tuple-element.282), channel_id=1, source_target_pairs={{0,16},{16,0},{1,17},{17,1},{2,18},{18,2},{3,19},{19,3},{4,20},{20... | collective-permute-start | bytes 3145736 | tf_op jit(solution)/shard_map/ppermute | solution.py:1183
  611.5 54.3 %collective-permute-start.56 = (bf16[8,32,1152]{2,1,0:T(8,128)(2,1)S(1)}, bf16[8,32,1152]{2,1,0:T(8,128)(2,1)S(1)}, u32[]{:S(2)}, u32[]{:S(2)}) collective-permute-start(bf16[8,32,1152]{2,1,0:T(8,128)(2,1)S(1)} %dynamic-slice_bitcast_fusion), channel_id=1, source_target_pairs={{0,16},{16,0},{1,17},{17,1},{2,18},{18,2},{3,19},{19,3},{4,20},{20... | collective-permute-start | bytes 1769480 | tf_op jit(solution)/shard_map/ppermute | solution.py:1183
  666.7 35.4 %all-to-all-start.6 = ((bf16[16,64,512]{2,1,0:T(8,128)(2,1)}), bf16[16,64,512]{2,1,0:T(8,128)(2,1)S(1)}, u32[]{:S(2)}, u32[]{:S(2)}) async-start(bf16[16,64,512]{2,1,0:T(8,128)(2,1)} %get-tuple-element.283), calls=%async_computation.8 | async-start | bytes 2097152 | tf_op jit(solution)/shard_map/all_to_all | solution.py:1187
  705.3 41.5 %all-to-all-start.7 = ((bf16[16,64,512]{2,1,0:T(8,128)(2,1)}), bf16[16,64,512]{2,1,0:T(8,128)(2,1)S(1)}, u32[]{:S(2)}, u32[]{:S(2)}) async-start(bf16[16,64,512]{2,1,0:T(8,128)(2,1)} %add_convert_fusion.5), calls=%async_computation.9 | async-start | bytes 2097152 | tf_op jit(solution)/shard_map/all_to_all | solution.py:1187
  750.0 36.9 %all-to-all-start.8 = ((bf16[8,32,2176]{2,1,0:T(8,128)(2,1)}), bf16[8,32,2176]{2,1,0:T(8,128)(2,1)}, u32[]{:S(2)}, u32[]{:S(2)}) async-start(bf16[8,32,2176]{2,1,0:T(8,128)(2,1)} %pad_maximum_fusion.3), calls=%async_computation.10 | async-start | bytes 2228224 | tf_op jit(solution)/shard_map/all_to_all | solution.py:1176
  (125 other events, 2005.9 us)
Sparse Core Ops, SparseCore 0:
  11.4 79.9 all-gather.2
  174.8 71.0 all-gather.4
  470.7 129.6 reduce-scatter.2
  613.1 132.3 reduce-scatter.4

commit v4 on v3

--- a/solution.py
+++ b/solution.py
@@ -779,11 +779,6 @@
 def slot_match(places, rows):
     numbers = lax.broadcasted_iota(jnp.int32, (rows, places.shape[1]), 0).astype(jnp.float32)
     return numbers == places
-
-
-def column_match(places, columns):
-    numbers = lax.broadcasted_iota(jnp.int32, (places.shape[0], columns), 1).astype(jnp.float32)
-    return jnp.where(numbers == places, 1.0, 0.0).astype(jnp.bfloat16)
 
 
 def both_match(places):
@@ -982,25 +977,28 @@
     )(order, places, gates, *blocks, d_hidden, weights, *kept)
 
 
-def output_kernel(order, columns, hidden, weights, first_half, second_half):
-    total = None
-    for e in range(columns.shape[2]):
-        out = nt(hidden[e], weights[0, :, e * F : (e + 1) * F]).astype(jnp.bfloat16)
-        spread = nn(column_match(columns[0, :, e : e + 1], CAP), out)
-        total = spread if total is None else total + spread
+def output_kernel(order, places, hidden, weights, first_half, second_half):
+    rows = jnp.concatenate(
+        [
+            nt(hidden[e], weights[0, :, e * F : (e + 1) * F]).astype(jnp.bfloat16)
+            for e in range(places.shape[1])
+        ],
+        axis=0,
+    )
+    total = nn(spread_match(places[0]), rows)
     first_half[...] = total[:, : D // 2].astype(jnp.bfloat16)
     second_half[...] = total[:, D // 2 :].astype(jnp.bfloat16)
 
 
-def output_pass(order, columns, hidden, weights):
-    devices, row_count, local = columns.shape
+def output_pass(order, places, hidden, weights):
+    devices, local, row_count = places.shape
     return pl.pallas_call(
         output_kernel,
         grid_spec=pltpu.PrefetchScalarGridSpec(
             num_scalar_prefetch=1,
             grid=(devices,),
             in_specs=[
-                pl.BlockSpec((1, row_count, local), lambda j, order: (order[j], 0, 0)),
+                pl.BlockSpec((1, local, row_count), lambda j, order: (order[j], 0, 0)),
                 pl.BlockSpec((local, CAP, F), lambda j, order: (0, j, 0)),
                 pl.BlockSpec((1, D, local * F), lambda j, order: (2, 0, 0)),
             ],
@@ -1013,7 +1011,7 @@
             transcendentals=0,
         ),
         name="output_pass",
-    )(order, columns, hidden, weights)
+    )(order, places, hidden, weights)
 
 
 def weight_grad_kernel(half, slot_rows, slot_grads, d_gate_pre, d_up, hidden, *out):
@@ -1275,7 +1273,6 @@
     packed = to_heads(outgoing)
     g_across[2], g_ups[3], g_downs[3] = step_2
     g_own[3] = newest(3, g_ups, g_downs, line_place)
-    slot_columns = slot_places.transpose(0, 2, 1)
     first_half = jnp.where(side == 0, w_experts, other_experts)
     second_half = jnp.where(side == 0, other_experts, w_experts)
     experts = jnp.concatenate([first_half, second_half], axis=1)
@@ -1334,7 +1331,7 @@
             downs.append(sent[2])
         own = newest(s + 1, ups, downs, line_place) if s < LINE - 1 else None
     slot_rows, hidden, d_gate_pre, d_up = kept
-    out_rows, late_rows = output_pass(order, slot_columns, hidden, experts)
+    out_rows, late_rows = output_pass(order, slot_places, hidden, experts)
     arrived, d_gate_parts, out_rows = scatter_sum(summed, line_place, d_gate_parts, out_rows)
     mixture = lax.psum_scatter(out_rows, "ctx", scatter_dimension=0, tiled=True)
     given = weight_grad(
@@ -1399,8 +1396,6 @@
     query_parts = jnp.concatenate(
         [query_parts, added(one_of(first_parts, side, 0), first_taken)], axis=2
     )
-    pair_back, query_parts = together((pair_back, query_parts))
-    query_owned = owner_last(query_parts)
     pairs = pair_back.astype(jnp.float32).reshape(KVH, 2, HD, row_count)
     d_pairs = jnp.concatenate(
         [
@@ -1409,7 +1404,9 @@
         ],
         axis=0,
     ).reshape(2 * narrow, row_count)
-    far_grad = core_swap(tt(normed_far, d_pairs).astype(jnp.bfloat16))
+    far_grad, query_parts = together((tt(normed_far, d_pairs).astype(jnp.bfloat16), query_parts))
+    far_grad = core_swap(far_grad)
+    query_owned = owner_last(query_parts)
     near_grad = tt(normed_near, d_pairs).astype(jnp.bfloat16)
     normed_grad = tt(d_query, full_qkv[:, :wide]) + tt(d_pairs, full_qkv[:, wide:])
     _, norm_back_attn = jax.vjp(rms_norm, inputs, gain_attn_full)

time: 827 us -> 827 us (level)
    unnamed x159 -> x155, local copies, waits for them, and re-layouts: 16.9 us -> 17.4 us
  transfers between devices with their start and end apart: 79 -> 79, of which waited for: 33 -> 33; matrix products, arithmetic and copies ran while one was open for 18% -> 17% of each run, Pallas kernels for 32% -> 32%
where the time goes in v4:
time: 827 us; the launch traced here: 818 us
  Pallas kernels  258 us (31%)
  waiting for transfers between devices  233 us (28%)
  starting transfers between devices  132 us (16%)
  other arithmetic  87.4 us (11%)
  local copies, waits for them, and re-layouts  51.9 us (6%)
  matrix products  37.8 us (5%)
  between operations  18 us (2%)
    ppermute x57, waiting for transfers between devices, move(): return lax.ppermute(values, 'ctx', pairs)  132 us
    pallas_call x5, Pallas kernels, expert_step(): pl.pallas_call(partial(expert_kernel, count), grid_spec=pltpu.PrefetchSca...  80 us
    all_to_all x8, waiting for transfers between devices, to_heads(): lax.all_to_all(values, 'ctx', split_axis=0, concat_axis=0, tiled=True)  67.3 us
    ppermute x57, starting transfers between devices, move(): return lax.ppermute(values, 'ctx', pairs)  58 us
    pallas_call x1, Pallas kernels, attention_backward(): pl.pallas_call(attention_backward_kernel, out_shape=(shape,) * 3, in_spec...  52.6 us
    all_to_all x8, starting transfers between devices, to_heads(): lax.all_to_all(values, 'ctx', split_axis=0, concat_axis=0, tiled=True)  50.7 us
    pallas_call x5, Pallas kernels, grad_step(): pl.pallas_call(partial(grad_kernel, count), grid_spec=pltpu.PrefetchScala...  36.6 us
    pallas_call x1, Pallas kernels, attention_forward(): pl.pallas_call(attention_forward_kernel, out_shape=(jax.ShapeDtypeStruct(...  31.4 us
  transfers between devices with their start and end apart: 79, of which 33 were waited for; matrix products, arithmetic and copies ran while one was open for 17% of the time, Pallas kernels for 32%

profile of v4, /device:TPU:0, one launch (start us, length us, event | category | flops | bytes accessed | tf_op | source)
XLA Modules:
  0.0 818.2 jit_solution(16672515577626006099)
XLA Ops:
  30.5 7.4 collective-permute-done.refs_1_
  37.9 7.0 collective-permute-done.1
  60.2 23.9 %collective-permute-done.3.refs_1_ = bf16[512,1024]{1,0:T(8,128)(2,1)} collective-permute-done((bf16[512,1024]{1,0:T(8,128)(2,1)}, bf16[512,1024]{1,0:T(8,128)(2,1)}, u32[]{:S(2)}, u32[]{:S(2)}) %collective-permute-start.3) | collective-permute-done | bytes 1048608 | tf_op jit(solution)/shard_map/ppermute | solution.py:1062
  108.8 13.5 %collective-permute-done.7.refs_1_ = bf16[512,1024]{1,0:T(8,128)(2,1)S(1)} collective-permute-done((bf16[512,1024]{1,0:T(8,128)(2,1)}, bf16[512,1024]{1,0:T(8,128)(2,1)S(1)}, u32[]{:S(2)}, u32[]{:S(2)}) %collective-permute-start.7) | collective-permute-done | bytes 1048608 | tf_op jit(solution)/shard_map/ppermute | solution.py:1062
  145.8 8.3 %grad_step.6 = (bf16[2,2560,1024]{2,1,0:T(8,128)(2,1)}, bf16[2,2560,512]{2,1,0:T(8,128)(2,1)}) custom-call(s32[4]{0:T(128)} %pad_add_fusion.3.order, f32[16,2,512]{2,1,0:T(2,128)} %copy-done.43, bf16[512,1024]{1,0:T(8,128)(2,1)} %broadcast_select_fusion.5.refs_0_, ...), custom_call_target="tpu_custom_call", output_to_operand_aliasing={{0}: (7, {}), {1}: (8, {})} | custom-call | flops 11500000256 | bytes 8388608 | tf_op jit(solution)/shard_map/grad_step/pallas_call | solution.py:832
  154.1 8.3 %grad_step.7 = (bf16[2,2560,1024]{2,1,0:T(8,128)(2,1)}, bf16[2,2560,512]{2,1,0:T(8,128)(2,1)}) custom-call(s32[4]{0:T(128)} %pad_add_fusion.2.order, f32[16,2,512]{2,1,0:T(2,128)} %copy-done.43, bf16[512,1024]{1,0:T(8,128)(2,1)} %broadcast_select_fusion.4.refs_0_, ...), custom_call_target="tpu_custom_call", output_to_operand_aliasing={{0}: (7, {}), {1}: (8, {})} | custom-call | flops 11500000256 | bytes 8388608 | tf_op jit(solution)/shard_map/grad_step/pallas_call | solution.py:832
  163.4 8.5 %grad_step.8 = (bf16[2,2560,1024]{2,1,0:T(8,128)(2,1)}, bf16[2,2560,512]{2,1,0:T(8,128)(2,1)}) custom-call(s32[4]{0:T(128)} %pad_add_fusion.1.order, f32[16,2,512]{2,1,0:T(2,128)} %copy-done.43, bf16[512,1024]{1,0:T(8,128)(2,1)} %select_select_fusion.1.refs_0_, bf16[512,1024]{1,0:T(8,128)(2,1)} %copy-done.63, ...), custom_call_target="tpu_custom_call", output_to_operand_aliasing={{0}: (7, {}), {1}: (8, {})} | custom-call | flops 11500000256 | bytes 8388608 | tf_op jit(solution)/shard_map/grad_step/pallas_call | solution.py:832
  178.6 31.4 %attention_forward.1 = (bf16[16,64,512]{2,1,0:T(8,128)(2,1)}, f32[64,8192]{1,0:T(8,128)}, f32[1,8192]{1,0:T(1,128)}) custom-call(s32[33]{0:T(128)} %pad_add_fusion.table, bf16[16,128,512]{2,1,0:T(8,128)(2,1)} %all-to-all-done.1.mine, bf16[16,128,512]{2,1,0:T(8,128)(2,1)} %copy-done.62), custom_call_target="tpu_custom_call" | custom-call | flops 41400000512 | bytes 4194304 | tf_op jit(solution)/shard_map/attention_forward/pallas_call | solution.py:729
  210.0 9.5 %all-to-all-start.2 = ((bf16[16,64,512]{2,1,0:T(8,128)(2,1)}), bf16[16,64,512]{2,1,0:T(8,128)(2,1)S(1)}, u32[]{:S(2)}, u32[]{:S(2)}) async-start(bf16[16,64,512]{2,1,0:T(8,128)(2,1)} %get-tuple-element.180), calls=%async_computation.2 | async-start | bytes 2097152 | tf_op jit(solution)/shard_map/all_to_all | solution.py:1185
  229.2 19.0 %all-to-all-done.2 = bf16[16,64,512]{2,1,0:T(8,128)(2,1)S(1)} async-done(((bf16[16,64,512]{2,1,0:T(8,128)(2,1)}), bf16[16,64,512]{2,1,0:T(8,128)(2,1)S(1)}, u32[]{:S(2)}, u32[]{:S(2)}) %all-to-all-start.2) | async-done | bytes 1048608 | tf_op jit(solution)/shard_map/all_to_all | solution.py:1185
  255.4 6.8 all-to-all-start.3
  269.7 11.4 %expert_step.5 = (bf16[2,2560,1024]{2,1,0:T(8,128)(2,1)}, bf16[2,2560,512]{2,1,0:T(8,128)(2,1)}, bf16[2,2560,512]{2,1,0:T(8,128)(2,1)}, bf16[2,2560,512]{2,1,0:T...) custom-call(s32[2]{0:T(128)} %pad_add_fusion.4.order, ...), custom_call_target="tpu_custom_call" | custom-call | flops 11500000256 | bytes 6291456 | tf_op jit(solution)/shard_map/expert_step/pallas_call | solution.py:936
  281.1 7.5 collective-permute-done.20.refs_1_
  301.0 18.9 %expert_step.6 = (bf16[2,2560,1024]{2,1,0:T(8,128)(2,1)}, bf16[2,2560,512]{2,1,0:T(8,128)(2,1)}, bf16[2,2560,512]{2,1,0:T(8,128)(2,1)}, bf16[2,2560,512]{2,1,0:T...) custom-call(s32[4]{0:T(128)} %pad_add_fusion.3.order, ...), custom_call_target="tpu_custom_call", output_to_operand_aliasing={{0}: (9, {}), {1}: (10, {}), {2}: (11, {}), {3}: (12, {})} | custom-call | flops 20700000256 | bytes 12582912 | tf_op jit(solution)/shard_map/expert_step/pallas_call | solution.py:936
  336.2 18.8 %expert_step.7 = (bf16[2,2560,1024]{2,1,0:T(8,128)(2,1)}, bf16[2,2560,512]{2,1,0:T(8,128)(2,1)}, bf16[2,2560,512]{2,1,0:T(8,128)(2,1)}, bf16[2,2560,512]{2,1,0:T...) custom-call(s32[4]{0:T(128)} %pad_add_fusion.2.order, ...), custom_call_target="tpu_custom_call", output_to_operand_aliasing={{0}: (9, {}), {1}: (10, {}), {2}: (11, {}), {3}: (12, {})} | custom-call | flops 20700000256 | bytes 12582912 | tf_op jit(solution)/shard_map/expert_step/pallas_call | solution.py:936
  367.6 19.4 %expert_step.8 = (bf16[2,2560,1024]{2,1,0:T(8,128)(2,1)}, bf16[2,2560,512]{2,1,0:T(8,128)(2,1)}, bf16[2,2560,512]{2,1,0:T(8,128)(2,1)}, bf16[2,2560,512]{2,1,0:T...) custom-call(s32[4]{0:T(128)} %pad_add_fusion.1.order, ...), custom_call_target="tpu_custom_call", output_to_operand_aliasing={{0}: (9, {}), {1}: (10, {}), {2}: (11, {}), {3}: (12, {})} | custom-call | flops 20700000256 | bytes 12582912 | tf_op jit(solution)/shard_map/expert_step/pallas_call | solution.py:936
  395.5 11.5 %expert_step.9 = (bf16[2,2560,1024]{2,1,0:T(8,128)(2,1)}, bf16[2,2560,512]{2,1,0:T(8,128)(2,1)}, bf16[2,2560,512]{2,1,0:T(8,128)(2,1)}, bf16[2,2560,512]{2,1,0:T...) custom-call(s32[2]{0:T(128)} %pad_add_fusion.5.order, ...), custom_call_target="tpu_custom_call", output_to_operand_aliasing={{0}: (7, {}), {1}: (8, {}), {2}: (9, {}), {3}: (10, {})} | custom-call | flops 11500000256 | bytes 6291456 | tf_op jit(solution)/shard_map/expert_step/pallas_call | solution.py:936
  418.0 18.9 %collective-permute-done.43 = bf16[512,1024]{1,0:T(8,128)(2,1)S(1)} collective-permute-done((bf16[512,1024]{1,0:T(8,128)(2,1)S(1)}, bf16[512,1024]{1,0:T(8,128)(2,1)S(1)}, u32[]{:S(2)}, u32[]{:S(2)}) %collective-permute-start.43) | collective-permute-done | bytes 1048608 | tf_op jit(solution)/shard_map/ppermute | solution.py:1062
  443.3 26.5 %output_pass.1 = (bf16[8192,512]{1,0:T(8,128)(2,1)}, bf16[8192,512]{1,0:T(8,128)(2,1)}) custom-call(s32[16]{0:T(128)} %stack.100.order, f32[16,2,512]{2,1,0:T(2,128)} %copy-done.43, bf16[2,2560,512]{2,1,0:T(8,128)(2,1)} %get-tuple-element.242.hidden, bf16[3,1024,1024]{2,1,0:T(8,128)(2,1)} %pad_maximum_fusion.refs_2_.refs_4_.refs_3_.refs_5_.weights), custom_call_target="tpu_custom_call" | custom-call | flops 29899999232 | bytes 25165824 | tf_op jit(solution)/shard_map/output_pass/pallas_call | solution.py:995
  481.7 16.2 %weight_grad.2 = (bf16[512,1024]{1,0:T(8,128)(2,1)}, bf16[512,1024]{1,0:T(8,128)(2,1)}, bf16[512,1024]{1,0:T(8,128)(2,1)}) custom-call(s32[1]{0:T(128)} %bitcast.44.half, bf16[2,2560,1024]{2,1,0:T(8,128)(2,1)} %get-tuple-element.255.slot_rows, bf16[2,2560,1024]{2,1,0:T(8,128)(2,1)} %get-tuple-element.256.slot_grads, ...), custom_call_target="tpu_custom_call" | custom-call | flops 17250000896 | bytes 41943040 | tf_op jit(solution)/shard_map/weight_grad/pallas_call | solution.py:1027
  520.2 14.7 %weight_grad.3 = (f32[512,1024]{1,0:T(8,128)}, f32[512,1024]{1,0:T(8,128)}, f32[512,1024]{1,0:T(8,128)}) custom-call(s32[1]{0:T(128)} %bitcast.45.half, bf16[2,2560,1024]{2,1,0:T(8,128)(2,1)} %get-tuple-element.255.slot_rows, bf16[2,2560,1024]{2,1,0:T(8,128)(2,1)} %get-tuple-element.256.slot_grads, bf16[2,2560,512]{2,1,0:T(8,128)(2,1)} %get-tuple-element.257.d_gate_pre, ...), custom_call_target="tpu_custom_call" | custom-call | flops 17250000896 | bytes 41943040 | tf_op jit(solution)/shard_map/weight_grad/pallas_call | solution.py:1027
  534.9 9.7 %collective-permute-done.54 = bf16[512,1024]{1,0:T(8,128)(2,1)} collective-permute-done((bf16[512,1024]{1,0:T(8,128)(2,1)}, bf16[512,1024]{1,0:T(8,128)(2,1)}, u32[]{:S(2)}, u32[]{:S(2)}) %collective-permute-start.54) | collective-permute-done | bytes 1048608 | tf_op jit(solution)/shard_map/ppermute | solution.py:1181
  544.6 12.3 %collective-permute-done.51 = bf16[512,1024]{1,0:T(8,128)(2,1)} collective-permute-done((bf16[512,1024]{1,0:T(8,128)(2,1)}, bf16[512,1024]{1,0:T(8,128)(2,1)}, u32[]{:S(2)}, u32[]{:S(2)}) %collective-permute-start.51) | collective-permute-done | bytes 1048608 | tf_op jit(solution)/shard_map/ppermute | solution.py:1062
  598.2 10.7 %all-to-all-done.5.d_out = bf16[16,64,512]{2,1,0:T(8,128)(2,1)} async-done(((bf16[16,64,512]{2,1,0:T(8,128)(2,1)}), bf16[16,64,512]{2,1,0:T(8,128)(2,1)}, u32[]{:S(2)}, u32[]{:S(2)}) %all-to-all-start.5) | async-done | bytes 1048608 | tf_op jit(solution)/shard_map/all_to_all | solution.py:1185
  611.6 52.6 %attention_backward.1 = (bf16[16,64,512]{2,1,0:T(8,128)(2,1)}, bf16[16,64,512]{2,1,0:T(8,128)(2,1)}, bf16[16,64,512]{2,1,0:T(8,128)(2,1)}) custom-call(s32[33]{0:T(128)} %pad_add_fusion.table, bf16[16,128,512]{2,1,0:T(8,128)(2,1)} %all-to-all-done.1.mine, bf16[16,128,512]{2,1,0:T(8,128)(2,1)} %copy-done.62, bf16[16,64,512]{2,1,0:T(8,128)(2,1)} %all-to-all-done.5.d_out, ...), custom_call_target="tpu_custom_call" | custom-call | flops 66700001280 | bytes 6291456 | tf_op jit(solution)/shard_map/attention_backward/pallas_call | solution.py:755
  665.0 7.0 all-to-all-start.6
  679.7 21.0 %all-to-all-done.6 = bf16[16,64,512]{2,1,0:T(8,128)(2,1)S(1)} async-done(((bf16[16,64,512]{2,1,0:T(8,128)(2,1)}), bf16[16,64,512]{2,1,0:T(8,128)(2,1)S(1)}, u32[]{:S(2)}, u32[]{:S(2)}) %all-to-all-start.6) | async-done | bytes 1048608 | tf_op jit(solution)/shard_map/all_to_all | solution.py:1185
  703.9 7.1 all-to-all-start.7
  719.6 8.3 %collective-permute-done.60 = bf16[8,32,1024]{2,1,0:T(8,128)(2,1)S(1)} collective-permute-done((bf16[8,32,1024]{2,1,0:T(8,128)(2,1)S(1)}, bf16[8,32,1024]{2,1,0:T(8,128)(2,1)S(1)}, u32[]{:S(2)}, u32[]{:S(2)}) %collective-permute-start.60) | collective-permute-done | bytes 524320 | tf_op jit(solution)/shard_map/ppermute | solution.py:1181
  729.3 16.4 %all-to-all-done.7 = bf16[16,64,512]{2,1,0:T(8,128)(2,1)S(1)} async-done(((bf16[16,64,512]{2,1,0:T(8,128)(2,1)}), bf16[16,64,512]{2,1,0:T(8,128)(2,1)S(1)}, u32[]{:S(2)}, u32[]{:S(2)}) %all-to-all-start.7) | async-done | bytes 1048608 | tf_op jit(solution)/shard_map/all_to_all | solution.py:1185
  749.0 6.9 all-to-all-start.8
  774.9 8.4 %collective-permute-done.64 = bf16[8,32,1]{1,0,2:T(8,128)(2,1)S(1)} collective-permute-done((bf16[8,32,1]{1,0,2:T(8,128)(2,1)S(1)}, bf16[8,32,1]{1,0,2:T(8,128)(2,1)S(1)}, u32[]{:S(2)}, u32[]{:S(2)}) %collective-permute-start.64) | collective-permute-done | bytes 544 | tf_op jit(solution)/shard_map/ppermute | solution.py:1181
  (428 shorter events, 332.6 us)
Async XLA Ops:
  7.2 84.1 %all-gather.3.cloned.1.call-start = ((), (), s32[]{:S(2)}) async-start(), calls=%async_computation.12 | async-start | bytes 4595712 | tf_op jit(solution)/shard_map/all_gather | solution.py:1213
  13.4 31.5 %collective-permute-start.1 = (bf16[512,1024]{1,0:T(8,128)(2,1)}, bf16[512,1024]{1,0:T(8,128)(2,1)S(1)}, u32[]{:S(2)}, u32[]{:S(2)}) collective-permute-start(bf16[512,1024]{1,0:T(8,128)(2,1)} %refs_0_.1), channel_id=1, source_target_pairs={{0,4},{1,5},{2,6},{3,7},{4,8},{5,9},{6,10},{7,11},{8,12},{9,13},{1... | collective-permute-start | bytes 3145736 | tf_op jit(solution)/shard_map/ppermute | solution.py:1062
  17.0 32.9 %collective-permute-start.2 = (bf16[512,1024]{1,0:T(8,128)(2,1)}, bf16[512,1024]{1,0:T(8,128)(2,1)S(1)}, u32[]{:S(2)}, u32[]{:S(2)}) collective-permute-start(bf16[512,1024]{1,0:T(8,128)(2,1)} %refs_0_.1), channel_id=1, source_target_pairs={{4,0},{5,1},{6,2},{7,3},{8,4},{9,5},{10,6},{11,7},{12,8},{13,9},{1... | collective-permute-start | bytes 3145736 | tf_op jit(solution)/shard_map/ppermute | solution.py:1062
  18.3 121.1 %collective-permute-start.16 = (bf16[512,1024]{1,0:T(8,128)(2,1)}, bf16[512,1024]{1,0:T(8,128)(2,1)}, u32[]{:S(2)}, u32[]{:S(2)}) collective-permute-start(bf16[512,1024]{1,0:T(8,128)(2,1)} %refs_0_.1), channel_id=1, source_target_pairs={{0,1},{1,0},{2,3},{3,2},{4,5},{5,4},{6,7},{7,6},{8,9},{9,8},{10,11... | collective-permute-start | bytes 3145736 | tf_op jit(solution)/shard_map/ppermute | solution.py:1062
  20.1 103.1 %all-to-all-start = ((f32[16,2,512]{2,1,0:T(2,128)}), f32[16,2,512]{2,1,0:T(2,128)S(1)}, u32[]{:S(2)}, u32[]{:S(2)}) async-start(f32[16,2,512]{2,1,0:T(2,128)} %reshape.436), calls=%async_computation | async-start | bytes 131072 | tf_op jit(solution)/shard_map/all_to_all | solution.py:1185
  26.2 82.6 %collective-permute-start.6 = (bf16[3,512,1024]{2,1,0:T(8,128)(2,1)}, bf16[3,512,1024]{2,1,0:T(8,128)(2,1)}, u32[]{:S(2)}, u32[]{:S(2)}) collective-permute-start(bf16[3,512,1024]{2,1,0:T(8,128)(2,1)} %param.22), channel_id=1, source_target_pairs={{0,16},{16,0},{1,17},{17,1},{2,18},{18,2},{3,19},{19,3},{4,20},{20... | collective-permute-start | bytes 9437192 | tf_op jit(solution)/shard_map/ppermute | solution.py:1181
  49.9 34.2 %collective-permute-start.4 = (bf16[512,1024]{1,0:T(8,128)(2,1)S(1)}, bf16[512,1024]{1,0:T(8,128)(2,1)}, u32[]{:S(2)}, u32[]{:S(2)}) collective-permute-start(bf16[512,1024]{1,0:T(8,128)(2,1)S(1)} %collective-permute-done.1), channel_id=1, source_target_pairs={{4,8},{5,9},{6,10},{7,11},{8,12},{9,13},{10,14},{11,15},{20,24},{2... | collective-permute-start | bytes 3145736 | tf_op jit(solution)/shard_map/ppermute | solution.py:1062
  51.5 39.3 %collective-permute-start.5 = (bf16[512,1024]{1,0:T(8,128)(2,1)S(1)}, bf16[512,1024]{1,0:T(8,128)(2,1)}, u32[]{:S(2)}, u32[]{:S(2)}) collective-permute-start(bf16[512,1024]{1,0:T(8,128)(2,1)S(1)} %collective-permute-done.2), channel_id=1, source_target_pairs={{4,0},{5,1},{6,2},{7,3},{8,4},{9,5},{10,6},{11,7},{20,16},{21,17},... | collective-permute-start | bytes 3145736 | tf_op jit(solution)/shard_map/ppermute | solution.py:1062
  53.9 30.2 %collective-permute-start.3 = (bf16[512,1024]{1,0:T(8,128)(2,1)}, bf16[512,1024]{1,0:T(8,128)(2,1)}, u32[]{:S(2)}, u32[]{:S(2)}) collective-permute-start(bf16[512,1024]{1,0:T(8,128)(2,1)} %broadcast_select_fusion.5.refs_0_), channel_id=1, source_target_pairs={{0,2},{1,3},{2,0},{3,1},{4,6},{5,7},{6,4},{7,5},{8,10},{9,11},{10,... | collective-permute-start | bytes 3145736 | tf_op jit(solution)/shard_map/ppermute | solution.py:1062
  91.3 31.0 %collective-permute-start.8 = (bf16[512,1024]{1,0:T(8,128)(2,1)}, bf16[512,1024]{1,0:T(8,128)(2,1)}, u32[]{:S(2)}, u32[]{:S(2)}) collective-permute-start(bf16[512,1024]{1,0:T(8,128)(2,1)} %collective-permute-done.4), channel_id=1, source_target_pairs={{8,12},{9,13},{10,14},{11,15},{24,28},{25,29},{26,30},{27,31}} | collective-permute-start | bytes 3145736 | tf_op jit(solution)/shard_map/ppermute | solution.py:1062
  108.8 36.7 %collective-permute-start.14 = (bf16[512,1024]{1,0:T(8,128)(2,1)}, bf16[512,1024]{1,0:T(8,128)(2,1)}, u32[]{:S(2)}, u32[]{:S(2)}) collective-permute-start(bf16[512,1024]{1,0:T(8,128)(2,1)} %broadcast_select_fusion.5.refs_0_), channel_id=1, source_target_pairs={{0,1},{1,0},{2,3},{3,2},{4,5},{5,4},{6,7},{7,6},{8,9},{9,8},{10,11... | collective-permute-start | bytes 3145736 | tf_op jit(solution)/shard_map/ppermute | solution.py:1062
  122.3 31.8 %collective-permute-start.12 = (bf16[512,1024]{1,0:T(8,128)(2,1)}, bf16[512,1024]{1,0:T(8,128)(2,1)}, u32[]{:S(2)}, u32[]{:S(2)}) collective-permute-start(bf16[512,1024]{1,0:T(8,128)(2,1)} %broadcast_select_fusion.4.refs_0_), channel_id=1, source_target_pairs={{0,1},{1,0},{2,3},{3,2},{4,5},{5,4},{6,7},{7,6},{8,9},{9,8},{10,11... | collective-permute-start | bytes 3145736 | tf_op jit(solution)/shard_map/ppermute | solution.py:1062
  123.2 30.9 %collective-permute-start.13 = (bf16[512,1024]{1,0:T(8,128)(2,1)}, bf16[512,1024]{1,0:T(8,128)(2,1)}, u32[]{:S(2)}, u32[]{:S(2)}) collective-permute-start(bf16[512,1024]{1,0:T(8,128)(2,1)} %collective-permute-done.3.refs_1_), channel_id=1, source_target_pairs={{0,1},{1,0},{2,3},{3,2},{4,5},{5,4},{6,7},{7,6},{8,9},{9,8},{10,11... | collective-permute-start | bytes 3145736 | tf_op jit(solution)/shard_map/ppermute | solution.py:1062
  123.9 48.1 %all-to-all-start.1 = ((bf16[16,128,512]{2,1,0:T(8,128)(2,1)}), bf16[16,128,512]{2,1,0:T(8,128)(2,1)}, u32[]{:S(2)}, u32[]{:S(2)}) async-start(bf16[16,128,512]{2,1,0:T(8,128)(2,1)} %pad_maximum_fusion.2), calls=%async_computation.1 | async-start | bytes 4194304 | tf_op jit(solution)/shard_map/all_to_all | solution.py:1185
  129.7 118.6 %all-gather.5.cloned.1.call-start = ((), (), s32[]{:S(2)}) async-start(), calls=%async_computation.13 | async-start | bytes 2162688 | tf_op jit(solution)/shard_map/all_gather | solution.py:1272
  174.4 35.6 %collective-permute-start.18 = (bf16[512,1024]{1,0:T(8,128)(2,1)}, bf16[512,1024]{1,0:T(8,128)(2,1)}, u32[]{:S(2)}, u32[]{:S(2)}) collective-permute-start(bf16[512,1024]{1,0:T(8,128)(2,1)} %select_select_fusion.1.refs_0_), channel_id=1, source_target_pairs={{0,2},{1,3},{2,0},{3,1},{4,6},{5,7},{6,4},{7,5},{8,10},{9,11},{10,... | collective-permute-start | bytes 3145736 | tf_op jit(solution)/shard_map/ppermute | solution.py:1062
  210.0 38.2 %all-to-all-start.2 = ((bf16[16,64,512]{2,1,0:T(8,128)(2,1)}), bf16[16,64,512]{2,1,0:T(8,128)(2,1)S(1)}, u32[]{:S(2)}, u32[]{:S(2)}) async-start(bf16[16,64,512]{2,1,0:T(8,128)(2,1)} %get-tuple-element.180), calls=%async_computation.2 | async-start | bytes 2097152 | tf_op jit(solution)/shard_map/all_to_all | solution.py:1185
  262.1 546.8 %reduce-scatter.3.cloned.1.call-start = ((), (), s32[]{:S(2)}) async-start(), calls=%async_computation.14 | async-start | bytes 8912896 | tf_op jit(solution)/shard_map/reduce_scatter | solution.py:1336
  437.3 32.4 %collective-permute-start.44 = (bf16[512,1024]{1,0:T(8,128)(2,1)S(1)}, bf16[512,1024]{1,0:T(8,128)(2,1)}, u32[]{:S(2)}, u32[]{:S(2)}) collective-permute-start(bf16[512,1024]{1,0:T(8,128)(2,1)S(1)} %fusion.15), channel_id=1, source_target_pairs={{0,4},{1,5},{2,6},{3,7},{16,20},{17,21},{18,22},{19,23}} | collective-permute-start | bytes 3145736 | tf_op jit(solution)/shard_map/ppermute | solution.py:1062
  497.9 37.0 %collective-permute-start.53 = (bf16[512,1024]{1,0:T(8,128)(2,1)}, bf16[512,1024]{1,0:T(8,128)(2,1)}, u32[]{:S(2)}, u32[]{:S(2)}) collective-permute-start(bf16[512,1024]{1,0:T(8,128)(2,1)} %get-tuple-element.259), channel_id=1, source_target_pairs={{0,16},{16,0},{1,17},{17,1},{2,18},{18,2},{3,19},{19,3},{4,20},{20... | collective-permute-start | bytes 3145736 | tf_op jit(solution)/shard_map/ppermute | solution.py:1181
  499.3 45.3 %collective-permute-start.54 = (bf16[512,1024]{1,0:T(8,128)(2,1)}, bf16[512,1024]{1,0:T(8,128)(2,1)}, u32[]{:S(2)}, u32[]{:S(2)}) collective-permute-start(bf16[512,1024]{1,0:T(8,128)(2,1)} %get-tuple-element.260), channel_id=1, source_target_pairs={{0,16},{16,0},{1,17},{17,1},{2,18},{18,2},{3,19},{19,3},{4,20},{20... | collective-permute-start | bytes 3145736 | tf_op jit(solution)/shard_map/ppermute | solution.py:1181
  501.3 43.3 %all-to-all-start.4 = ((f32[16,2,512]{2,1,0:T(2,128)}), f32[16,2,512]{2,1,0:T(2,128)S(1)}, u32[]{:S(2)}, u32[]{:S(2)}) async-start(f32[16,2,512]{2,1,0:T(2,128)} %gather_fusion), calls=%async_computation.5 | async-start | bytes 131072 | tf_op jit(solution)/shard_map/all_to_all | solution.py:1185
  513.8 43.0 %collective-permute-start.51 = (bf16[512,1024]{1,0:T(8,128)(2,1)}, bf16[512,1024]{1,0:T(8,128)(2,1)}, u32[]{:S(2)}, u32[]{:S(2)}) collective-permute-start(bf16[512,1024]{1,0:T(8,128)(2,1)} %get-tuple-element.309), channel_id=1, source_target_pairs={{0,4},{1,5},{2,6},{3,7},{4,8},{5,9},{6,10},{7,11},{8,12},{9,13},{1... | collective-permute-start | bytes 3145736 | tf_op jit(solution)/shard_map/ppermute | solution.py:1062
  516.1 42.8 %collective-permute-start.52 = (bf16[512,1024]{1,0:T(8,128)(2,1)}, bf16[512,1024]{1,0:T(8,128)(2,1)}, u32[]{:S(2)}, u32[]{:S(2)}) collective-permute-start(bf16[512,1024]{1,0:T(8,128)(2,1)} %get-tuple-element.308), channel_id=1, source_target_pairs={{4,0},{5,1},{6,2},{7,3},{8,4},{9,5},{10,6},{11,7},{12,8},{13,9},{1... | collective-permute-start | bytes 3145736 | tf_op jit(solution)/shard_map/ppermute | solution.py:1062
  517.4 41.5 %collective-permute-start.50 = (bf16[512,1024]{1,0:T(8,128)(2,1)}, bf16[512,1024]{1,0:T(8,128)(2,1)}, u32[]{:S(2)}, u32[]{:S(2)}) collective-permute-start(bf16[512,1024]{1,0:T(8,128)(2,1)} %slice_bitcast_fusion.2), channel_id=1, source_target_pairs={{0,2},{1,3},{2,0},{3,1},{4,6},{5,7},{6,4},{7,5},{8,10},{9,11},{10,... | collective-permute-start | bytes 3145736 | tf_op jit(solution)/shard_map/ppermute | solution.py:1062
  575.2 33.7 %all-to-all-start.5 = ((bf16[16,64,512]{2,1,0:T(8,128)(2,1)}), bf16[16,64,512]{2,1,0:T(8,128)(2,1)}, u32[]{:S(2)}, u32[]{:S(2)}) async-start(bf16[16,64,512]{2,1,0:T(8,128)(2,1)} %bitcast.194), calls=%async_computation.6 | async-start | bytes 2097152 | tf_op jit(solution)/shard_map/all_to_all | solution.py:1185
  580.2 228.7 %reduce-scatter.5.cloned.1.call-start = ((), (), s32[]{:S(2)}) async-start(), calls=%async_computation.15 | async-start | bytes 8912896 | tf_op jit(solution)/shard_map/reduce_scatter | solution.py:1377
  592.8 71.4 %collective-permute-start.57 = (bf16[512,1024]{1,0:T(8,128)(2,1)}, bf16[512,1024]{1,0:T(8,128)(2,1)}, u32[]{:S(2)}, u32[]{:S(2)}) collective-permute-start(bf16[512,1024]{1,0:T(8,128)(2,1)} %get-tuple-element.282), channel_id=1, source_target_pairs={{0,16},{16,0},{1,17},{17,1},{2,18},{18,2},{3,19},{19,3},{4,20},{20... | collective-permute-start | bytes 3145736 | tf_op jit(solution)/shard_map/ppermute | solution.py:1181
  610.1 54.1 %collective-permute-start.56 = (bf16[8,32,1152]{2,1,0:T(8,128)(2,1)S(1)}, bf16[8,32,1152]{2,1,0:T(8,128)(2,1)S(1)}, u32[]{:S(2)}, u32[]{:S(2)}) collective-permute-start(bf16[8,32,1152]{2,1,0:T(8,128)(2,1)S(1)} %dynamic-slice_bitcast_fusion), channel_id=1, source_target_pairs={{0,16},{16,0},{1,17},{17,1},{2,18},{18,2},{3,19},{19,3},{4,20},{20... | collective-permute-start | bytes 1769480 | tf_op jit(solution)/shard_map/ppermute | solution.py:1181
  665.0 35.7 %all-to-all-start.6 = ((bf16[16,64,512]{2,1,0:T(8,128)(2,1)}), bf16[16,64,512]{2,1,0:T(8,128)(2,1)S(1)}, u32[]{:S(2)}, u32[]{:S(2)}) async-start(bf16[16,64,512]{2,1,0:T(8,128)(2,1)} %get-tuple-element.283), calls=%async_computation.8 | async-start | bytes 2097152 | tf_op jit(solution)/shard_map/all_to_all | solution.py:1185
  703.9 41.8 %all-to-all-start.7 = ((bf16[16,64,512]{2,1,0:T(8,128)(2,1)}), bf16[16,64,512]{2,1,0:T(8,128)(2,1)S(1)}, u32[]{:S(2)}, u32[]{:S(2)}) async-start(bf16[16,64,512]{2,1,0:T(8,128)(2,1)} %add_convert_fusion.5), calls=%async_computation.9 | async-start | bytes 2097152 | tf_op jit(solution)/shard_map/all_to_all | solution.py:1185
  749.0 36.8 %all-to-all-start.8 = ((bf16[8,32,2176]{2,1,0:T(8,128)(2,1)}), bf16[8,32,2176]{2,1,0:T(8,128)(2,1)}, u32[]{:S(2)}, u32[]{:S(2)}) async-start(bf16[8,32,2176]{2,1,0:T(8,128)(2,1)} %pad_maximum_fusion.3), calls=%async_computation.10 | async-start | bytes 2228224 | tf_op jit(solution)/shard_map/all_to_all | solution.py:1174
  (123 other events, 1951.8 us)
Sparse Core Ops, SparseCore 0:
  11.4 79.8 all-gather.2
  174.5 71.2 all-gather.4
  469.9 129.0 reduce-scatter.2
  611.7 132.7 reduce-scatter.4
